TPU v7x, 32 devices: a whole 2x2x4 slice. The times are simulated.
32 devices in a mesh: cell: 16 (over z, y, x), gene: 2 (over core).
Axes of the slice: x: 2, y: 2, z: 4, core: 2. Of those that a mesh axis runs over, the one named last changes fastest.
Arguments:
- gene_in: bfloat16 [64, 2048, 256], P('cell', 'gene'), may hold values from -6 to 6
- class_in: bfloat16 [64, 8, 256], P('cell'), may hold values from -6 to 6
- expressed: int32 [64], P('cell'), may hold values from 256 to 2048, as said below
- ln1_gain: float32 [256], replicated, may hold values from 0.1 to 1.9
- ln1_bias: float32 [256], replicated, may hold values from -1.75 to 1.75
- w_qkv: bfloat16 [256, 768], replicated, may hold values from -0.375 to 0.375
- w_out: bfloat16 [256, 256], replicated, may hold values from -10 to 10
- ln2_gain: float32 [256], replicated, may hold values from 0.1 to 1.9
- ln2_bias: float32 [256], replicated, may hold values from -1.75 to 1.75
- w_up: bfloat16 [256, 1024], replicated, may hold values from -0.375 to 0.375
- b_up: float32 [1024], replicated, may hold values from -1.75 to 1.75
- w_down: bfloat16 [1024, 256], replicated, may hold values from -0.1875 to 0.1875
- b_down: float32 [256], replicated, may hold values from -1.75 to 1.75
- gene_cot: bfloat16 [64, 2048, 256], P('cell', 'gene'), may hold values from -6 to 6
- class_cot: bfloat16 [64, 8, 256], P('cell'), may hold values from -6 to 6
Outputs:
- gene_out: bfloat16 [64, 2048, 256], P('cell', 'gene')
- class_out: bfloat16 [64, 8, 256], P('cell')
- gene_grad: bfloat16 [64, 2048, 256], P('cell', 'gene')
- class_grad: bfloat16 [64, 8, 256], P('cell')
- grad_ln1_gain: float32 [256], replicated
- grad_ln1_bias: float32 [256], replicated
- grad_qkv: float32 [256, 768], replicated
- grad_out: float32 [256, 256], replicated
- grad_ln2_gain: float32 [256], replicated
- grad_ln2_bias: float32 [256], replicated
- grad_up: float32 [256, 1024], replicated
- grad_up_bias: float32 [1024], replicated
- grad_down: float32 [1024, 256], replicated
- grad_down_bias: float32 [256], replicated
Inputs may be any that keep to these rules, and one draw needn't show every extreme that they name: Each cell's gene tokens at positions below its count are expressed, the others are padding. In each aligned block of 4 cells (the cells of one index of the cell axis) one cell has all 2048 and another has 256.
All inputs are finite; a program needn't handle non-finite values.
Results may differ from a plain program's by a relative error of at most 0.015.
Values may be sent and summed in bfloat16 or wider, within the bound.
A program may use at most 256 MiB of HBM per device.

v0:
```python
import jax
import jax.numpy as jnp
from jax import lax
from jax.sharding import PartitionSpec as P

HEADS = 4


EPS = 1e-05
NEG = -1e30


def combined_all(value, axis, join):
    pieces = jax.tree.map(lambda part: lax.all_gather(part, axis), value)
    head = jax.tree.map(lambda part: part[0], pieces)
    tail = jax.tree.map(lambda part: part[1:], pieces)
    so_far, _ = lax.scan(lambda so_far, share: (join(so_far, share), None), head, tail)
    return so_far


def exact_gelu(values):
    return jax.nn.gelu(values, approximate=False)


def split_heads(array, head_count):
    return array.reshape(array.shape[:-1] + (head_count, array.shape[-1] // head_count))


def join_blocks(stat):
    return jnp.swapaxes(stat, 0, 1).reshape(stat.shape[1], -1)


def table_part(key_table, head_count, second):
    model_width = key_table.shape[-1] // 2
    if second:
        return split_heads(key_table[:, model_width:], head_count)
    return split_heads(key_table[:, :model_width], head_count)


def normalize(values, gain, bias):
    average = jnp.mean(values, -1, keepdims=True)
    centered = values - average
    spread = jnp.mean(centered * centered, -1, keepdims=True)
    inverse = lax.rsqrt(spread + EPS)
    unit_rows = centered * inverse
    return (unit_rows * gain + bias, unit_rows, inverse)


def normalize_back(grad_rows, unit_rows, inverse, gain):
    scaled = grad_rows * gain
    return inverse * (
        scaled
        - jnp.mean(scaled, -1, keepdims=True)
        - unit_rows * jnp.mean(scaled * unit_rows, -1, keepdims=True)
    )


def combine_partials(first_part, second_part):
    first_max, first_sum = first_part
    second_max, second_sum = second_part
    joint_max = jnp.maximum(first_max, second_max)
    joint_sum = first_sum * jnp.exp(first_max - joint_max) + second_sum * jnp.exp(
        second_max - joint_max
    )
    return (joint_max, joint_sum)


def attend(queries, class_table, gene_table, key_valid, head_count, factor):
    query_count, model_width = queries.shape
    block_rows = min(512, query_count)
    class_keys = table_part(class_table, head_count, False)
    class_values = table_part(class_table, head_count, True)
    gene_keys = table_part(gene_table, head_count, False)
    gene_values = table_part(gene_table, head_count, True)

    def attend_one_block(query_rows):
        query_heads = split_heads(query_rows, head_count)
        class_scores = (
            jnp.einsum("qhd,khd->hqk", query_heads, class_keys, preferred_element_type=jnp.float32)
            * factor
        )
        gene_scores = (
            jnp.einsum("qhd,khd->hqk", query_heads, gene_keys, preferred_element_type=jnp.float32)
            * factor
        )
        gene_scores = jnp.where(key_valid, gene_scores, NEG)
        row_max = jnp.maximum(jnp.max(class_scores, -1), jnp.max(gene_scores, -1))
        class_exp = jnp.exp(class_scores - row_max[..., None])
        gene_exp = jnp.where(key_valid, jnp.exp(gene_scores - row_max[..., None]), 0.0)
        row_sum = jnp.sum(class_exp, -1) + jnp.sum(gene_exp, -1)
        class_weights = (class_exp / row_sum[..., None]).astype(jnp.bfloat16)
        gene_weights = (gene_exp / row_sum[..., None]).astype(jnp.bfloat16)
        weighted = jnp.einsum(
            "hqk,khd->qhd", class_weights, class_values, preferred_element_type=jnp.float32
        )
        weighted = weighted + jnp.einsum(
            "hqk,khd->qhd", gene_weights, gene_values, preferred_element_type=jnp.float32
        )
        return (weighted.reshape(block_rows, model_width), row_max, row_sum)

    weighted, row_max, row_sum = lax.map(
        attend_one_block, queries.reshape(query_count // block_rows, block_rows, model_width)
    )
    return (weighted.reshape(query_count, model_width), join_blocks(row_max), join_blocks(row_sum))


def pair_grads(
    queries,
    query_grads,
    row_max,
    row_sum,
    row_delta,
    class_table,
    gene_table,
    key_valid,
    head_count,
    factor,
):
    query_count, model_width = queries.shape
    block_rows = min(512, query_count)
    block_count = query_count // block_rows
    class_keys = table_part(class_table, head_count, False)
    class_values = table_part(class_table, head_count, True)
    gene_keys = table_part(gene_table, head_count, False)
    gene_values = table_part(gene_table, head_count, True)

    def by_block(stat):
        return jnp.swapaxes(stat.reshape(head_count, block_count, block_rows), 0, 1)

    def pair_one_block(carried, pieces):
        query_rows, grad_rows, block_max, block_sum, block_delta = pieces
        query_heads = split_heads(query_rows, head_count)
        grad_heads = split_heads(grad_rows, head_count)
        class_scores = (
            jnp.einsum("qhd,khd->hqk", query_heads, class_keys, preferred_element_type=jnp.float32)
            * factor
        )
        gene_scores = (
            jnp.einsum("qhd,khd->hqk", query_heads, gene_keys, preferred_element_type=jnp.float32)
            * factor
        )
        class_probs = jnp.exp(class_scores - block_max[..., None]) / block_sum[..., None]
        gene_probs = jnp.where(
            key_valid, jnp.exp(gene_scores - block_max[..., None]) / block_sum[..., None], 0.0
        )
        class_dprob = jnp.einsum(
            "qhd,khd->hqk", grad_heads, class_values, preferred_element_type=jnp.float32
        )
        gene_dprob = jnp.einsum(
            "qhd,khd->hqk", grad_heads, gene_values, preferred_element_type=jnp.float32
        )
        class_dscore = (class_probs * (class_dprob - block_delta[..., None])).astype(jnp.bfloat16)
        gene_dscore = (gene_probs * (gene_dprob - block_delta[..., None])).astype(jnp.bfloat16)
        query_part = jnp.einsum(
            "hqk,khd->qhd", class_dscore, class_keys, preferred_element_type=jnp.float32
        )
        query_part = query_part + jnp.einsum(
            "hqk,khd->qhd", gene_dscore, gene_keys, preferred_element_type=jnp.float32
        )
        query_part = (query_part * factor).reshape(block_rows, model_width)
        class_dkey, class_dvalue, gene_dkey, gene_dvalue = carried
        class_dkey = (
            class_dkey
            + jnp.einsum(
                "hqk,qhd->khd", class_dscore, query_heads, preferred_element_type=jnp.float32
            )
            * factor
        )
        class_dvalue = class_dvalue + jnp.einsum(
            "hqk,qhd->khd",
            class_probs.astype(jnp.bfloat16),
            grad_heads,
            preferred_element_type=jnp.float32,
        )
        gene_dkey = (
            gene_dkey
            + jnp.einsum(
                "hqk,qhd->khd", gene_dscore, query_heads, preferred_element_type=jnp.float32
            )
            * factor
        )
        gene_dvalue = gene_dvalue + jnp.einsum(
            "hqk,qhd->khd",
            gene_probs.astype(jnp.bfloat16),
            grad_heads,
            preferred_element_type=jnp.float32,
        )
        carried = (class_dkey, class_dvalue, gene_dkey, gene_dvalue)
        return (carried, query_part)

    initial = tuple(
        (
            jnp.zeros((key_table.shape[0], head_count, model_width // head_count), jnp.float32)
            for key_table in (class_table, class_table, gene_table, gene_table)
        )
    )
    carried, query_parts = lax.scan(
        pair_one_block,
        initial,
        (
            queries.reshape(block_count, block_rows, model_width),
            query_grads.reshape(block_count, block_rows, model_width),
            by_block(row_max),
            by_block(row_sum),
            by_block(row_delta),
        ),
    )
    query_result = query_parts.reshape(query_count, query_parts.shape[-1])
    class_result = jnp.concatenate(
        [carried[0].reshape(-1, model_width), carried[1].reshape(-1, model_width)], -1
    )
    gene_result = jnp.concatenate(
        [carried[2].reshape(-1, model_width), carried[3].reshape(-1, model_width)], -1
    )
    return (query_result, class_result, gene_result)


def shards(
    gene_in,
    class_in,
    expressed,
    ln1_gain,
    ln1_bias,
    w_qkv,
    w_out,
    ln2_gain,
    ln2_bias,
    w_up,
    b_up,
    w_down,
    b_down,
    gene_cot,
    class_cot,
):
    cell_count, local_genes, model_width = gene_in.shape
    class_count = class_in.shape[1]
    head_count = HEADS
    factor = (model_width // head_count) ** (-0.5)
    shard_count = lax.axis_size("gene")
    gene_total = local_genes * shard_count
    offset = lax.axis_index("gene") * local_genes
    row_count = class_count + local_genes
    all_valid = jnp.arange(gene_total, dtype=jnp.int32)[None, :] < expressed[:, None]
    own_valid = (offset + jnp.arange(local_genes, dtype=jnp.int32))[None, :] < expressed[:, None]
    row_weight = jnp.where(jnp.arange(row_count) < class_count, 1.0 / shard_count, 1.0).astype(
        jnp.float32
    )[None, :, None]
    half_weight = row_weight.astype(jnp.bfloat16)
    tokens = jnp.concatenate([class_in, gene_in], axis=1).astype(jnp.float32)
    first_norm, first_unit, first_inverse = normalize(tokens, ln1_gain, ln1_bias)
    first_low = first_norm.astype(jnp.bfloat16)
    packed = jnp.einsum("crd,de->cre", first_low, w_qkv, preferred_element_type=jnp.float32).astype(
        jnp.bfloat16
    )
    queries = packed[..., :model_width]
    key_value = packed[..., model_width:]
    class_tables = key_value[:, :class_count]
    own_tables = key_value[:, class_count:]
    gene_table = lax.all_gather(own_tables, "gene", axis=1, tiled=True)

    def cell_attend(entry_pack):
        cell_queries, cell_class, cell_genes, cell_valid = entry_pack
        return attend(cell_queries, cell_class, cell_genes, cell_valid, head_count, factor)

    gene_mix, gene_max, gene_sum = lax.map(
        cell_attend, (queries[:, class_count:], class_tables, gene_table, all_valid)
    )
    class_heads = split_heads(queries[:, :class_count], head_count)
    own_keys = split_heads(own_tables[..., :model_width], head_count)
    own_values = split_heads(own_tables[..., model_width:], head_count)
    class_keys = split_heads(class_tables[..., :model_width], head_count)
    class_values = split_heads(class_tables[..., model_width:], head_count)
    mask_own = own_valid[:, None, None, :]
    partial_scores = (
        jnp.einsum("cqhd,ckhd->chqk", class_heads, own_keys, preferred_element_type=jnp.float32)
        * factor
    )
    partial_scores = jnp.where(mask_own, partial_scores, NEG)
    partial_max = jnp.max(partial_scores, -1)
    partial_sum = jnp.sum(
        jnp.where(mask_own, jnp.exp(partial_scores - partial_max[..., None]), 0.0), -1
    )
    merged_max, merged_sum = combined_all((partial_max, partial_sum), "gene", combine_partials)
    self_scores = (
        jnp.einsum("cqhd,ckhd->chqk", class_heads, class_keys, preferred_element_type=jnp.float32)
        * factor
    )
    class_max = jnp.maximum(merged_max, jnp.max(self_scores, -1))
    self_exp = jnp.exp(self_scores - class_max[..., None])
    class_sum = merged_sum * jnp.exp(merged_max - class_max) + jnp.sum(self_exp, -1)
    partial_probs = jnp.where(
        mask_own, jnp.exp(partial_scores - class_max[..., None]) / class_sum[..., None], 0.0
    )
    self_probs = self_exp / class_sum[..., None]
    partial_low = partial_probs.astype(jnp.bfloat16)
    self_low = self_probs.astype(jnp.bfloat16)
    own_mix = jnp.einsum(
        "chqk,ckhd->cqhd", partial_low, own_values, preferred_element_type=jnp.float32
    )
    shared_mix = lax.psum(own_mix.astype(jnp.bfloat16), "gene").astype(jnp.float32)
    class_mix = shared_mix + jnp.einsum(
        "chqk,ckhd->cqhd", self_low, class_values, preferred_element_type=jnp.float32
    )
    attended = jnp.concatenate(
        [class_mix.reshape(cell_count, class_count, model_width), gene_mix], axis=1
    )
    attended_low = attended.astype(jnp.bfloat16)
    middle = tokens + jnp.einsum(
        "crd,de->cre", attended_low, w_out, preferred_element_type=jnp.float32
    )
    second_norm, second_unit, second_inverse = normalize(middle, ln2_gain, ln2_bias)
    second_low = second_norm.astype(jnp.bfloat16)
    up_proj = jnp.einsum("crd,df->crf", second_low, w_up, preferred_element_type=jnp.float32) + b_up
    activated, gelu_pull = jax.vjp(exact_gelu, up_proj)
    activated_low = activated.astype(jnp.bfloat16)
    result = (
        middle
        + jnp.einsum("crf,fd->crd", activated_low, w_down, preferred_element_type=jnp.float32)
        + b_down
    )
    grad_y = jnp.concatenate([class_cot, gene_cot], axis=1)
    grad_down = jnp.einsum(
        "crf,crd->fd", activated_low, grad_y * half_weight, preferred_element_type=jnp.float32
    )
    grad_down_bias = jnp.sum(grad_y.astype(jnp.float32) * row_weight, axis=(0, 1))
    grad_act = jnp.einsum("crd,fd->crf", grad_y, w_down, preferred_element_type=jnp.float32)
    grad_up_low = gelu_pull(grad_act)[0].astype(jnp.bfloat16)
    grad_up = jnp.einsum(
        "crd,crf->df", second_low, grad_up_low * half_weight, preferred_element_type=jnp.float32
    )
    grad_up_bias = jnp.sum(grad_up_low.astype(jnp.float32) * row_weight, axis=(0, 1))
    second_back = jnp.einsum("crf,df->crd", grad_up_low, w_up, preferred_element_type=jnp.float32)
    grad_ln2_gain = jnp.sum(second_back * second_unit * row_weight, axis=(0, 1))
    grad_ln2_bias = jnp.sum(second_back * row_weight, axis=(0, 1))
    grad_middle = grad_y.astype(jnp.float32) + normalize_back(
        second_back, second_unit, second_inverse, ln2_gain
    )
    grad_middle_low = grad_middle.astype(jnp.bfloat16)
    grad_out = jnp.einsum(
        "crd,cre->de",
        attended_low,
        grad_middle_low * half_weight,
        preferred_element_type=jnp.float32,
    )
    grad_attended = jnp.einsum(
        "cre,de->crd", grad_middle_low, w_out, preferred_element_type=jnp.float32
    ).astype(jnp.bfloat16)
    row_delta = jnp.swapaxes(
        jnp.sum(
            split_heads(grad_attended.astype(jnp.float32), head_count)
            * split_heads(attended, head_count),
            -1,
        ),
        1,
        2,
    )
    class_delta = row_delta[..., :class_count]
    gene_delta = row_delta[..., class_count:]
    class_grad_heads = split_heads(grad_attended[:, :class_count], head_count)
    partial_dprob = jnp.einsum(
        "cqhd,ckhd->chqk", class_grad_heads, own_values, preferred_element_type=jnp.float32
    )
    partial_dscore = (partial_probs * (partial_dprob - class_delta[..., None])).astype(jnp.bfloat16)
    class_query_part = (
        jnp.einsum("chqk,ckhd->cqhd", partial_dscore, own_keys, preferred_element_type=jnp.float32)
        * factor
    ).reshape(cell_count, class_count, model_width)
    own_dkey = (
        jnp.einsum(
            "chqk,cqhd->ckhd", partial_dscore, class_heads, preferred_element_type=jnp.float32
        )
        * factor
    )
    own_dvalue = jnp.einsum(
        "chqk,cqhd->ckhd", partial_low, class_grad_heads, preferred_element_type=jnp.float32
    )
    own_from_class = jnp.concatenate(
        [
            own_dkey.reshape(cell_count, local_genes, model_width),
            own_dvalue.reshape(cell_count, local_genes, model_width),
        ],
        -1,
    )
    self_dprob = jnp.einsum(
        "cqhd,ckhd->chqk", class_grad_heads, class_values, preferred_element_type=jnp.float32
    )
    self_dscore = (self_probs * (self_dprob - class_delta[..., None])).astype(jnp.bfloat16)
    class_query_self = (
        jnp.einsum("chqk,ckhd->cqhd", self_dscore, class_keys, preferred_element_type=jnp.float32)
        * factor
    ).reshape(cell_count, class_count, model_width)
    self_dkey = (
        jnp.einsum("chqk,cqhd->ckhd", self_dscore, class_heads, preferred_element_type=jnp.float32)
        * factor
    )
    self_dvalue = jnp.einsum(
        "chqk,cqhd->ckhd", self_low, class_grad_heads, preferred_element_type=jnp.float32
    )
    class_from_class = jnp.concatenate(
        [
            self_dkey.reshape(cell_count, class_count, model_width),
            self_dvalue.reshape(cell_count, class_count, model_width),
        ],
        -1,
    )
    gene_queries = queries[:, class_count:]
    gene_grads = grad_attended[:, class_count:]

    def cell_both(entry_pack):
        cell_q, cell_g, cell_max, cell_sum, cell_delta, cell_class, cell_genes, cell_valid = (
            entry_pack
        )
        return pair_grads(
            cell_q,
            cell_g,
            cell_max,
            cell_sum,
            cell_delta,
            cell_class,
            cell_genes,
            cell_valid,
            head_count,
            factor,
        )

    gene_query_grad, class_partial, gene_partial = lax.map(
        cell_both,
        (
            gene_queries,
            gene_grads,
            gene_max,
            gene_sum,
            gene_delta,
            class_tables,
            gene_table,
            all_valid,
        ),
    )
    class_query_sum, class_from_genes = (
        lax.psum(class_query_part.astype(jnp.bfloat16), "gene").astype(jnp.float32),
        lax.psum(class_partial.astype(jnp.bfloat16), "gene").astype(jnp.float32),
    )
    own_from_genes = lax.psum_scatter(
        gene_partial.astype(jnp.bfloat16), "gene", scatter_dimension=1, tiled=True
    ).astype(jnp.float32)
    query_grad = jnp.concatenate([class_query_sum + class_query_self, gene_query_grad], axis=1)
    key_grad = jnp.concatenate(
        [class_from_genes + class_from_class, own_from_genes + own_from_class], axis=1
    )
    packed_grad = jnp.concatenate([query_grad, key_grad], axis=-1).astype(jnp.bfloat16)
    grad_qkv = jnp.einsum(
        "crd,cre->de", first_low, packed_grad * half_weight, preferred_element_type=jnp.float32
    )
    first_back = jnp.einsum("cre,de->crd", packed_grad, w_qkv, preferred_element_type=jnp.float32)
    grad_ln1_gain = jnp.sum(first_back * first_unit * row_weight, axis=(0, 1))
    grad_ln1_bias = jnp.sum(first_back * row_weight, axis=(0, 1))
    grad_tokens = grad_middle + normalize_back(first_back, first_unit, first_inverse, ln1_gain)
    summed = lax.psum(
        (
            grad_ln1_gain,
            grad_ln1_bias,
            grad_qkv,
            grad_out,
            grad_ln2_gain,
            grad_ln2_bias,
            grad_up,
            grad_up_bias,
            grad_down,
            grad_down_bias,
        ),
        ("cell", "gene"),
    )
    return (
        result[:, class_count:].astype(jnp.bfloat16),
        result[:, :class_count].astype(jnp.bfloat16),
        grad_tokens[:, class_count:].astype(jnp.bfloat16),
        grad_tokens[:, :class_count].astype(jnp.bfloat16),
        summed[0],
        summed[1],
        summed[2],
        summed[3],
        summed[4],
        summed[5],
        summed[6],
        summed[7],
        summed[8],
        summed[9],
    )


def solution(mesh):
    placed = (
        P("cell", "gene", None),
        P("cell", None, None),
        P("cell"),
        P(),
        P(),
        P(),
        P(),
        P(),
        P(),
        P(),
        P(),
        P(),
        P(),
        P("cell", "gene", None),
        P("cell", None, None),
    )
    return jax.shard_map(
        shards,
        mesh=mesh,
        in_specs=placed,
        out_specs=(
            P("cell", "gene", None),
            P("cell", None, None),
            P("cell", "gene", None),
            P("cell", None, None),
            P(),
            P(),
            P(),
            P(),
            P(),
            P(),
            P(),
            P(),
            P(),
            P(),
        ),
        check_vma=False,
    )
```

profile of v0, /device:TPU:3, one launch (start us, length us, event | category | flops | bytes accessed | tf_op | source)
XLA Modules:
  0.0 927.0 jit_solution(8896576818050206116)
XLA Ops:
  55.4 11.6 %copy.118 = bf16[4,2048,512]{1,2,0:T(8,128)(2,1)} copy(bf16[4,2048,512]{2,1,0:T(8,128)(2,1)} %all-gather.4.cloned.1.call-done) | data formatting | bytes 16777216 | tf_op jit(solution)/shard_map/while | solution.py:265
  67.0 140.7 %while.73 = (s32[]{:T(128)}, f32[4,1024,256]{2,1,0:T(8,128)}, f32[4,4,1024]{2,1,0:T(4,128)}, f32[4,4,1024]{2,1,0:T(4,128)}, bf16[4,1024,256]{2,1,0:T(8,128)(2,1)...) while((s32[]{:T(128)}, f32[4,1024,256]{2,1,0:T(8,128)}, ...), condition=%wide.region_14.15_spmd.clone, body=%wide.region_7.14_spmd.sunk.clone | while | flops 1136898048 | bytes 73895784 | solution.py:265
  72.6 26.7 %while.72 = (s32[]{:T(128)}, f32[2,512,256]{2,1,0:T(8,128)}, f32[2,4,512]{2,1,0:T(4,128)S(1)}, f32[2,4,512]{2,1,0:T(4,128)S(1)}, bf16[2,512,256]{2,1,0:T(8,128)(...) while((s32[]{:T(128)}, f32[2,512,256]{2,1,0:T(8,128)}, ...), condition=%wide.region_13.13_spmd, body=%wide.region_8.12_spmd.sunk | while | flops 1136898048 | bytes 62225044 | solution.py:101
  107.7 26.7 %while.72 = (s32[]{:T(128)}, f32[2,512,256]{2,1,0:T(8,128)}, f32[2,4,512]{2,1,0:T(4,128)S(1)}, f32[2,4,512]{2,1,0:T(4,128)S(1)}, bf16[2,512,256]{2,1,0:T(8,128)(...) while((s32[]{:T(128)}, f32[2,512,256]{2,1,0:T(8,128)}, ...), condition=%wide.region_13.13_spmd, body=%wide.region_8.12_spmd.sunk | while | flops 1136898048 | bytes 62225044 | solution.py:101
  142.9 26.7 %while.72 = (s32[]{:T(128)}, f32[2,512,256]{2,1,0:T(8,128)}, f32[2,4,512]{2,1,0:T(4,128)S(1)}, f32[2,4,512]{2,1,0:T(4,128)S(1)}, bf16[2,512,256]{2,1,0:T(8,128)(...) while((s32[]{:T(128)}, f32[2,512,256]{2,1,0:T(8,128)}, ...), condition=%wide.region_13.13_spmd, body=%wide.region_8.12_spmd.sunk | while | flops 1136898048 | bytes 62225044 | solution.py:101
  178.1 26.7 %while.72 = (s32[]{:T(128)}, f32[2,512,256]{2,1,0:T(8,128)}, f32[2,4,512]{2,1,0:T(4,128)S(1)}, f32[2,4,512]{2,1,0:T(4,128)S(1)}, bf16[2,512,256]{2,1,0:T(8,128)(...) while((s32[]{:T(128)}, f32[2,512,256]{2,1,0:T(8,128)}, ...), condition=%wide.region_13.13_spmd, body=%wide.region_8.12_spmd.sunk | while | flops 1136898048 | bytes 62225044 | solution.py:101
  221.4 11.3 %fusion.62 = (u8[1032,1024]{1,0:T(8,128)(4,1)S(1)}, u8[1032,1024]{1,0:T(8,128)(4,1)S(1)}, f32[4,1032,1024]{2,1,0:T(8,128)}) fusion(f32[1024]{0:T(1024)S(1)} %copy-done.70, bf16[256,1024]{1,0:T(8,128)(2,1)S(1)} %copy-done, f32[4,1032,256]{2,1,0:T(8,128)S(1)} %get-tuple-element.602, f32[256]{0:T(256)S(1)} %copy-done.72, f32[256]{0:T(256)S(1)} %copy-done.59, ...), kind=kOutput, calls=%fused_computation.135 | convolution fusion | flops 2226610176 | bytes 23812352 | tf_op jit(solution)/shard_map/crd,df->crf/dot_general | solution.py:313
  232.8 41.2 %multiply_convert_fusion.1 = (bf16[4,1032,1024]{2,1,0:T(8,128)(2,1)}, f32[4,1032,1024]{2,1,0:T(8,128)}) fusion(f32[4,1032,1024]{2,1,0:T(8,128)} %get-tuple-element.603, u8[1032,1024]{1,0:T(8,128)(4,1)S(1)} %get-tuple-element.447, u8[1032,1024]{1,0:T(8,128)(4,1)S(1)} %get-tuple-element.446), kind=kLoop, calls=%fused_computation.80 | loop fusion | flops 295895040 | bytes 44384256 | tf_op jit(solution)/shard_map/convert_element_type | solution.py:315
  273.9 18.1 %multiply_reduce_fusion = (f32[1024]{0:T(1024)}, bf16[4,1032,1024]{2,1,0:T(8,128)(2,1)}) fusion(f32[1032]{0:T(1024)S(1)} %copy-done.55, f32[4,1032,1024]{2,1,0:T(8,128)} %get-tuple-element.566, f32[4,1032,1024]{2,1,0:T(8,128)} %get-tuple-element.603, bf16[4,1032,256]{2,1,0:T(8,128)(2,1)} %constant_dynamic-update-slice_fusion.5, ...), kind=kOutput, calls=%fused_computation.78 | convolution fusion | flops 2236120064 | bytes 44916768 | tf_op jit(solution)/shard_map/crd,fd->crf/dot_general | solution.py:326
  320.4 383.0 %while.75 = (s32[]{:T(128)}, bf16[4,1024,256]{2,1,0:T(8,128)(2,1)}, bf16[4,8,512]{2,1,0:T(8,128)(2,1)}, bf16[4,2048,512]{2,1,0:T(8,128)(2,1)}, bf16[4,1024,256]{...) while((s32[]{:T(128)}, bf16[4,1024,256]{2,1,0:T(8,128)(2,1)}, ...), condition=%wide.region_24.25_spmd.clone, body=%wide.region_21.24_spmd.sunk.clone | while | flops 2735745024 | bytes 156119584 | solution.py:426
  329.0 77.7 %while.74 = (s32[]{:T(128)}, f32[8,4,64]{2,0,1:T(8,128)S(1)}, f32[8,4,64]{2,0,1:T(8,128)S(1)}, f32[2048,4,64]{0,2,1:T(8,128)S(1)}, f32[2048,4,64]{0,2,1:T(8,128)...) while((s32[]{:T(128)}, f32[8,4,64]{2,0,1:T(8,128)S(1)}, ...), condition=%wide.region_23.23_spmd.clone, body=%wide.region_22.22_spmd.clone.sunk | while | flops 2731534336 | bytes 127580888 | solution.py:197
  330.2 9.3 %divide_select_fusion.5 = f32[4,512,2048]{2,1,0:T(8,128)} fusion(f32[4,512]{1,0:T(4,128)S(1)} %get-tuple-element.991, f32[4,512]{1,0:T(4,128)S(1)} %dynamic-slice_bitcast_fusion.18, pred[2048]{0:T(1024)(128)(4,1)S(1)} %get-tuple-element.1175, bf16[512,4,64]{0,2,1:T(8,128)(2,1)S(1)} %bitcast.326, bf16[2048,4,64]{0,2,1:T(8,128)(2,1)} %get-tuple-element.1176), kind=kOutput, calls=%fused_computation.21.clone.1 | convolution fusion | flops 553648128 | bytes 18106368 | tf_op jit(solution)/shard_map/while/body/eval_jaxpr/while/body/eval_jaxpr/qhd,khd->hqk/dot_general | solution.py:139
  368.8 9.3 %divide_select_fusion.5 = f32[4,512,2048]{2,1,0:T(8,128)} fusion(f32[4,512]{1,0:T(4,128)S(1)} %get-tuple-element.991, f32[4,512]{1,0:T(4,128)S(1)} %dynamic-slice_bitcast_fusion.18, pred[2048]{0:T(1024)(128)(4,1)S(1)} %get-tuple-element.1175, bf16[512,4,64]{0,2,1:T(8,128)(2,1)S(1)} %bitcast.326, bf16[2048,4,64]{0,2,1:T(8,128)(2,1)} %get-tuple-element.1176), kind=kOutput, calls=%fused_computation.21.clone.1 | convolution fusion | flops 553648128 | bytes 18106368 | tf_op jit(solution)/shard_map/while/body/eval_jaxpr/while/body/eval_jaxpr/qhd,khd->hqk/dot_general | solution.py:139
  424.7 77.7 %while.74 = (s32[]{:T(128)}, f32[8,4,64]{2,0,1:T(8,128)S(1)}, f32[8,4,64]{2,0,1:T(8,128)S(1)}, f32[2048,4,64]{0,2,1:T(8,128)S(1)}, f32[2048,4,64]{0,2,1:T(8,128)...) while((s32[]{:T(128)}, f32[8,4,64]{2,0,1:T(8,128)S(1)}, ...), condition=%wide.region_23.23_spmd.clone, body=%wide.region_22.22_spmd.clone.sunk | while | flops 2731534336 | bytes 127580888 | solution.py:197
  426.0 9.3 %divide_select_fusion.5 = f32[4,512,2048]{2,1,0:T(8,128)} fusion(f32[4,512]{1,0:T(4,128)S(1)} %get-tuple-element.991, f32[4,512]{1,0:T(4,128)S(1)} %dynamic-slice_bitcast_fusion.18, pred[2048]{0:T(1024)(128)(4,1)S(1)} %get-tuple-element.1175, bf16[512,4,64]{0,2,1:T(8,128)(2,1)S(1)} %bitcast.326, bf16[2048,4,64]{0,2,1:T(8,128)(2,1)} %get-tuple-element.1176), kind=kOutput, calls=%fused_computation.21.clone.1 | convolution fusion | flops 553648128 | bytes 18106368 | tf_op jit(solution)/shard_map/while/body/eval_jaxpr/while/body/eval_jaxpr/qhd,khd->hqk/dot_general | solution.py:139
  464.6 9.3 %divide_select_fusion.5 = f32[4,512,2048]{2,1,0:T(8,128)} fusion(f32[4,512]{1,0:T(4,128)S(1)} %get-tuple-element.991, f32[4,512]{1,0:T(4,128)S(1)} %dynamic-slice_bitcast_fusion.18, pred[2048]{0:T(1024)(128)(4,1)S(1)} %get-tuple-element.1175, bf16[512,4,64]{0,2,1:T(8,128)(2,1)S(1)} %bitcast.326, bf16[2048,4,64]{0,2,1:T(8,128)(2,1)} %get-tuple-element.1176), kind=kOutput, calls=%fused_computation.21.clone.1 | convolution fusion | flops 553648128 | bytes 18106368 | tf_op jit(solution)/shard_map/while/body/eval_jaxpr/while/body/eval_jaxpr/qhd,khd->hqk/dot_general | solution.py:139
  520.5 77.8 %while.74 = (s32[]{:T(128)}, f32[8,4,64]{2,0,1:T(8,128)S(1)}, f32[8,4,64]{2,0,1:T(8,128)S(1)}, f32[2048,4,64]{0,2,1:T(8,128)S(1)}, f32[2048,4,64]{0,2,1:T(8,128)...) while((s32[]{:T(128)}, f32[8,4,64]{2,0,1:T(8,128)S(1)}, ...), condition=%wide.region_23.23_spmd.clone, body=%wide.region_22.22_spmd.clone.sunk | while | flops 2731534336 | bytes 127580888 | solution.py:197
  521.8 9.3 %divide_select_fusion.5 = f32[4,512,2048]{2,1,0:T(8,128)} fusion(f32[4,512]{1,0:T(4,128)S(1)} %get-tuple-element.991, f32[4,512]{1,0:T(4,128)S(1)} %dynamic-slice_bitcast_fusion.18, pred[2048]{0:T(1024)(128)(4,1)S(1)} %get-tuple-element.1175, bf16[512,4,64]{0,2,1:T(8,128)(2,1)S(1)} %bitcast.326, bf16[2048,4,64]{0,2,1:T(8,128)(2,1)} %get-tuple-element.1176), kind=kOutput, calls=%fused_computation.21.clone.1 | convolution fusion | flops 553648128 | bytes 18106368 | tf_op jit(solution)/shard_map/while/body/eval_jaxpr/while/body/eval_jaxpr/qhd,khd->hqk/dot_general | solution.py:139
  560.4 9.3 %divide_select_fusion.5 = f32[4,512,2048]{2,1,0:T(8,128)} fusion(f32[4,512]{1,0:T(4,128)S(1)} %get-tuple-element.991, f32[4,512]{1,0:T(4,128)S(1)} %dynamic-slice_bitcast_fusion.18, pred[2048]{0:T(1024)(128)(4,1)S(1)} %get-tuple-element.1175, bf16[512,4,64]{0,2,1:T(8,128)(2,1)S(1)} %bitcast.326, bf16[2048,4,64]{0,2,1:T(8,128)(2,1)} %get-tuple-element.1176), kind=kOutput, calls=%fused_computation.21.clone.1 | convolution fusion | flops 553648128 | bytes 18106368 | tf_op jit(solution)/shard_map/while/body/eval_jaxpr/while/body/eval_jaxpr/qhd,khd->hqk/dot_general | solution.py:139
  616.3 77.8 %while.74 = (s32[]{:T(128)}, f32[8,4,64]{2,0,1:T(8,128)S(1)}, f32[8,4,64]{2,0,1:T(8,128)S(1)}, f32[2048,4,64]{0,2,1:T(8,128)S(1)}, f32[2048,4,64]{0,2,1:T(8,128)...) while((s32[]{:T(128)}, f32[8,4,64]{2,0,1:T(8,128)S(1)}, ...), condition=%wide.region_23.23_spmd.clone, body=%wide.region_22.22_spmd.clone.sunk | while | flops 2731534336 | bytes 127580888 | solution.py:197
  617.5 9.3 %divide_select_fusion.5 = f32[4,512,2048]{2,1,0:T(8,128)} fusion(f32[4,512]{1,0:T(4,128)S(1)} %get-tuple-element.991, f32[4,512]{1,0:T(4,128)S(1)} %dynamic-slice_bitcast_fusion.18, pred[2048]{0:T(1024)(128)(4,1)S(1)} %get-tuple-element.1175, bf16[512,4,64]{0,2,1:T(8,128)(2,1)S(1)} %bitcast.326, bf16[2048,4,64]{0,2,1:T(8,128)(2,1)} %get-tuple-element.1176), kind=kOutput, calls=%fused_computation.21.clone.1 | convolution fusion | flops 553648128 | bytes 18106368 | tf_op jit(solution)/shard_map/while/body/eval_jaxpr/while/body/eval_jaxpr/qhd,khd->hqk/dot_general | solution.py:139
  656.1 9.3 %divide_select_fusion.5 = f32[4,512,2048]{2,1,0:T(8,128)} fusion(f32[4,512]{1,0:T(4,128)S(1)} %get-tuple-element.991, f32[4,512]{1,0:T(4,128)S(1)} %dynamic-slice_bitcast_fusion.18, pred[2048]{0:T(1024)(128)(4,1)S(1)} %get-tuple-element.1175, bf16[512,4,64]{0,2,1:T(8,128)(2,1)S(1)} %bitcast.326, bf16[2048,4,64]{0,2,1:T(8,128)(2,1)} %get-tuple-element.1176), kind=kOutput, calls=%fused_computation.21.clone.1 | convolution fusion | flops 553648128 | bytes 18106368 | tf_op jit(solution)/shard_map/while/body/eval_jaxpr/while/body/eval_jaxpr/qhd,khd->hqk/dot_general | solution.py:139
  783.0 40.0 %all-reduce = (f32[256]{0:T(256)}, f32[256]{0:T(256)}, f32[256]{0:T(256)}, f32[256]{0:T(256)}, f32[1024]{0:T(1024)}, /*index=5*/f32[256]{0:T(256)}) all-reduce(f32[256]{0:T(256)S(1)} %get-tuple-element.450, f32[256]{0:T(256)S(1)} %get-tuple-element.453, f32[256]{0:T(256)S(1)} %copy-done.63, ...), channel_id=1, replica_groups=mesh['cell'=16,'gene'=2] {'cell','gene'}, use_global_device_ids=true, to_apply=%region_30.31 | all-reduce | flops 2304 | bytes 18432 | tf_op jit(solution)/shard_map/psum | solution.py:458
  822.9 89.9 %all-reduce.5.cloned.1.call-done = (f32[256,768]{1,0:T(8,128)}, f32[256,256]{1,0:T(8,128)}, f32[256,1024]{1,0:T(8,128)}, f32[1024,256]{1,0:T(8,128)}) async-done(((f32[256,768]{1,0:T(8,128)}, f32[256,256]{1,0:T(8,128)}, f32[256,1024]{1,0:T(8,128)}, f32[1024,256]{1,0:T(8,128)}), (f32[256,768]{1,0:T(8,128)}, f32[256,256]{1,0:T(8,128)}, f32[256,1024]{1,0:T(8,128)}, ...) | async-done | bytes 3145744 | tf_op jit(solution)/shard_map/psum | solution.py:458
  (692 shorter events, 623.5 us)
Async XLA Ops:
  7.2 214.2 %copy-start = (bf16[256,1024]{1,0:T(8,128)(2,1)S(1)}, bf16[256,1024]{1,0:T(8,128)(2,1)}, u32[]{:S(2)}) copy-start(bf16[256,1024]{1,0:T(8,128)(2,1)} %param.32) | copy-start | bytes 1572868
  7.3 48.1 %all-gather.4.cloned.1.call-start = ((), (), s32[]{:S(2)}) async-start(), calls=%async_computation.1 | async-start | bytes 12582912 | tf_op jit(solution)/shard_map/all_gather | solution.py:259
  21.1 735.2 %reduce-scatter.2.cloned.1.call-start = ((), (), s32[]{:S(2)}) async-start(), calls=%async_computation.2 | async-start | bytes 12582912 | tf_op jit(solution)/shard_map/reduce_scatter | solution.py:443
  23.3 18.9 %copy-start.24 = (bf16[4,8,4,64]{3,2,1,0:T(4,128)(2,1)}, bf16[4,8,4,64]{3,2,1,0:T(4,128)(2,1)S(1)}, u32[]{:S(2)}) copy-start(bf16[4,8,4,64]{3,2,1,0:T(4,128)(2,1)S(1)} %reshape.333) | copy-start | bytes 49156
  29.2 8.4 copy-start.58
  32.4 12.4 %copy-start.6 = (bf16[4,1024,256]{1,2,0:T(8,128)(2,1)}, bf16[4,1024,256]{1,2,0:T(8,128)(2,1)S(1)}, u32[]{:S(2)}) copy-start(bf16[4,1024,256]{1,2,0:T(8,128)(2,1)S(1)} %copy.111) | copy-start | bytes 6291460
  32.5 12.3 %copy-start.26 = (bf16[4,8,4,64]{3,2,1,0:T(4,128)(2,1)}, bf16[4,8,4,64]{3,2,1,0:T(4,128)(2,1)S(1)}, u32[]{:S(2)}) copy-start(bf16[4,8,4,64]{3,2,1,0:T(4,128)(2,1)S(1)} %reshape.335) | copy-start | bytes 49156
  37.5 11.1 %copy-start.49 = (bf16[4,8,4,64]{3,2,1,0:T(4,128)(2,1)}, bf16[4,8,4,64]{3,2,1,0:T(4,128)(2,1)S(1)}, u32[]{:S(2)}) copy-start(bf16[4,8,4,64]{3,2,1,0:T(4,128)(2,1)S(1)} %reshape.336) | copy-start | bytes 49156
  37.6 13.3 %copy-start.54 = (bf16[4,8,256]{2,1,0:T(8,128)(2,1)S(1)}, bf16[4,8,256]{2,1,0:T(8,128)(2,1)}, u32[]{:S(2)}) copy-start(bf16[4,8,256]{2,1,0:T(8,128)(2,1)} %param.37) | copy-start | bytes 49156
  42.4 12.3 %copy-start.29 = (f32[4,4,8,8]{2,3,1,0:T(8,128)}, f32[4,4,8,8]{2,3,1,0:T(8,128)S(1)}, u32[]{:S(2)}) copy-start(f32[4,4,8,8]{2,3,1,0:T(8,128)S(1)} %get-tuple-element.596) | copy-start | bytes 12292
  42.4 12.3 %copy-start.38 = (f32[4,4,8]{2,1,0:T(4,128)}, f32[4,4,8]{2,1,0:T(4,128)S(1)}, u32[]{:S(2)}) copy-start(f32[4,4,8]{2,1,0:T(4,128)S(1)} %fusion.133) | copy-start | bytes 1540
  219.5 13.3 %copy-start.12 = (f32[4,1032,256]{2,1,0:T(8,128)}, f32[4,1032,256]{2,1,0:T(8,128)S(1)}, u32[]{:S(2)}) copy-start(f32[4,1032,256]{2,1,0:T(8,128)S(1)} %get-tuple-element.602) | copy-start | bytes 12681220
  219.5 81.7 %copy-start.31 = (f32[4,1032]{1,0:T(4,128)}, f32[4,1032]{1,0:T(4,128)S(1)}, u32[]{:S(2)}) copy-start(f32[4,1032]{1,0:T(4,128)S(1)} %broadcast_multiply_fusion.4) | copy-start | bytes 49540
  221.4 79.9 %copy-start.43 = (f32[4,1032]{1,0:T(4,128)}, f32[4,1032]{1,0:T(4,128)S(1)}, u32[]{:S(2)}) copy-start(f32[4,1032]{1,0:T(4,128)S(1)} %add_rsqrt_fusion) | copy-start | bytes 49540
  232.7 41.2 %copy-start.55 = (f32[1032]{0:T(1024)S(1)}, f32[1032]{0:T(1024)}, u32[]{:S(2)}) copy-start(f32[1032]{0:T(1024)} %fusion.131) | copy-start | bytes 12388
  232.8 41.2 %copy-start.66 = (bf16[1024,256]{1,0:T(8,128)(2,1)S(1)}, bf16[1024,256]{1,0:T(8,128)(2,1)}, u32[]{:S(2)}) copy-start(bf16[1024,256]{1,0:T(8,128)(2,1)} %param.34) | copy-start | bytes 1572868
  292.1 9.2 copy-start.13
  309.0 11.4 %copy-start.5 = (bf16[4,1032,256]{2,1,0:T(8,128)(2,1)}, bf16[4,1032,256]{2,1,0:T(8,128)(2,1)S(1)}, u32[]{:S(2)}) copy-start(bf16[4,1032,256]{2,1,0:T(8,128)(2,1)S(1)} %convolution_convert_fusion.1) | copy-start | bytes 6340612
  703.4 209.4 %all-reduce.5.cloned.1.call-start = ((), (), s32[]{:S(2)}) async-start(), calls=%async_computation.3 | async-start | bytes 6291456 | tf_op jit(solution)/shard_map/psum | solution.py:458
  729.1 9.5 %copy-start.19 = (bf16[4,1024,256]{2,1,0:T(8,128)(2,1)S(1)}, bf16[4,1024,256]{2,1,0:T(8,128)(2,1)}, u32[]{:S(2)}) copy-start(bf16[4,1024,256]{2,1,0:T(8,128)(2,1)} %convert.31) | copy-start | bytes 6291460
  729.1 9.5 %copy-start.53 = (bf16[4,8,256]{2,1,0:T(8,128)(2,1)S(1)}, bf16[4,8,256]{2,1,0:T(8,128)(2,1)}, u32[]{:S(2)}) copy-start(bf16[4,8,256]{2,1,0:T(8,128)(2,1)} %reshape.337) | copy-start | bytes 49156
  734.6 8.1 copy-start.73
  738.6 12.2 %slice-start.3 = ((s8[8454144]{0:T(1024)(128)(4,1)}), s8[4194304]{0:T(1024)(128)(4,1)S(1)}, s32[]{:S(2)}) async-start(s8[8454144]{0:T(1024)(128)(4,1)} %bitcast.348), calls=%async_computation.7 | async-start | bytes 8388608
  780.9 139.1 %copy-start.1 = (bf16[256,1024]{1,0:T(8,128)(2,1)S(1)}, bf16[256,1024]{1,0:T(8,128)(2,1)}, u32[]{:S(2)}) copy-start(bf16[256,1024]{1,0:T(8,128)(2,1)} %param.32) | copy-start | bytes 1572868
  (78 other events, 355.7 us)
Sparse Core Ops, SparseCore 0:
  21.2 21.8 all-gather.3
  703.6 18.2 reduce-scatter.1
  774.8 137.9 all-reduce.4
where the time goes:
time: 940 us; the launch traced here: 927 us
  matrix products  446 us (47%)
  local copies, waits for them, and re-layouts  196 us (21%)
  other arithmetic  126 us (13%)
  waiting for transfers between devices  90 us (10%)
  blocking collectives  51.3 us (5%)
  between operations  15.3 us (2%)
    psum x1, waiting for transfers between devices, shards(): lax.psum((grad_ln1_gain, grad_ln1_bias, grad_qkv, grad_out, grad_ln2_gain...  89.9 us
    dot_general x8, matrix products, pair_one_block(): jnp.einsum('qhd,khd->hqk', query_heads, gene_keys, preferred_element_type...  74.2 us
    dot_general x8, matrix products, pair_one_block(): jnp.einsum('hqk,qhd->khd', gene_probs.astype(jnp.bfloat16), grad_heads, p...  71.8 us
    dot_general x8, matrix products, pair_one_block(): jnp.einsum('qhd,khd->hqk', grad_heads, gene_values, preferred_element_typ...  59.5 us
    dot_general x8, matrix products, pair_one_block(): jnp.einsum('hqk,qhd->khd', gene_dscore, query_heads, preferred_element_ty...  41.6 us
    convert_element_type x1, other arithmetic, shards(): activated_low = activated.astype(jnp.bfloat16)  41.2 us
    psum x1, blocking collectives, shards(): lax.psum((grad_ln1_gain, grad_ln1_bias, grad_qkv, grad_out, grad_ln2_gain...  40 us
    dot_general x8, matrix products, attend_one_block(): jnp.einsum('hqk,khd->qhd', gene_weights, gene_values, preferred_element_t...  37.8 us
  transfers between devices with their start and end apart: 3, of which 1 were waited for; matrix products, arithmetic and copies ran while one was open for 9% of the time, Pallas kernels for 0%

commit v1 on v0

v1 whole, which is shorter than its diff:
```python
import functools

import jax
import jax.numpy as jnp
from jax import lax
from jax.experimental import pallas as pl
from jax.experimental.pallas import tpu as pltpu
from jax.sharding import PartitionSpec as P

HEADS = 4
EPS = 1e-05
LOG2E = 1.4426950408889634
SAFE = 40.0
KB = 256
VMEM = 63 * 2**20
F32 = jnp.float32
BF16 = jnp.bfloat16


def dot(left, right):
    return jnp.dot(left, right, preferred_element_type=F32)


def dot_nt(left, right):
    return lax.dot_general(left, right, (((1,), (1,)), ((), ())), preferred_element_type=F32)


def dot_tn(left, right):
    return lax.dot_general(left, right, (((0,), (0,)), ((), ())), preferred_element_type=F32)


def spread_column(row):
    return jnp.broadcast_to(row, (128, row.shape[1])).T


def widen(column, lanes):
    return jnp.concatenate([column] * (lanes // 128), axis=1)


def fold_lanes(values):
    total = values[:, :128]
    for start in range(128, values.shape[1], 128):
        total = total + values[:, start : start + 128]
    return total


def norm_rows(values):
    centered = values - jnp.mean(values, -1, keepdims=True)
    inverse = lax.rsqrt(jnp.mean(centered * centered, -1, keepdims=True) + EPS)
    return centered * inverse, inverse


def norm_columns(values):
    scale = 1.0 / values.shape[0]
    centered = values - jnp.sum(values, 0, keepdims=True) * scale
    inverse = lax.rsqrt(jnp.sum(centered * centered, 0, keepdims=True) * scale + EPS)
    return centered * inverse, inverse


def project_kernel(
    counts, place, x, xc, gain, bias, w, qt, qr, kr, vr, kt, va, stat, pc, w_t, gain_c, bias_c
):
    cell, half = pl.program_id(0), pl.program_id(1)
    genes, width = x.shape[1:]
    head = width // HEADS

    @pl.when((cell == 0) & (half == 0))
    def _():
        w_t[...] = w[...].T
        gain_c[...] = spread_column(gain[...])
        bias_c[...] = spread_column(bias[...])

    stat[...] = jnp.zeros_like(stat)
    own = half == place[0]
    needed = half * genes < counts[cell]

    def low_rows():
        unit, _ = norm_columns(x[0].T.astype(F32))
        return unit * widen(gain_c[...], genes) + widen(bias_c[...], genes)

    def norms(columns, first):
        for h in range(HEADS):
            part = columns[h * head : (h + 1) * head]
            size = jnp.sum(part * part, 0, keepdims=True)
            best = size[:, :128]
            for start in range(128, genes, 128):
                best = jnp.maximum(best, size[:, start : start + 128])
            stat[0, 0, first + h : first + h + 1, :] = best

    @pl.when(needed)
    def _():
        spot = half * genes + lax.broadcasted_iota(jnp.int32, (1, genes), 1)
        valid = spot < counts[cell]
        low = jnp.where(valid, low_rows(), 0.0).astype(BF16)
        low_r = low.T
        packed_t = dot(w_t[width:, :], low)
        kt[0] = packed_t[:width].astype(BF16)
        mark = jnp.where(
            (lax.broadcasted_iota(jnp.int32, (16, genes), 0) == 0) & valid, 1.0, 0.0
        ).astype(BF16)
        for h in range(HEADS):
            va[0, h, :head, :] = packed_t[width + h * head : width + (h + 1) * head].astype(BF16)
            va[0, h, head:, :] = mark
        packed = dot(low_r, w[:, width:])
        kr[0] = packed[:, :width].astype(BF16)
        vr[0] = packed[:, width:].astype(BF16)
        norms(packed_t[:width], 0)

    @pl.when(own)
    def _():
        low = low_rows().astype(BF16)
        query_t = dot(w_t[:width, :], low).astype(BF16) * (head**-0.5)
        qt[0] = query_t
        qr[0] = query_t.T
        norms(query_t.astype(F32), HEADS)

    @pl.when(half == 0)
    def _():
        unit, _ = norm_rows(xc[0].astype(F32))
        low = (unit * gain[...] + bias[...]).astype(BF16)
        pc[0] = dot(low, w[...]).astype(BF16).astype(F32)


def project(counts, place, x_all, xc, gain, bias, w):
    cells, total, width = x_all.shape
    genes = total // 2
    classes = xc.shape[1]
    head = width // HEADS
    whole = lambda shape: pl.BlockSpec(shape, lambda c, h, *_: (0,) * len(shape))
    rows = pl.BlockSpec((1, genes, width), lambda c, h, *_: (c, h, 0))
    columns = pl.BlockSpec((1, width, genes), lambda c, h, *_: (c, 0, h))
    own_rows = pl.BlockSpec((1, genes, width), lambda c, h, *_: (c, 0, 0))
    own_columns = pl.BlockSpec((1, width, genes), lambda c, h, *_: (c, 0, 0))
    per_cell = lambda shape: pl.BlockSpec((1,) + shape, lambda c, h, *_: (c,) + (0,) * len(shape))
    out = lambda shape, kind=BF16: jax.ShapeDtypeStruct(shape, kind)
    return pl.pallas_call(
        project_kernel,
        grid_spec=pltpu.PrefetchScalarGridSpec(
            num_scalar_prefetch=2,
            grid=(cells, 2),
            in_specs=[
                rows,
                per_cell((classes, width)),
                whole((1, width)),
                whole((1, width)),
                whole((width, 3 * width)),
            ],
            out_specs=[
                own_columns,
                own_rows,
                rows,
                rows,
                columns,
                pl.BlockSpec((1, HEADS, head + 16, genes), lambda c, h, *_: (c, 0, 0, h)),
                pl.BlockSpec((1, 1, 8, 128), lambda c, h, *_: (c, h, 0, 0)),
                per_cell((classes, 3 * width)),
            ],
            scratch_shapes=[
                pltpu.VMEM((3 * width, width), BF16),
                pltpu.VMEM((width, 128), F32),
                pltpu.VMEM((width, 128), F32),
            ],
        ),
        out_shape=[
            out((cells, width, genes)),
            out((cells, genes, width)),
            out((cells, total, width)),
            out((cells, total, width)),
            out((cells, width, total)),
            out((cells, HEADS, head + 16, total)),
            out((cells, 2, 8, 128), F32),
            out((cells, classes, 3 * width), F32),
        ],
        compiler_params=pltpu.CompilerParams(vmem_limit_bytes=VMEM),
        name="project",
    )(counts, place, x_all, xc, gain, bias, w)


def gelu_parts(u):
    root = 0.7071067811865476
    t = pl.reciprocal(1.0 + (0.3275911 * root) * jnp.abs(u), approx=True)
    bell = jnp.exp2((-0.5 * LOG2E) * (u * u))
    poly = t * (
        0.127414796
        + t * (-0.142248368 + t * (0.7107068705 + t * (-0.7265760135 + t * 0.5307027145)))
    )
    tail = poly * bell
    phi = jnp.where(u >= 0.0, 1.0 - tail, tail)
    return u * phi, phi + (u * 0.3989422804014327) * bell


def layer_kernel(
    counts,
    qt,
    qr,
    kr,
    vr,
    kt,
    va,
    stat,
    pc,
    x,
    xc,
    cot,
    cotc,
    w_out,
    gain,
    bias,
    w_up,
    b_up,
    w_down,
    b_down,
    y,
    yc,
    dq,
    dqc,
    dk,
    dv,
    dkvc,
    gm,
    gmc,
    g_up,
    g_down,
    g_out,
    g_vec,
    w_out_t,
    w_up_t,
    w_down_t,
    gain_c,
    bias_c,
    b_up_c,
    b_down_c,
    probs,
    probs_ck,
    probs_cq,
    mix,
    shift,
    shift_q,
    inv_sum,
    qz,
    qn,
    dz,
    dn,
    delta,
    att,
    datt,
    x_t,
    dq_t,
    up_acc,
    up_bias_acc,
    gain_acc,
    bias_acc,
    down_bias_acc,
):
    cell = pl.program_id(0)
    cells = pl.num_programs(0)
    genes, width = x.shape[1:]
    classes = xc.shape[1]
    head = width // HEADS
    ff = w_up.shape[1]
    stack = HEADS * classes
    factor = head**-0.5
    count = counts[cell]
    blocks = (count + (KB - 1)) // KB
    total_blocks = kr.shape[1] // KB

    @pl.when(cell == 0)
    def _():
        w_out_t[...] = w_out[...].T
        w_up_t[...] = w_up[...].T
        w_down_t[...] = w_down[...].T
        gain_c[...] = spread_column(gain[...])
        bias_c[...] = spread_column(bias[...])
        b_up_c[...] = spread_column(b_up[...])
        b_down_c[...] = spread_column(b_down[...])
        up_acc[...] = jnp.zeros_like(up_acc)
        up_bias_acc[...] = jnp.zeros_like(up_bias_acc)
        gain_acc[...] = jnp.zeros_like(gain_acc)
        bias_acc[...] = jnp.zeros_like(bias_acc)
        down_bias_acc[...] = jnp.zeros_like(down_bias_acc)
        g_down[...] = jnp.zeros_like(g_down)
        g_out[...] = jnp.zeros_like(g_out)

    head_mask = lax.broadcasted_iota(jnp.int32, (stack, width), 1) // head == (
        lax.broadcasted_iota(jnp.int32, (stack, width), 0) // classes
    )
    pair_mask = lax.broadcasted_iota(jnp.int32, (stack, stack), 1) // classes == (
        lax.broadcasted_iota(jnp.int32, (stack, stack), 0) // classes
    )

    def by_head(rows):
        return jnp.where(head_mask, jnp.concatenate([rows] * HEADS, 0), 0.0)

    def from_heads(rows):
        kept = jnp.where(head_mask, rows, 0.0)
        total = kept[:classes]
        for h in range(1, HEADS):
            total = total + kept[h * classes : (h + 1) * classes]
        return total

    packed_c = pc[0]
    query_c = by_head(packed_c[:, :width] * factor)
    key_c = by_head(packed_c[:, width : 2 * width])
    value_c = by_head(packed_c[:, 2 * width :])
    key_c_t = key_c.T.astype(BF16)
    value_c_t = value_c.T.astype(BF16)
    query_cb, key_cb, value_cb = query_c.astype(BF16), key_c.astype(BF16), value_c.astype(BF16)

    half_rows = lax.broadcasted_iota(jnp.int32, (2 * head, genes), 0) // head
    half_lanes = lax.broadcasted_iota(jnp.int32, (genes, 2 * head), 1) // head
    for h in range(HEADS):
        pair = slice((h // 2) * 2 * head, (h // 2 + 1) * 2 * head)
        qz[h] = jnp.where(half_rows == h % 2, qt[0, pair, :].astype(F32), 0.0).astype(BF16)
        qn[h] = jnp.where(half_lanes == h % 2, qr[0, :, pair].astype(F32), 0.0).astype(BF16)

    size_k = jnp.max(jnp.maximum(stat[0, 0, :HEADS], stat[0, 1, :HEADS]))
    size_q = jnp.max(jnp.maximum(stat[0, 0, HEADS:], stat[0, 1, HEADS:]))
    size_k = jnp.maximum(size_k, jnp.max(jnp.sum(key_c * key_c, -1, keepdims=True)))
    size_q = jnp.maximum(size_q, jnp.max(jnp.sum(query_c * query_c, -1, keepdims=True)))
    safe = size_k * size_q < SAFE * SAFE

    def key_mask(start, shape, axis):
        return start + lax.broadcasted_iota(jnp.int32, shape, axis) < count

    shift[...] = jnp.zeros_like(shift)
    shift_q[...] = jnp.zeros_like(shift_q)

    @pl.when(jnp.logical_not(safe))
    def _():
        class_scores = dot(key_cb, qt[0])
        for h in range(HEADS):
            shift[h] = jnp.max(class_scores[h * classes : (h + 1) * classes], 0, keepdims=True)
        own_scores = jnp.where(pair_mask, dot(query_cb, key_c_t), -1e30)
        shift_q[...] = jnp.broadcast_to(jnp.max(own_scores, -1, keepdims=True), shift_q.shape)

        @pl.loop(0, blocks)
        def _(block):
            start = pl.multiple_of(block * KB, KB)
            for h in range(HEADS):
                scores = dot(
                    kr[0, pl.ds(start, KB), (h // 2) * 2 * head : (h // 2 + 1) * 2 * head], qz[h]
                )
                scores = jnp.where(key_mask(start, scores.shape, 0), scores, -1e30)
                shift[h] = jnp.maximum(shift[h], jnp.max(scores, 0, keepdims=True))
            scores = dot(query_cb, kt[0, :, pl.ds(start, KB)])
            scores = jnp.where(key_mask(start, scores.shape, 1), scores, -1e30)
            shift_q[...] = jnp.maximum(shift_q[...], jnp.max(scores, -1, keepdims=True))

        shift[...] = shift[...] * LOG2E
        shift_q[...] = shift_q[...] * LOG2E

    class_scores = dot(key_cb, qt[0])
    shift_rows = jnp.concatenate(
        [jnp.broadcast_to(shift[h], (classes, genes)) for h in range(HEADS)], 0
    )
    class_exp = jnp.exp2(class_scores * LOG2E - shift_rows).astype(BF16)
    probs_ck[...] = class_exp
    class_mix = dot(value_c_t, class_exp)
    for h in range(HEADS):
        mix[h, :head, :] = class_mix[h * head : (h + 1) * head]
        sums = jnp.sum(
            class_exp[h * classes : (h + 1) * classes].astype(F32), 0, keepdims=True
        )
        mix[h, head:, :] = jnp.where(
            lax.broadcasted_iota(jnp.int32, (16, genes), 0) == 0, sums, 0.0
        )
    shift_qc = shift_q[:, :1]
    own_exp = jnp.where(
        pair_mask, jnp.exp2(dot(query_cb, key_c_t) * LOG2E - shift_qc), 0.0
    ).astype(BF16)
    own_mix = dot(own_exp, value_cb)
    own_sum = jnp.sum(own_exp.astype(F32), -1, keepdims=True)

    def forward_block(block, carried, shifted):
        class_total, class_sum = carried
        start = pl.multiple_of(block * KB, KB)
        keys = pl.ds(start, KB)
        scores = [
            dot(kr[0, keys, (h // 2) * 2 * head : (h // 2 + 1) * 2 * head], qz[h])
            for h in range(1)
        ]
        class_scores = dot(query_cb, kt[0, :, keys]) * LOG2E - shift_qc
        for h in range(HEADS):
            if h + 1 < HEADS:
                g = h + 1
                scores.append(
                    dot(kr[0, keys, (g // 2) * 2 * head : (g // 2 + 1) * 2 * head], qz[g])
                )
            scaled = scores[h] * LOG2E
            if shifted:
                scaled = jnp.minimum(scaled - shift[h], 60.0)
            exps = jnp.exp2(scaled).astype(BF16)
            probs[h, keys, :] = exps
            mix[h] += dot(va[0, h, :, keys], exps)
        class_exp = jnp.where(
            key_mask(start, class_scores.shape, 1), jnp.exp2(class_scores), 0.0
        ).astype(BF16)
        probs_cq[:, keys] = class_exp
        class_total = class_total + dot(class_exp, vr[0, keys, :])
        class_sum = class_sum + jnp.sum(class_exp.astype(F32), -1, keepdims=True)
        return class_total, class_sum

    carried = lax.cond(
        safe,
        lambda: lax.fori_loop(
            0, blocks, functools.partial(forward_block, shifted=False), (own_mix, own_sum)
        ),
        lambda: lax.fori_loop(
            0, blocks, functools.partial(forward_block, shifted=True), (own_mix, own_sum)
        ),
    )
    class_total, class_sum = carried
    class_inv = 1.0 / class_sum
    class_att = from_heads(class_total * class_inv)
    for h in range(HEADS):
        inverse = 1.0 / mix[h, head : head + 1, :]
        inv_sum[h] = inverse
        att[h * head : (h + 1) * head, :genes] = (mix[h, :head, :] * inverse).astype(BF16)

    def pad_rows(rows):
        return jnp.concatenate([rows, jnp.zeros((128 - rows.shape[0], width), F32)], 0)

    x_t[:, :genes] = x[0].T.astype(F32)
    x_t[:, genes:] = pad_rows(xc[0].astype(F32)).T
    att[:, genes:] = pad_rows(class_att).T.astype(BF16)

    def feed(start, columns, with_class):
        lanes = columns + (128 if with_class else 0)
        span = pl.ds(start, lanes)
        wide_gain, wide_bias = widen(gain_c[...], lanes), widen(bias_c[...], lanes)
        cot_r = cot[0, pl.ds(start, columns), :]
        cot_t = cot_r.T
        if with_class:
            padded = pad_rows(cotc[0].astype(F32))
            cot_t = jnp.concatenate([cot_t, padded.T.astype(BF16)], 1)
            cot_r = jnp.concatenate([cot_r, (padded * 0.5).astype(BF16)], 0)
            share = jnp.where(
                lax.broadcasted_iota(jnp.int32, (1, lanes), 1) < columns, 1.0, 0.5
            )
            weigh = lambda values: values * share
            row_share = jnp.where(
                lax.broadcasted_iota(jnp.int32, (lanes, 1), 0) < columns, 1.0, 0.5
            )
            weigh_rows = lambda rows: (rows.astype(F32) * row_share).astype(BF16)
        else:
            weigh = lambda values: values
            weigh_rows = lambda rows: rows
        att_low = att[:, span]
        middle = x_t[:, span] + dot(w_out_t[...], att_low)
        grad_act = dot(w_down[...], cot_t)
        unit, inverse = norm_columns(middle)
        low = (unit * wide_gain + wide_bias).astype(BF16)
        up = dot(w_up_t[...], low) + widen(b_up_c[...], lanes)
        active, slope = gelu_parts(up)
        active = active.astype(BF16)
        grad_up = slope * grad_act
        up_bias_acc[...] += fold_lanes(weigh(grad_up))
        grad_up = grad_up.astype(BF16)
        result = middle + dot(w_down_t[...], active) + widen(b_down_c[...], lanes)
        back = dot(w_up[...], grad_up)
        scaled = back * wide_gain
        scale = 1.0 / width
        grad_middle = cot_t.astype(F32) + inverse * (
            scaled
            - jnp.sum(scaled, 0, keepdims=True) * scale
            - unit * (jnp.sum(scaled * unit, 0, keepdims=True) * scale)
        )
        grad_middle = grad_middle.astype(BF16)
        datt[:, span] = dot(w_out[...], grad_middle).astype(BF16)
        gain_acc[...] += fold_lanes(weigh(back * unit))
        bias_acc[...] += fold_lanes(weigh(back))
        middle_r = grad_middle.T
        g_down[...] += dot(active, cot_r)
        up_acc[...] += dot(grad_up, weigh_rows(low.T))
        g_out[...] += dot(att_low, weigh_rows(middle_r))
        cot_sum = jnp.sum(cot_r.astype(F32), 0, keepdims=True)
        down_bias_acc[...] += cot_sum
        result_r = result.T
        y[0, pl.ds(start, columns), :] = result_r[:columns].astype(BF16)
        gm[0, pl.ds(start, columns), :] = middle_r[:columns]
        if with_class:
            yc[0] = result_r[columns : columns + classes].astype(BF16)
            gmc[0] = middle_r[columns:].astype(F32)[:classes]

    feed_step = 256
    pieces = genes // feed_step

    @pl.loop(0, pieces - 1)
    def _(piece):
        feed(pl.multiple_of(piece * feed_step, feed_step), feed_step, False)

    feed((pieces - 1) * feed_step, feed_step, True)

    for h in range(HEADS):
        own = slice(h * head, (h + 1) * head)
        inverse = inv_sum[h]
        grad = (datt[own, :genes].astype(F32) * inverse).astype(BF16)
        delta[h] = jnp.sum(grad.astype(F32) * (mix[h, :head, :] * inverse), 0, keepdims=True)
        datt[own, :genes] = grad
        blank = jnp.zeros_like(grad)
        dz[h] = jnp.concatenate([grad, blank] if h % 2 == 0 else [blank, grad], 0)
    grad_r = datt[:, :genes].T
    for h in range(HEADS):
        pair = slice((h // 2) * 2 * head, (h // 2 + 1) * 2 * head)
        dn[h] = jnp.where(half_lanes == h % 2, grad_r[:, pair].astype(F32), 0.0).astype(BF16)

    class_grad = datt[:, genes:].astype(F32).T[:classes]
    class_grad = by_head(class_grad) * class_inv
    class_grad_b = class_grad.astype(BF16)
    class_grad_h = (class_grad * 0.5).astype(BF16)
    query_ch = (query_c * 0.5).astype(BF16)
    class_delta = jnp.sum(
        class_grad_b.astype(F32) * (class_total * class_inv), -1, keepdims=True
    )

    class_dprob = dot(value_cb, datt[:, :genes])
    delta_rows = jnp.concatenate(
        [jnp.broadcast_to(delta[h], (classes, genes)) for h in range(HEADS)], 0
    )
    class_probs = probs_ck[...]
    class_dscore = (class_probs.astype(F32) * (class_dprob - delta_rows)).astype(BF16)
    dq_t[...] = dot(key_c_t, class_dscore)
    class_dkey = dot(class_dscore, qr[0])
    class_dvalue = dot(class_probs, grad_r)
    own_dprob = dot(class_grad_b, value_c_t)
    own_dscore = (own_exp.astype(F32) * (own_dprob - class_delta)).astype(BF16)
    class_dquery = dot(own_dscore, key_cb)
    class_dkey = class_dkey + dot(own_dscore.astype(F32).T.astype(BF16), query_ch)
    class_dvalue = class_dvalue + dot(own_exp.astype(F32).T.astype(BF16), class_grad_h)

    def backward_block(block, class_dquery):
        start = pl.multiple_of(block * KB, KB)
        keys = pl.ds(start, KB)
        class_weights = probs_cq[:, keys]
        class_dprob = dot_nt(class_grad_b, vr[0, keys, :])
        dprobs = [dot(vr[0, keys, : 2 * head], dz[0])]
        class_dscore = (class_weights.astype(F32) * (class_dprob - class_delta)).astype(BF16)
        dkey = dot_tn(class_dscore, query_ch)
        dvalue = dot_tn(class_weights, class_grad_h)
        dkeys = [dkey[:, : 2 * head], dkey[:, 2 * head :]]
        dvalues = [dvalue[:, : 2 * head], dvalue[:, 2 * head :]]
        for h in range(HEADS):
            if h + 1 < HEADS:
                g = h + 1
                dprobs.append(
                    dot(vr[0, keys, (g // 2) * 2 * head : (g // 2 + 1) * 2 * head], dz[g])
                )
            weights = probs[h, keys, :]
            dscore = weights * (dprobs[h] - delta[h]).astype(BF16)
            own = slice(h * head, (h + 1) * head)
            dq_t[own, :] += dot(kt[0, own, keys], dscore)
            dkeys[h // 2] = dkeys[h // 2] + dot(dscore, qn[h])
            dvalues[h // 2] = dvalues[h // 2] + dot(weights, dn[h])
        valid = key_mask(start, (KB, width), 0)
        dk[0, keys, :] = jnp.where(valid, jnp.concatenate(dkeys, 1), 0.0).astype(BF16)
        dv[0, keys, :] = jnp.where(valid, jnp.concatenate(dvalues, 1), 0.0).astype(BF16)
        return class_dquery + dot(class_dscore, kr[0, keys, :])

    class_dquery = lax.fori_loop(0, blocks, backward_block, class_dquery)

    @pl.loop(blocks, total_blocks)
    def _(block):
        keys = pl.ds(pl.multiple_of(block * KB, KB), KB)
        dk[0, keys, :] = jnp.zeros((KB, width), BF16)
        dv[0, keys, :] = jnp.zeros((KB, width), BF16)

    dq[0] = (dq_t[...] * factor).astype(BF16).T
    dqc[0] = from_heads(class_dquery) * factor
    dkvc[0] = jnp.concatenate([from_heads(class_dkey), from_heads(class_dvalue)], 1)

    @pl.when(cell == cells - 1)
    def _():
        g_up[...] = up_acc[...].T
        g_vec[...] = jnp.zeros_like(g_vec)
        g_vec[0:1, :] = jnp.sum(up_bias_acc[...].T, 0, keepdims=True)
        g_vec[1:2, :width] = jnp.sum(gain_acc[...].T, 0, keepdims=True)
        g_vec[1:2, width : 2 * width] = jnp.sum(bias_acc[...].T, 0, keepdims=True)
        g_vec[1:2, 2 * width : 3 * width] = down_bias_acc[...]


def layer(
    counts, tables, x, xc, cot, cotc, w_out, gain, bias, w_up, b_up, w_down, b_down
):
    cells, genes, width = x.shape
    classes = xc.shape[1]
    total = tables[2].shape[1]
    head = width // HEADS
    ff = w_up.shape[1]
    stack = HEADS * classes
    whole = lambda shape: pl.BlockSpec(
        shape, lambda c, *_: (0,) * len(shape), pipeline_mode=pl.Buffered(1)
    )
    per_cell = lambda *shape: pl.BlockSpec((1,) + shape, lambda c, *_: (c,) + (0,) * len(shape))
    kept = lambda *shape: pl.BlockSpec(shape, lambda c, *_: (0,) * len(shape))
    out = lambda shape, kind=BF16: jax.ShapeDtypeStruct(shape, kind)
    vmem = lambda *shape, kind=BF16: pltpu.VMEM(shape, kind)
    f32 = functools.partial(vmem, kind=F32)
    return pl.pallas_call(
        layer_kernel,
        grid_spec=pltpu.PrefetchScalarGridSpec(
            num_scalar_prefetch=1,
            grid=(cells,),
            in_specs=[
                per_cell(width, genes),
                per_cell(genes, width),
                per_cell(total, width),
                per_cell(total, width),
                per_cell(width, total),
                per_cell(HEADS, head + 16, total),
                per_cell(2, 8, 128),
                per_cell(classes, 3 * width),
                per_cell(genes, width),
                per_cell(classes, width),
                per_cell(genes, width),
                per_cell(classes, width),
                whole((width, width)),
                whole((1, width)),
                whole((1, width)),
                whole((width, ff)),
                whole((1, ff)),
                whole((ff, width)),
                whole((1, width)),
            ],
            out_specs=[
                per_cell(genes, width),
                per_cell(classes, width),
                per_cell(genes, width),
                per_cell(classes, width),
                per_cell(total, width),
                per_cell(total, width),
                per_cell(classes, 2 * width),
                per_cell(genes, width),
                per_cell(classes, width),
                kept(width, ff),
                kept(ff, width),
                kept(width, width),
                kept(8, ff),
            ],
            scratch_shapes=[
                vmem(width, width),
                vmem(ff, width),
                vmem(width, ff),
                f32(width, 128),
                f32(width, 128),
                f32(ff, 128),
                f32(width, 128),
                vmem(HEADS, total, genes),
                vmem(stack, genes),
                vmem(stack, total),
                f32(HEADS, head + 16, genes),
                f32(HEADS, 1, genes),
                f32(stack, 128),
                f32(HEADS, 1, genes),
                vmem(HEADS, 2 * head, genes),
                vmem(HEADS, genes, 2 * head),
                vmem(HEADS, 2 * head, genes),
                vmem(HEADS, genes, 2 * head),
                f32(HEADS, 1, genes),
                vmem(width, genes + 128),
                vmem(width, genes + 128),
                f32(width, genes + 128),
                f32(width, genes),
                f32(ff, width),
                f32(ff, 128),
                f32(width, 128),
                f32(width, 128),
                f32(1, width),
            ],
        ),
        out_shape=[
            out((cells, genes, width)),
            out((cells, classes, width)),
            out((cells, genes, width)),
            out((cells, classes, width), F32),
            out((cells, total, width)),
            out((cells, total, width)),
            out((cells, classes, 2 * width), F32),
            out((cells, genes, width)),
            out((cells, classes, width), F32),
            out((width, ff), F32),
            out((ff, width), F32),
            out((width, width), F32),
            out((8, ff), F32),
        ],
        compiler_params=pltpu.CompilerParams(vmem_limit_bytes=VMEM),
        name="layer",
    )(counts, *tables, x, xc, cot, cotc, w_out, gain, bias, w_up, b_up, w_down, b_down)


def tokens_kernel(
    x, xc, gm, gmc, dq, dqc, dk, dv, dkvc, gain, bias, w, g_x, g_xc, g_qkv, g_vec, w_t
):
    cell = pl.program_id(0)
    genes, width = x.shape[1:]
    classes = xc.shape[1]

    @pl.when(cell == 0)
    def _():
        w_t[...] = w[...].T
        g_qkv[...] = jnp.zeros_like(g_qkv)
        g_vec[...] = jnp.zeros_like(g_vec)

    blank = jnp.zeros((16 - classes, width), F32)

    def joined(genes_part, class_part):
        return jnp.concatenate([genes_part.astype(F32), class_part.astype(F32), blank], 0)

    unit, inverse = norm_rows(joined(x[0], xc[0]))
    low = (unit * gain[...] + bias[...]).astype(BF16)
    rows = genes + 16
    spot = lax.broadcasted_iota(jnp.int32, (rows, 1), 0)
    share = jnp.where(spot < genes, 1.0, jnp.where(spot < genes + classes, 0.5, 0.0))
    class_grads = [dqc[0], dkvc[0][:, :width], dkvc[0][:, width:]]
    packed = jnp.concatenate(
        [
            jnp.concatenate([part, jnp.concatenate([class_part, blank], 0).astype(BF16)], 0)
            for part, class_part in zip((dq[0], dk[0], dv[0]), class_grads)
        ],
        1,
    )
    back = dot(packed, w_t[...])
    g_qkv[...] += dot_tn((low.astype(F32) * share).astype(BF16), packed)
    weighed = back * share
    g_vec[0:1, :] += jnp.sum(weighed * unit, 0, keepdims=True)
    g_vec[1:2, :] += jnp.sum(weighed, 0, keepdims=True)
    scaled = back * gain[...]
    result = joined(gm[0], gmc[0]) + inverse * (
        scaled
        - jnp.mean(scaled, -1, keepdims=True)
        - unit * jnp.mean(scaled * unit, -1, keepdims=True)
    )
    g_x[0] = result[:genes].astype(BF16)
    g_xc[0] = result[genes : genes + classes].astype(BF16)


def tokens(x, xc, gm, gmc, dq, dqc, dk, dv, dkvc, gain, bias, w):
    cells, genes, width = x.shape
    classes = xc.shape[1]
    whole = lambda shape: pl.BlockSpec(shape, lambda c: (0,) * len(shape))
    per_cell = lambda *shape: pl.BlockSpec((1,) + shape, lambda c: (c,) + (0,) * len(shape))
    out = lambda shape, kind=BF16: jax.ShapeDtypeStruct(shape, kind)
    return pl.pallas_call(
        tokens_kernel,
        grid=(cells,),
        in_specs=[
            per_cell(genes, width),
            per_cell(classes, width),
            per_cell(genes, width),
            per_cell(classes, width),
            per_cell(genes, width),
            per_cell(classes, width),
            per_cell(genes, width),
            per_cell(genes, width),
            per_cell(classes, 2 * width),
            whole((1, width)),
            whole((1, width)),
            whole((width, 3 * width)),
        ],
        out_specs=[
            per_cell(genes, width),
            per_cell(classes, width),
            whole((width, 3 * width)),
            whole((8, width)),
        ],
        out_shape=[
            out((cells, genes, width)),
            out((cells, classes, width)),
            out((width, 3 * width), F32),
            out((8, width), F32),
        ],
        scratch_shapes=[pltpu.VMEM((3 * width, width), BF16)],
        compiler_params=pltpu.CompilerParams(vmem_limit_bytes=VMEM),
        name="tokens",
    )(x, xc, gm, gmc, dq, dqc, dk, dv, dkvc, gain, bias, w)


def shards(
    gene_in,
    class_in,
    expressed,
    ln1_gain,
    ln1_bias,
    w_qkv,
    w_out,
    ln2_gain,
    ln2_bias,
    w_up,
    b_up,
    w_down,
    b_down,
    gene_cot,
    class_cot,
):
    width = gene_in.shape[-1]
    row = lambda vector: vector.reshape(1, -1)
    place = lax.axis_index("gene").reshape(1)
    everything = lax.all_gather(gene_in, "gene", axis=1, tiled=True)
    tables = project(
        expressed, place, everything, class_in, row(ln1_gain), row(ln1_bias), w_qkv
    )
    gene_out, class_out, dq, dqc, dk, dv, dkvc, gm, gmc, g_up, g_down, g_out, g_vec = layer(
        expressed,
        tables,
        gene_in,
        class_in,
        gene_cot,
        class_cot,
        w_out,
        row(ln2_gain),
        row(ln2_bias),
        w_up,
        row(b_up),
        w_down,
        row(b_down),
    )
    dk = lax.psum_scatter(dk, "gene", scatter_dimension=1, tiled=True)
    dv = lax.psum_scatter(dv, "gene", scatter_dimension=1, tiled=True)
    dkvc = lax.psum(dkvc, "gene")
    gene_grad, class_grad, g_qkv, g_vec1 = tokens(
        gene_in,
        class_in,
        gm,
        gmc,
        dq,
        dqc,
        dk,
        dv,
        dkvc,
        row(ln1_gain),
        row(ln1_bias),
        w_qkv,
    )
    g_up, g_down, g_out, g_vec, g_qkv, g_vec1 = lax.psum(
        (g_up, g_down, g_out, g_vec, g_qkv, g_vec1), ("cell", "gene")
    )
    return (
        gene_out,
        class_out,
        gene_grad,
        class_grad,
        g_vec1[0],
        g_vec1[1],
        g_qkv,
        g_out,
        g_vec[1, :width],
        g_vec[1, width : 2 * width],
        g_up,
        g_vec[0],
        g_down,
        g_vec[1, 2 * width : 3 * width],
    )


def solution(mesh):
    genes, cells, whole = P("cell", "gene", None), P("cell", None, None), P()
    return jax.shard_map(
        shards,
        mesh=mesh,
        in_specs=(genes, cells, P("cell")) + (whole,) * 10 + (genes, cells),
        out_specs=(genes, cells, genes, cells) + (whole,) * 10,
        check_vma=False,
    )
```

time: 940 us -> 388 us (0.41)
  matrix products: 446 us -> 0 us
  local copies, waits for them, and re-layouts: 196 us -> 7.72 us
  Pallas kernels: 0 us -> 128 us
  other arithmetic: 126 us -> 0 us
  waiting for transfers between devices: 90 us -> 191 us
  blocking collectives: 51.3 us -> 39.6 us
    dot_general x136 -> x0, matrix products: 446 us -> none  [the longest x8 74.2 us: pair_one_block(): jnp.einsum('qhd,khd->hqk', query_heads, gene_keys, preferred_element_type...]
    pallas_call x0 -> x3, Pallas kernels: none -> 128 us  [the longest x1 102 us: layer(): pl.pallas_call(layer_kernel, grid_spec=pltpu.PrefetchScalarGridSpec(num_s...]
    psum x1 -> x2, waiting for transfers between devices: 89.9 us -> 140 us  [the longest x1 96.6 us: shards(): lax.psum((g_up, g_down, g_out, g_vec, g_qkv, g_vec1), ('cell', 'gene'))]
    dynamic_update_slice x52 -> x0, local copies, waits for them, and re-layouts: 47.8 us -> none  [the longest x8 17.6 us: shards(): lax.map(cell_both, (gene_queries, gene_grads, gene_max, gene_sum, gene_de...]
    reduce_sum x22 -> x0, other arithmetic: 45.6 us -> none  [the longest x16 34.7 us: attend_one_block(): row_sum = jnp.sum(class_exp, -1) + jnp.sum(gene_exp, -1)]
    convert_element_type x2 -> x0, other arithmetic: 41.2 us -> none  [the longest x1 41.2 us: shards(): activated_low = activated.astype(jnp.bfloat16)]
    dynamic_slice x64 -> x0, local copies, waits for them, and re-layouts: 37.3 us -> none  [the longest x16 19.3 us: shards(): lax.map(cell_attend, (queries[:, class_count:], class_tables, gene_table,...]
    slice x31 -> x2, local copies, waits for them, and re-layouts: 35.7 us -> 1.18 us  [the longest x1 0.6 us: shards(): g_vec[0]]
  transfers between devices with their start and end apart: 3 -> 5, of which waited for: 1 -> 5; matrix products, arithmetic and copies ran while one was open for 9% -> 0% of each run, Pallas kernels for 0% -> 0%
where the time goes in v1:
time: 388 us; the launch traced here: 380 us
  waiting for transfers between devices  191 us (49%)
  Pallas kernels  128 us (33%)
  blocking collectives  39.6 us (10%)
  between operations  13.8 us (4%)
  local copies, waits for them, and re-layouts  7.72 us (2%)
    pallas_call x1, Pallas kernels, layer(): pl.pallas_call(layer_kernel, grid_spec=pltpu.PrefetchScalarGridSpec(num_s...  102 us
    psum x1, waiting for transfers between devices, shards(): lax.psum((g_up, g_down, g_out, g_vec, g_qkv, g_vec1), ('cell', 'gene'))  96.6 us
    psum x1, waiting for transfers between devices, shards(): dkvc = lax.psum(dkvc, 'gene')  43.7 us
    psum x1, blocking collectives, shards(): lax.psum((g_up, g_down, g_out, g_vec, g_qkv, g_vec1), ('cell', 'gene'))  39.6 us
    all_gather x1, waiting for transfers between devices, shards(): everything = lax.all_gather(gene_in, 'gene', axis=1, tiled=True)  17.3 us
    pallas_call x1, Pallas kernels, project(): pl.pallas_call(project_kernel, grid_spec=pltpu.PrefetchScalarGridSpec(num...  15.9 us
    reduce_scatter x1, waiting for transfers between devices, shards(): dv = lax.psum_scatter(dv, 'gene', scatter_dimension=1, tiled=True)  15.6 us
    reduce_scatter x1, waiting for transfers between devices, shards(): dk = lax.psum_scatter(dk, 'gene', scatter_dimension=1, tiled=True)  15.6 us
  transfers between devices with their start and end apart: 5, of which 5 were waited for; matrix products, arithmetic and copies ran while one was open for 0% of the time, Pallas kernels for 0%

profile of v1, /device:TPU:3, one launch (start us, length us, event | category | flops | bytes accessed | tf_op | source)
XLA Modules:
  0.0 380.5 jit_solution(15630983735224859667)
XLA Ops:
  7.2 0.0 all-gather.2.cloned.1.call-start
  7.2 0.7 all-gather.2.cloned.1.call-update
  7.9 0.0 all-reduce.5.cloned.1.call-start
  8.0 17.3 %all-gather.2.cloned.1.call-done.x = bf16[4,2048,256]{2,1,0:T(8,128)(2,1)} async-done(((bf16[4,1024,256]{2,1,0:T(8,128)(2,1)}), bf16[4,2048,256]{2,1,0:T(8,128)(2,1)}) %all-gather.2.cloned.1.call-update) | async-done | bytes 4194320 | tf_op jit(solution)/shard_map/all_gather | solution.py:797
  25.2 15.9 %project.1 = (bf16[4,256,1024]{2,1,0:T(8,128)(2,1)}, bf16[4,1024,256]{2,1,0:T(8,128)(2,1)}, bf16[4,2048,256]{2,1,0:T(8,128)(2,1)}, bf16[4,2048,256]{2,1,0:T(8,12...) custom-call(s32[4]{0:T(128)} %counts.3, ...), custom_call_target="tpu_custom_call" | custom-call | tf_op jit(solution)/shard_map/project/pallas_call | solution.py:136
  41.1 102.2 %layer.1 = (bf16[4,1024,256]{2,1,0:T(8,128)(2,1)}, bf16[4,8,256]{2,1,0:T(8,128)(2,1)}, bf16[4,1024,256]{2,1,0:T(8,128)(2,1)}, f32[4,8,256]{2,1,0:T(8,128)}, bf16...) custom-call(s32[4]{0:T(128)} %counts.3, ...), custom_call_target="tpu_custom_call" | custom-call | tf_op jit(solution)/shard_map/layer/pallas_call | solution.py:598
  143.3 0.0 reduce-scatter.3.cloned.1.call-start
  143.4 0.7 reduce-scatter.3.cloned.1.call-update
  144.1 0.0 reduce-scatter.5.cloned.1.call-start
  144.1 0.5 reduce-scatter.5.cloned.1.call-update
  144.6 0.0 all-reduce.7.cloned.1.call-start
  144.7 43.7 %all-reduce.5.cloned.1.call-done.dkvc = f32[4,8,512]{2,1,0:T(8,128)} async-done(((f32[4,8,512]{2,1,0:T(8,128)}), f32[4,8,512]{2,1,0:T(8,128)}) %all-reduce.5.cloned.1.call-update) | async-done | bytes 65552 | tf_op jit(solution)/shard_map/psum | solution.py:818
  188.4 15.6 %reduce-scatter.3.cloned.1.call-done.dk = bf16[4,1024,256]{2,1,0:T(8,128)(2,1)} async-done(((bf16[4,2048,256]{2,1,0:T(8,128)(2,1)}), bf16[4,1024,256]{2,1,0:T(8,128)(2,1)}) %reduce-scatter.3.cloned.1.call-update) | async-done | bytes 2097168 | tf_op jit(solution)/shard_map/reduce_scatter | solution.py:816
  204.0 15.6 %reduce-scatter.5.cloned.1.call-done.dv = bf16[4,1024,256]{2,1,0:T(8,128)(2,1)} async-done(((bf16[4,2048,256]{2,1,0:T(8,128)(2,1)}), bf16[4,1024,256]{2,1,0:T(8,128)(2,1)}) %reduce-scatter.5.cloned.1.call-update) | async-done | bytes 2097168 | tf_op jit(solution)/shard_map/reduce_scatter | solution.py:817
  219.6 10.3 %tokens.1 = (bf16[4,1024,256]{2,1,0:T(8,128)(2,1)}, bf16[4,8,256]{2,1,0:T(8,128)(2,1)}, f32[256,768]{1,0:T(8,128)}, f32[8,256]{1,0:T(8,128)}) custom-call(bf16[4,1024,256]{2,1,0:T(8,128)(2,1)} %x.3, bf16[4,8,256]{2,1,0:T(8,128)(2,1)} %xc.5, bf16[4,1024,256]{2,1,0:T(8,128)(2,1)} %get-tuple-element.49.gm, f32[4,8,256]{2,1,0:T(8,128)} %get-tuple-element.50.gmc, ...), custom_call_target="tpu_custom_call" | custom-call | tf_op jit(solution)/shard_map/tokens/pallas_call | solution.py:742
  230.0 0.7 copy-done.2
  230.7 39.6 %all-reduce = (f32[8,256]{1,0:T(8,128)S(1)}, f32[8,1024]{1,0:T(8,128)S(1)}) all-reduce(f32[8,256]{1,0:T(8,128)S(1)} %copy-done.3, f32[8,1024]{1,0:T(8,128)S(1)} %copy-done.2), channel_id=1, replica_groups=mesh['cell'=16,'gene'=2] {'cell','gene'}, use_global_device_ids=true, to_apply=%region_3.0 | all-reduce | flops 10240 | bytes 81920 | tf_op jit(solution)/shard_map/psum | solution.py:833
  270.3 0.6 slice.28
  270.9 0.6 fusion
  271.5 96.6 %all-reduce.7.cloned.1.call-done = (f32[256,768]{1,0:T(8,128)}, f32[256,256]{1,0:T(8,128)}, f32[256,1024]{1,0:T(8,128)}, f32[1024,256]{1,0:T(8,128)}) async-done(((f32[256,768]{1,0:T(8,128)}, f32[256,256]{1,0:T(8,128)}, f32[256,1024]{1,0:T(8,128)}, f32[1024,256]{1,0:T(8,128)}), (f32[256,768]{1,0:T(8,128)}, f32[256,256]{1,0:T(8,128)}, f32[256,1024]{1,0:T(8,128)}, ...) | async-done | bytes 3145744 | tf_op jit(solution)/shard_map/psum | solution.py:833
  368.1 2.2 copy.34
  370.3 1.7 copy.35
  372.0 1.0 copy.36
  373.0 1.0 copy.37
  (9 shorter events, 0.0 us)
Async XLA Ops:
  7.2 18.0 %all-gather.2.cloned.1.call-start = ((), (), s32[]{:S(2)}) async-start(), calls=%async_computation.2 | async-start | bytes 6291456 | tf_op jit(solution)/shard_map/all_gather | solution.py:797
  7.9 180.5 %all-reduce.5.cloned.1.call-start = ((), (), s32[]{:S(2)}) async-start(), calls=%async_computation.5 | async-start | bytes 131072 | tf_op jit(solution)/shard_map/psum | solution.py:818
  143.3 60.7 %reduce-scatter.3.cloned.1.call-start = ((), (), s32[]{:S(2)}) async-start(), calls=%async_computation.3 | async-start | bytes 6291456 | tf_op jit(solution)/shard_map/reduce_scatter | solution.py:816
  144.1 75.5 %reduce-scatter.5.cloned.1.call-start = ((), (), s32[]{:S(2)}) async-start(), calls=%async_computation.4 | async-start | bytes 6291456 | tf_op jit(solution)/shard_map/reduce_scatter | solution.py:817
  144.6 223.5 %all-reduce.7.cloned.1.call-start = ((), (), s32[]{:S(2)}) async-start(), calls=%async_computation.6 | async-start | bytes 6291456 | tf_op jit(solution)/shard_map/psum | solution.py:833
  229.9 0.8 copy-start.2
  229.9 0.8 copy-start.3
  368.1 3.9 %copy-start.1 = (f32[256,1024]{1,0:T(8,128)S(1)}, f32[256,1024]{1,0:T(8,128)}, u32[]{:S(2)}) copy-start(f32[256,1024]{1,0:T(8,128)} %get-tuple-element.87) | copy-start | bytes 3145732
  368.1 4.9 %copy-start = (f32[1024,256]{1,0:T(8,128)S(1)}, f32[1024,256]{1,0:T(8,128)}, u32[]{:S(2)}) copy-start(f32[1024,256]{1,0:T(8,128)} %get-tuple-element.89) | copy-start | bytes 3145732
Sparse Core Ops, SparseCore 0:
  9.6 15.6 all-gather.1
  143.4 44.9 all-reduce.4
  190.7 13.2 reduce-scatter.2
  206.2 13.3 reduce-scatter.4
  230.1 137.9 all-reduce.6

commit v2 on v1

--- a/solution.py
+++ b/solution.py
@@ -12,9 +12,12 @@
 LOG2E = 1.4426950408889634
 SAFE = 40.0
 KB = 256
+STREAMS = 3
+VECTOR_ROWS = 32
 VMEM = 63 * 2**20
 F32 = jnp.float32
 BF16 = jnp.bfloat16
+MESH = pl.DeviceIdType.MESH
 
 
 def dot(left, right):
@@ -57,26 +60,65 @@
     return centered * inverse, inverse
 
 
+def flip(index, stride):
+    return index + stride * (1 - 2 * ((index // stride) % 2))
+
+
+def greet(partners):
+    barrier = pltpu.get_barrier_semaphore()
+    for partner in partners:
+        pl.semaphore_signal(barrier, inc=1, device_id=partner, device_id_type=MESH)
+    pl.semaphore_wait(barrier, len(partners))
+
+
 def project_kernel(
-    counts, place, x, xc, gain, bias, w, qt, qr, kr, vr, kt, va, stat, pc, w_t, gain_c, bias_c
+    counts,
+    x,
+    x_hbm,
+    xc,
+    gain,
+    bias,
+    w,
+    qt,
+    kr,
+    vr,
+    kt,
+    va,
+    ut,
+    stat,
+    pc,
+    w_t,
+    gain_c,
+    bias_c,
+    other,
+    sent,
+    received,
 ):
     cell, half = pl.program_id(0), pl.program_id(1)
+    cells = x_hbm.shape[0]
     genes, width = x.shape[1:]
     head = width // HEADS
+    place = lax.axis_index("gene")
+    partner = {"cell": lax.axis_index("cell"), "gene": 1 - place}
+
+    def swap(index):
+        return pltpu.make_async_remote_copy(
+            src_ref=x_hbm.at[index],
+            dst_ref=other.at[index],
+            send_sem=sent.at[index],
+            recv_sem=received.at[index],
+            device_id=partner,
+            device_id_type=MESH,
+        )
 
     @pl.when((cell == 0) & (half == 0))
     def _():
+        greet([partner])
+        for index in range(cells):
+            swap(index).start()
         w_t[...] = w[...].T
         gain_c[...] = spread_column(gain[...])
         bias_c[...] = spread_column(bias[...])
-
-    stat[...] = jnp.zeros_like(stat)
-    own = half == place[0]
-    needed = half * genes < counts[cell]
-
-    def low_rows():
-        unit, _ = norm_columns(x[0].T.astype(F32))
-        return unit * widen(gain_c[...], genes) + widen(bias_c[...], genes)
 
     def norms(columns, first):
         for h in range(HEADS):
@@ -87,13 +129,15 @@
                 best = jnp.maximum(best, size[:, start : start + 128])
             stat[0, 0, first + h : first + h + 1, :] = best
 
-    @pl.when(needed)
-    def _():
-        spot = half * genes + lax.broadcasted_iota(jnp.int32, (1, genes), 1)
+    def tables(values, origin):
+        unit, _ = norm_columns(values.T.astype(F32))
+        ut[0] = unit.astype(BF16)
+        low = unit * widen(gain_c[...], genes) + widen(bias_c[...], genes)
+        spot = origin + lax.broadcasted_iota(jnp.int32, (1, genes), 1)
         valid = spot < counts[cell]
-        low = jnp.where(valid, low_rows(), 0.0).astype(BF16)
-        low_r = low.T
-        packed_t = dot(w_t[width:, :], low)
+        kept = jnp.where(valid, low, 0.0).astype(BF16)
+        packed_t = dot(w_t[width:, :], kept)
+        packed = dot(kept.T, w[:, width:])
         kt[0] = packed_t[:width].astype(BF16)
         mark = jnp.where(
             (lax.broadcasted_iota(jnp.int32, (16, genes), 0) == 0) & valid, 1.0, 0.0
@@ -101,79 +145,88 @@
         for h in range(HEADS):
             va[0, h, :head, :] = packed_t[width + h * head : width + (h + 1) * head].astype(BF16)
             va[0, h, head:, :] = mark
-        packed = dot(low_r, w[:, width:])
         kr[0] = packed[:, :width].astype(BF16)
         vr[0] = packed[:, width:].astype(BF16)
+        stat[...] = jnp.zeros_like(stat)
         norms(packed_t[:width], 0)
-
-    @pl.when(own)
-    def _():
-        low = low_rows().astype(BF16)
-        query_t = dot(w_t[:width, :], low).astype(BF16) * (head**-0.5)
-        qt[0] = query_t
-        qr[0] = query_t.T
-        norms(query_t.astype(F32), HEADS)
+        return low
 
     @pl.when(half == 0)
     def _():
+        low = tables(x[0], place * genes)
+        query_t = dot(w_t[:width, :], low.astype(BF16)).astype(BF16) * (head**-0.5)
+        qt[0] = query_t
+        norms(query_t.astype(F32), HEADS)
         unit, _ = norm_rows(xc[0].astype(F32))
-        low = (unit * gain[...] + bias[...]).astype(BF16)
-        pc[0] = dot(low, w[...]).astype(BF16).astype(F32)
-
-
-def project(counts, place, x_all, xc, gain, bias, w):
-    cells, total, width = x_all.shape
-    genes = total // 2
+        class_low = (unit * gain[...] + bias[...]).astype(BF16)
+        pc[0] = dot(class_low, w[...]).astype(BF16).astype(F32)
+
+    @pl.when(half == 1)
+    def _():
+        swap(cell).wait_recv()
+        tables(other[cell], (1 - place) * genes)
+
+    @pl.when((cell == cells - 1) & (half == 1))
+    def _():
+        for index in range(cells):
+            swap(index).wait_send()
+
+
+def project(counts, x, xc, gain, bias, w):
+    cells, genes, width = x.shape
+    total = 2 * genes
     classes = xc.shape[1]
     head = width // HEADS
-    whole = lambda shape: pl.BlockSpec(shape, lambda c, h, *_: (0,) * len(shape))
-    rows = pl.BlockSpec((1, genes, width), lambda c, h, *_: (c, h, 0))
-    columns = pl.BlockSpec((1, width, genes), lambda c, h, *_: (c, 0, h))
-    own_rows = pl.BlockSpec((1, genes, width), lambda c, h, *_: (c, 0, 0))
-    own_columns = pl.BlockSpec((1, width, genes), lambda c, h, *_: (c, 0, 0))
-    per_cell = lambda shape: pl.BlockSpec((1,) + shape, lambda c, h, *_: (c,) + (0,) * len(shape))
+    whole = lambda shape: pl.BlockSpec(shape, lambda c, h: (0,) * len(shape))
+    rows = pl.BlockSpec((1, genes, width), lambda c, h: (c, h, 0))
+    columns = pl.BlockSpec((1, width, genes), lambda c, h: (c, 0, h))
+    per_cell = lambda *shape: pl.BlockSpec((1,) + shape, lambda c, h: (c,) + (0,) * len(shape))
     out = lambda shape, kind=BF16: jax.ShapeDtypeStruct(shape, kind)
     return pl.pallas_call(
         project_kernel,
-        grid_spec=pltpu.PrefetchScalarGridSpec(
-            num_scalar_prefetch=2,
-            grid=(cells, 2),
-            in_specs=[
-                rows,
-                per_cell((classes, width)),
-                whole((1, width)),
-                whole((1, width)),
-                whole((width, 3 * width)),
-            ],
-            out_specs=[
-                own_columns,
-                own_rows,
-                rows,
-                rows,
-                columns,
-                pl.BlockSpec((1, HEADS, head + 16, genes), lambda c, h, *_: (c, 0, 0, h)),
-                pl.BlockSpec((1, 1, 8, 128), lambda c, h, *_: (c, h, 0, 0)),
-                per_cell((classes, 3 * width)),
-            ],
-            scratch_shapes=[
-                pltpu.VMEM((3 * width, width), BF16),
-                pltpu.VMEM((width, 128), F32),
-                pltpu.VMEM((width, 128), F32),
-            ],
-        ),
+        grid=(cells, 2),
+        in_specs=[
+            pl.BlockSpec(memory_space=pltpu.SMEM),
+            per_cell(genes, width),
+            pl.BlockSpec(memory_space=pl.ANY),
+            per_cell(classes, width),
+            whole((1, width)),
+            whole((1, width)),
+            whole((width, 3 * width)),
+        ],
+        out_specs=[
+            per_cell(width, genes),
+            rows,
+            rows,
+            columns,
+            pl.BlockSpec((1, HEADS, head + 16, genes), lambda c, h: (c, 0, 0, h)),
+            columns,
+            pl.BlockSpec((1, 1, 8, 128), lambda c, h: (c, h, 0, 0)),
+            per_cell(classes, 3 * width),
+        ],
         out_shape=[
             out((cells, width, genes)),
-            out((cells, genes, width)),
             out((cells, total, width)),
             out((cells, total, width)),
             out((cells, width, total)),
             out((cells, HEADS, head + 16, total)),
+            out((cells, width, total)),
             out((cells, 2, 8, 128), F32),
             out((cells, classes, 3 * width), F32),
         ],
-        compiler_params=pltpu.CompilerParams(vmem_limit_bytes=VMEM),
+        scratch_shapes=[
+            pltpu.VMEM((3 * width, width), BF16),
+            pltpu.VMEM((width, 128), F32),
+            pltpu.VMEM((width, 128), F32),
+            pltpu.VMEM((cells, genes, width), BF16),
+            pltpu.SemaphoreType.DMA((cells,)),
+            pltpu.SemaphoreType.DMA((cells,)),
+        ],
+        compiler_params=pltpu.CompilerParams(
+            vmem_limit_bytes=VMEM, collective_id=0, has_side_effects=True
+        ),
         name="project",
-    )(counts, place, x_all, xc, gain, bias, w)
+    )(counts, x, x, xc, gain, bias, w)
 
 
 def gelu_parts(u):
@@ -191,12 +244,13 @@
 
 def layer_kernel(
     counts,
+    place,
     qt,
-    qr,
     kr,
     vr,
     kt,
     va,
+    ut,
     stat,
     pc,
     x,
@@ -214,14 +268,11 @@
     yc,
     dq,
     dqc,
-    dk,
-    dv,
+    dkv,
     dkvc,
     gm,
     gmc,
-    g_up,
-    g_down,
-    g_out,
+    slab,
     g_vec,
     w_out_t,
     w_up_t,
@@ -239,7 +290,6 @@
     inv_sum,
     qz,
     qn,
-    dz,
     dn,
     delta,
     att,
@@ -247,10 +297,14 @@
     x_t,
     dq_t,
     up_acc,
+    g_down,
+    g_out,
+    qkv_acc,
     up_bias_acc,
     gain_acc,
     bias_acc,
     down_bias_acc,
+    packed_sum,
 ):
     cell = pl.program_id(0)
     cells = pl.num_programs(0)
@@ -261,8 +315,16 @@
     stack = HEADS * classes
     factor = head**-0.5
     count = counts[cell]
-    blocks = (count + (KB - 1)) // KB
-    total_blocks = kr.shape[1] // KB
+    own_count = jnp.clip(count - place[0] * genes, 0, genes)
+    other_count = jnp.clip(count - (1 - place[0]) * genes, 0, genes)
+    own_blocks = (own_count + (KB - 1)) // KB
+    other_blocks = (other_count + (KB - 1)) // KB
+    half_blocks = genes // KB
+    blocks = own_blocks + other_blocks
+
+    def nth_block(index):
+        block = jnp.where(index < own_blocks, index, index - own_blocks + half_blocks)
+        return pl.multiple_of(block * KB, KB)
 
     @pl.when(cell == 0)
     def _():
@@ -280,6 +342,8 @@
         down_bias_acc[...] = jnp.zeros_like(down_bias_acc)
         g_down[...] = jnp.zeros_like(g_down)
         g_out[...] = jnp.zeros_like(g_out)
+        qkv_acc[...] = jnp.zeros_like(qkv_acc)
+        packed_sum[...] = jnp.zeros_like(packed_sum)
 
     head_mask = lax.broadcasted_iota(jnp.int32, (stack, width), 1) // head == (
         lax.broadcasted_iota(jnp.int32, (stack, width), 0) // classes
@@ -308,10 +372,11 @@
 
     half_rows = lax.broadcasted_iota(jnp.int32, (2 * head, genes), 0) // head
     half_lanes = lax.broadcasted_iota(jnp.int32, (genes, 2 * head), 1) // head
+    query_r = qt[0].T
     for h in range(HEADS):
         pair = slice((h // 2) * 2 * head, (h // 2 + 1) * 2 * head)
         qz[h] = jnp.where(half_rows == h % 2, qt[0, pair, :].astype(F32), 0.0).astype(BF16)
-        qn[h] = jnp.where(half_lanes == h % 2, qr[0, :, pair].astype(F32), 0.0).astype(BF16)
+        qn[h] = jnp.where(half_lanes == h % 2, query_r[:, pair].astype(F32), 0.0).astype(BF16)
 
     size_k = jnp.max(jnp.maximum(stat[0, 0, :HEADS], stat[0, 1, :HEADS]))
     size_q = jnp.max(jnp.maximum(stat[0, 0, HEADS:], stat[0, 1, HEADS:]))
@@ -320,7 +385,8 @@
     safe = size_k * size_q < SAFE * SAFE
 
     def key_mask(start, shape, axis):
-        return start + lax.broadcasted_iota(jnp.int32, shape, axis) < count
+        limit = jnp.where(start < genes, own_count, genes + other_count)
+        return start + lax.broadcasted_iota(jnp.int32, shape, axis) < limit
 
     shift[...] = jnp.zeros_like(shift)
     shift_q[...] = jnp.zeros_like(shift_q)
@@ -335,7 +401,7 @@
 
         @pl.loop(0, blocks)
         def _(block):
-            start = pl.multiple_of(block * KB, KB)
+            start = nth_block(block)
             for h in range(HEADS):
                 scores = dot(
                     kr[0, pl.ds(start, KB), (h // 2) * 2 * head : (h // 2 + 1) * 2 * head], qz[h]
@@ -373,7 +439,7 @@
 
     def forward_block(block, carried, shifted):
         class_total, class_sum = carried
-        start = pl.multiple_of(block * KB, KB)
+        start = nth_block(block)
         keys = pl.ds(start, KB)
         scores = [
             dot(kr[0, keys, (h // 2) * 2 * head : (h // 2 + 1) * 2 * head], qz[h])
@@ -420,8 +486,8 @@
     def pad_rows(rows):
         return jnp.concatenate([rows, jnp.zeros((128 - rows.shape[0], width), F32)], 0)
 
-    x_t[:, :genes] = x[0].T.astype(F32)
-    x_t[:, genes:] = pad_rows(xc[0].astype(F32)).T
+    x_t[:, :genes] = x[0].T
+    x_t[:, genes:] = pad_rows(xc[0].astype(F32)).T.astype(BF16)
     att[:, genes:] = pad_rows(class_att).T.astype(BF16)
 
     def feed(start, columns, with_class):
@@ -446,7 +512,7 @@
             weigh = lambda values: values
             weigh_rows = lambda rows: rows
         att_low = att[:, span]
-        middle = x_t[:, span] + dot(w_out_t[...], att_low)
+        middle = x_t[:, span].astype(F32) + dot(w_out_t[...], att_low)
         grad_act = dot(w_down[...], cot_t)
         unit, inverse = norm_columns(middle)
         low = (unit * wide_gain + wide_bias).astype(BF16)
@@ -498,7 +564,7 @@
         delta[h] = jnp.sum(grad.astype(F32) * (mix[h, :head, :] * inverse), 0, keepdims=True)
         datt[own, :genes] = grad
         blank = jnp.zeros_like(grad)
-        dz[h] = jnp.concatenate([grad, blank] if h % 2 == 0 else [blank, grad], 0)
+        qz[h] = jnp.concatenate([grad, blank] if h % 2 == 0 else [blank, grad], 0)
     grad_r = datt[:, :genes].T
     for h in range(HEADS):
         pair = slice((h // 2) * 2 * head, (h // 2 + 1) * 2 * head)
@@ -520,7 +586,7 @@
     class_probs = probs_ck[...]
     class_dscore = (class_probs.astype(F32) * (class_dprob - delta_rows)).astype(BF16)
     dq_t[...] = dot(key_c_t, class_dscore)
-    class_dkey = dot(class_dscore, qr[0])
+    class_dkey = dot_nt(class_dscore, qt[0])
     class_dvalue = dot(class_probs, grad_r)
     own_dprob = dot(class_grad_b, value_c_t)
     own_dscore = (own_exp.astype(F32) * (own_dprob - class_delta)).astype(BF16)
@@ -529,11 +595,11 @@
     class_dvalue = class_dvalue + dot(own_exp.astype(F32).T.astype(BF16), class_grad_h)
 
     def backward_block(block, class_dquery):
-        start = pl.multiple_of(block * KB, KB)
+        start = nth_block(block)
         keys = pl.ds(start, KB)
         class_weights = probs_cq[:, keys]
         class_dprob = dot_nt(class_grad_b, vr[0, keys, :])
-        dprobs = [dot(vr[0, keys, : 2 * head], dz[0])]
+        dprobs = [dot(vr[0, keys, : 2 * head], qz[0])]
         class_dscore = (class_weights.astype(F32) * (class_dprob - class_delta)).astype(BF16)
         dkey = dot_tn(class_dscore, query_ch)
         dvalue = dot_tn(class_weights, class_grad_h)
@@ -543,7 +609,7 @@
             if h + 1 < HEADS:
                 g = h + 1
                 dprobs.append(
-                    dot(vr[0, keys, (g // 2) * 2 * head : (g // 2 + 1) * 2 * head], dz[g])
+                    dot(vr[0, keys, (g // 2) * 2 * head : (g // 2 + 1) * 2 * head], qz[g])
                 )
             weights = probs[h, keys, :]
             dscore = weights * (dprobs[h] - delta[h]).astype(BF16)
@@ -551,62 +617,98 @@
             dq_t[own, :] += dot(kt[0, own, keys], dscore)
             dkeys[h // 2] = dkeys[h // 2] + dot(dscore, qn[h])
             dvalues[h // 2] = dvalues[h // 2] + dot(weights, dn[h])
-        valid = key_mask(start, (KB, width), 0)
-        dk[0, keys, :] = jnp.where(valid, jnp.concatenate(dkeys, 1), 0.0).astype(BF16)
-        dv[0, keys, :] = jnp.where(valid, jnp.concatenate(dvalues, 1), 0.0).astype(BF16)
+        valid = key_mask(start, (KB, 2 * width), 0)
+        grads = jnp.where(valid, jnp.concatenate(dkeys + dvalues, 1), 0.0)
+        packed_sum[:, width:] += jnp.sum(grads, 0, keepdims=True)
+        grads = grads.astype(BF16)
+        dkv[0, keys, :] = grads
+        qkv_acc[:, width:] += dot(ut[0, :, keys], grads)
         return class_dquery + dot(class_dscore, kr[0, keys, :])
 
     class_dquery = lax.fori_loop(0, blocks, backward_block, class_dquery)
 
-    @pl.loop(blocks, total_blocks)
-    def _(block):
-        keys = pl.ds(pl.multiple_of(block * KB, KB), KB)
-        dk[0, keys, :] = jnp.zeros((KB, width), BF16)
-        dv[0, keys, :] = jnp.zeros((KB, width), BF16)
-
-    dq[0] = (dq_t[...] * factor).astype(BF16).T
-    dqc[0] = from_heads(class_dquery) * factor
-    dkvc[0] = jnp.concatenate([from_heads(class_dkey), from_heads(class_dvalue)], 1)
+    def blank_rows(block):
+        dkv[0, pl.ds(pl.multiple_of(block * KB, KB), KB), :] = jnp.zeros((KB, 2 * width), BF16)
+
+    pl.loop(own_blocks, half_blocks)(blank_rows)
+    pl.loop(half_blocks + other_blocks, 2 * half_blocks)(blank_rows)
+
+    dquery = dq_t[...] * factor
+    dquery_r = dquery.astype(BF16).T
+    dq[0] = dquery_r
+    qkv_acc[:, :width] += dot(ut[0, :, :genes], dquery_r)
+    class_dquery = from_heads(class_dquery) * factor
+    class_dkv = jnp.concatenate([from_heads(class_dkey), from_heads(class_dvalue)], 1)
+    dqc[0] = class_dquery
+    dkvc[0] = class_dkv
+    class_packed = jnp.concatenate([class_dquery * 0.5, class_dkv], 1)
+    class_unit, _ = norm_rows(xc[0].astype(F32))
+    pad = jnp.zeros((128 - classes, width), F32)
+    class_unit_t = jnp.concatenate([class_unit, pad], 0).T.astype(BF16)
+    class_packed_p = jnp.concatenate([class_packed] + [jnp.zeros((128 - classes, 3 * width), F32)], 0)
+    qkv_acc[...] += dot(class_unit_t, class_packed_p.astype(BF16))
+    packed_sum[:, :width] += jnp.sum(dquery_r.astype(F32), 0, keepdims=True)
+    packed_sum[...] += jnp.sum(class_packed, 0, keepdims=True)
 
     @pl.when(cell == cells - 1)
     def _():
-        g_up[...] = up_acc[...].T
+        first = 0
+
+        def put(values):
+            nonlocal first
+            rows = values.shape[0]
+            for start in range(0, values.shape[1], 128):
+                slab[first : first + rows, :] = values[:, start : start + 128].astype(BF16)
+                first += rows
+
+        put(up_acc[...].T)
+        put(g_down[...])
+        put(g_out[...])
+        put(qkv_acc[...])
         g_vec[...] = jnp.zeros_like(g_vec)
-        g_vec[0:1, :] = jnp.sum(up_bias_acc[...].T, 0, keepdims=True)
-        g_vec[1:2, :width] = jnp.sum(gain_acc[...].T, 0, keepdims=True)
-        g_vec[1:2, width : 2 * width] = jnp.sum(bias_acc[...].T, 0, keepdims=True)
-        g_vec[1:2, 2 * width : 3 * width] = down_bias_acc[...]
+        line = 0
+        for vector in (
+            jnp.sum(up_bias_acc[...].T, 0, keepdims=True),
+            jnp.sum(gain_acc[...].T, 0, keepdims=True),
+            jnp.sum(bias_acc[...].T, 0, keepdims=True),
+            down_bias_acc[...],
+            packed_sum[...],
+        ):
+            for start in range(0, vector.shape[1], 128):
+                g_vec[line : line + 1, :] = vector[:, start : start + 128]
+                line += 1
 
 
 def layer(
-    counts, tables, x, xc, cot, cotc, w_out, gain, bias, w_up, b_up, w_down, b_down
+    counts, place, tables, x, xc, cot, cotc, w_out, gain, bias, w_up, b_up, w_down, b_down
 ):
     cells, genes, width = x.shape
     classes = xc.shape[1]
-    total = tables[2].shape[1]
+    total = tables[1].shape[1]
     head = width // HEADS
     ff = w_up.shape[1]
     stack = HEADS * classes
+    slab_rows = (2 * ff + 4 * width) * width // 128
     whole = lambda shape: pl.BlockSpec(
         shape, lambda c, *_: (0,) * len(shape), pipeline_mode=pl.Buffered(1)
     )
     per_cell = lambda *shape: pl.BlockSpec((1,) + shape, lambda c, *_: (c,) + (0,) * len(shape))
-    kept = lambda *shape: pl.BlockSpec(shape, lambda c, *_: (0,) * len(shape))
+    kept = lambda *shape: whole(shape)
     out = lambda shape, kind=BF16: jax.ShapeDtypeStruct(shape, kind)
     vmem = lambda *shape, kind=BF16: pltpu.VMEM(shape, kind)
     f32 = functools.partial(vmem, kind=F32)
     return pl.pallas_call(
         layer_kernel,
         grid_spec=pltpu.PrefetchScalarGridSpec(
-            num_scalar_prefetch=1,
+            num_scalar_prefetch=2,
             grid=(cells,),
             in_specs=[
                 per_cell(width, genes),
-                per_cell(genes, width),
                 per_cell(total, width),
                 per_cell(total, width),
                 per_cell(width, total),
                 per_cell(HEADS, head + 16, total),
+                per_cell(width, total),
                 per_cell(2, 8, 128),
                 per_cell(classes, 3 * width),
                 per_cell(genes, width),
@@ -626,15 +728,12 @@
                 per_cell(classes, width),
                 per_cell(genes, width),
                 per_cell(classes, width),
-                per_cell(total, width),
-                per_cell(total, width),
+                per_cell(total, 2 * width),
                 per_cell(classes, 2 * width),
                 per_cell(genes, width),
                 per_cell(classes, width),
-                kept(width, ff),
-                kept(ff, width),
-                kept(width, width),
-                kept(8, ff),
+                kept(slab_rows, 128),
+                kept(VECTOR_ROWS, 128),
             ],
             scratch_shapes=[
                 vmem(width, width),
@@ -653,18 +752,21 @@
                 f32(HEADS, 1, genes),
                 vmem(HEADS, 2 * head, genes),
                 vmem(HEADS, genes, 2 * head),
-                vmem(HEADS, 2 * head, genes),
                 vmem(HEADS, genes, 2 * head),
                 f32(HEADS, 1, genes),
                 vmem(width, genes + 128),
                 vmem(width, genes + 128),
-                f32(width, genes + 128),
+                vmem(width, genes + 128),
                 f32(width, genes),
                 f32(ff, width),
+                f32(ff, width),
+                f32(width, width),
+                f32(width, 3 * width),
                 f32(ff, 128),
                 f32(width, 128),
                 f32(width, 128),
                 f32(1, width),
+                f32(1, 3 * width),
             ],
         ),
         out_shape=[
@@ -672,106 +774,344 @@
             out((cells, classes, width)),
             out((cells, genes, width)),
             out((cells, classes, width), F32),
-            out((cells, total, width)),
-            out((cells, total, width)),
+            out((cells, total, 2 * width)),
             out((cells, classes, 2 * width), F32),
             out((cells, genes, width)),
             out((cells, classes, width), F32),
-            out((width, ff), F32),
-            out((ff, width), F32),
-            out((width, width), F32),
-            out((8, ff), F32),
+            out((slab_rows, 128)),
+            out((VECTOR_ROWS, 128), F32),
         ],
         compiler_params=pltpu.CompilerParams(vmem_limit_bytes=VMEM),
         name="layer",
-    )(counts, *tables, x, xc, cot, cotc, w_out, gain, bias, w_up, b_up, w_down, b_down)
-
-
-def tokens_kernel(
-    x, xc, gm, gmc, dq, dqc, dk, dv, dkvc, gain, bias, w, g_x, g_xc, g_qkv, g_vec, w_t
+    )(counts, place, *tables, x, xc, cot, cotc, w_out, gain, bias, w_up, b_up, w_down, b_down)
+
+
+def finish_kernel(
+    orders,
+    slab,
+    vec,
+    x,
+    gm,
+    dq,
+    dkv,
+    dkv_hbm,
+    xc,
+    gmc,
+    dqc,
+    dkvc,
+    gain,
+    bias,
+    w,
+    g_x,
+    g_xc,
+    slab_out,
+    vec_out,
+    w_t,
+    work,
+    summed,
+    inbox,
+    vec_in,
+    other,
+    other_c,
+    send_sems,
+    recv_sems,
+    vec_send,
+    vec_recv,
+    swap_send,
+    swap_recv,
+    class_send,
+    class_recv,
 ):
-    cell = pl.program_id(0)
-    genes, width = x.shape[1:]
+    step, steps = pl.program_id(0), pl.num_programs(0)
+    cells = dkv_hbm.shape[0]
+    genes = dkv_hbm.shape[1] // 2
+    rows, width = x.shape[1:]
     classes = xc.shape[1]
-
-    @pl.when(cell == 0)
+    per_cell = genes // rows
+    me, place = lax.axis_index("cell"), lax.axis_index("gene")
+    bits = len(orders[0])
+    part = slab.shape[0] // STREAMS
+    half = part // 2
+    mate = {"cell": me, "gene": 1 - place}
+
+    def peer(bit):
+        return {"cell": flip(me, 1 << bit), "gene": place}
+
+    def remote(source, target, send, receive, device):
+        return pltpu.make_async_remote_copy(
+            src_ref=source,
+            dst_ref=target,
+            send_sem=send,
+            recv_sem=receive,
+            device_id=device,
+            device_id_type=MESH,
+        )
+
+    def swap(cell):
+        return remote(
+            dkv_hbm.at[cell, pl.ds(genes, genes), :],
+            other.at[cell],
+            swap_send.at[cell],
+            swap_recv.at[cell],
+            mate,
+        )
+
+    def swap_class():
+        return remote(dkvc, other_c, class_send, class_recv, mate)
+
+    def low(stream, level):
+        start, size = 0, half
+        for i in range(level - 1):
+            size = size // 2
+            start = start + ((me // (1 << orders[stream][i])) % 2) * size
+        return pl.multiple_of(start, 16) if level > 1 else start
+
+    def length(level):
+        return part >> level
+
+    def box(level):
+        return half - (half >> (level - 1)) + half if level else 0
+
+    def gather(stream, level):
+        sems = send_sems.at[stream, level], recv_sems.at[stream, level]
+        if level == 0:
+            source = slab.at[pl.ds(pl.multiple_of(stream * part + (1 - place) * half, 16), half), :]
+            return remote(source, inbox.at[stream, pl.ds(0, half), :], *sems, mate)
+        size = length(level + 1)
+        bit = orders[stream][level - 1]
+        away = 1 - (me // (1 << bit)) % 2
+        start = pl.multiple_of(low(stream, level) + away * size, 16)
+        return remote(
+            work.at[stream, pl.ds(start, size), :],
+            inbox.at[stream, pl.ds(box(level), size), :],
+            *sems,
+            peer(bit),
+        )
+
+    def add(stream, level):
+        size = length(level + 1)
+        if level == 0:
+            mine = slab[pl.ds(pl.multiple_of(stream * part + place * half, 16), half), :]
+            start = 0
+        else:
+            start = low(stream, level + 1)
+            mine = work[stream, pl.ds(start, size), :]
+        total = mine.astype(F32) + inbox[stream, pl.ds(box(level), size), :].astype(F32)
+        total = total.astype(BF16)
+        if level == bits:
+            summed[pl.ds(pl.multiple_of(stream * part + place * half + start, 16), size), :] = total
+        else:
+            work[stream, pl.ds(start, size), :] = total
+
+    def spread(stream, level):
+        sems = send_sems.at[stream, 2 * bits + 1 - level], recv_sems.at[stream, 2 * bits + 1 - level]
+        size = length(level + 1)
+        start = low(stream, level + 1) if level else 0
+        span = pl.ds(pl.multiple_of(stream * part + place * half + start, 16), size)
+        device = peer(orders[stream][level - 1]) if level else mate
+        return remote(summed.at[span, :], summed.at[span, :], *sems, device)
+
+    def vector(level):
+        device = peer(orders[0][level - 1]) if level else mate
+        return remote(
+            vec if level == 0 else vec_out,
+            vec_in.at[level],
+            vec_send.at[level],
+            vec_recv.at[level],
+            device,
+        )
+
+    def stage(index):
+        if index > 0:
+            if index - 1 <= bits:
+                for stream in range(STREAMS):
+                    gather(stream, index - 1).wait()
+                    add(stream, index - 1)
+                vector(index - 1).wait()
+                before = vec[...] if index == 1 else vec_out[...]
+                vec_out[...] = before + vec_in[index - 1]
+            else:
+                for stream in range(STREAMS):
+                    spread(stream, 2 * bits + 2 - index).wait()
+        if index <= bits:
+            for stream in range(STREAMS):
+                gather(stream, index).start()
+            vector(index).start()
+        elif index < 2 * bits + 2:
+            for stream in range(STREAMS):
+                spread(stream, 2 * bits + 1 - index).start()
+
+    def rows_back(values, grads, packed):
+        unit, inverse = norm_rows(values)
+        scaled = dot(packed, w_t[...]) * gain[...]
+        return grads + inverse * (
+            scaled
+            - jnp.mean(scaled, -1, keepdims=True)
+            - unit * jnp.mean(scaled * unit, -1, keepdims=True)
+        )
+
+    stages = 2 * bits + 3
+    last = cells * per_cell - 1
+    for index in range(min(stages, last + 1)):
+
+        @pl.when(step == index)
+        def _(index=index):
+            if index == 0:
+                greet([mate] + [peer(bit) for bit in range(bits)])
+            stage(index)
+            if index == 0:
+                for cell in range(cells):
+                    swap(cell).start()
+                swap_class().start()
+                w_t[...] = w[...].T
+
+    cell = step // per_cell
+
+    @pl.when(step % per_cell == 0)
     def _():
-        w_t[...] = w[...].T
-        g_qkv[...] = jnp.zeros_like(g_qkv)
-        g_vec[...] = jnp.zeros_like(g_vec)
-
-    blank = jnp.zeros((16 - classes, width), F32)
-
-    def joined(genes_part, class_part):
-        return jnp.concatenate([genes_part.astype(F32), class_part.astype(F32), blank], 0)
-
-    unit, inverse = norm_rows(joined(x[0], xc[0]))
-    low = (unit * gain[...] + bias[...]).astype(BF16)
-    rows = genes + 16
-    spot = lax.broadcasted_iota(jnp.int32, (rows, 1), 0)
-    share = jnp.where(spot < genes, 1.0, jnp.where(spot < genes + classes, 0.5, 0.0))
-    class_grads = [dqc[0], dkvc[0][:, :width], dkvc[0][:, width:]]
-    packed = jnp.concatenate(
-        [
-            jnp.concatenate([part, jnp.concatenate([class_part, blank], 0).astype(BF16)], 0)
-            for part, class_part in zip((dq[0], dk[0], dv[0]), class_grads)
-        ],
-        1,
-    )
-    back = dot(packed, w_t[...])
-    g_qkv[...] += dot_tn((low.astype(F32) * share).astype(BF16), packed)
-    weighed = back * share
-    g_vec[0:1, :] += jnp.sum(weighed * unit, 0, keepdims=True)
-    g_vec[1:2, :] += jnp.sum(weighed, 0, keepdims=True)
-    scaled = back * gain[...]
-    result = joined(gm[0], gmc[0]) + inverse * (
-        scaled
-        - jnp.mean(scaled, -1, keepdims=True)
-        - unit * jnp.mean(scaled * unit, -1, keepdims=True)
-    )
-    g_x[0] = result[:genes].astype(BF16)
-    g_xc[0] = result[genes : genes + classes].astype(BF16)
-
-
-def tokens(x, xc, gm, gmc, dq, dqc, dk, dv, dkvc, gain, bias, w):
+        swap(cell).wait()
+
+    grads = dkv[0].astype(F32) + other[
+        cell, pl.ds(pl.multiple_of((step % per_cell) * rows, 16), rows), :
+    ].astype(F32)
+    packed = jnp.concatenate([dq[0], grads.astype(BF16)], 1)
+    g_x[0] = rows_back(x[0].astype(F32), gm[0].astype(F32), packed).astype(BF16)
+
+    @pl.when(step == steps - 1)
+    def _():
+        swap_class().wait()
+        class_grads = dkvc[...] + other_c[...]
+        stack = cells * classes
+        packed = jnp.concatenate([dqc[...], class_grads], 2).reshape(stack, 3 * width)
+        values = xc[...].astype(F32).reshape(stack, width)
+        result = rows_back(values, gmc[...].reshape(stack, width), packed.astype(BF16))
+        g_xc[...] = result.reshape(cells, classes, width).astype(BF16)
+        for index in range(last + 1, stages):
+            stage(index)
+        slab_out[...] = summed[...]
+
+
+def finish(orders, slab, vec, x, xc, gm, gmc, dq, dqc, dkv, dkvc, gain, bias, w):
     cells, genes, width = x.shape
     classes = xc.shape[1]
-    whole = lambda shape: pl.BlockSpec(shape, lambda c: (0,) * len(shape))
-    per_cell = lambda *shape: pl.BlockSpec((1,) + shape, lambda c: (c,) + (0,) * len(shape))
+    rows = genes // 2
+    per_cell = genes // rows
+    bits = len(orders[0])
+    part = slab.shape[0] // STREAMS
+    whole = lambda array: pl.BlockSpec(array.shape, lambda i: (0,) * array.ndim)
+    piece = lambda lanes: pl.BlockSpec((1, rows, lanes), lambda i: (i // per_cell, i % per_cell, 0))
     out = lambda shape, kind=BF16: jax.ShapeDtypeStruct(shape, kind)
+    dma = lambda *shape: pltpu.SemaphoreType.DMA(shape)
+    outs = [
+        out((cells, genes, width)),
+        out((cells, classes, width)),
+        out(slab.shape),
+        out(vec.shape, F32),
+    ]
     return pl.pallas_call(
-        tokens_kernel,
-        grid=(cells,),
+        functools.partial(finish_kernel, orders),
+        grid=(cells * per_cell,),
         in_specs=[
-            per_cell(genes, width),
-            per_cell(classes, width),
-            per_cell(genes, width),
-            per_cell(classes, width),
-            per_cell(genes, width),
-            per_cell(classes, width),
-            per_cell(genes, width),
-            per_cell(genes, width),
-            per_cell(classes, 2 * width),
-            whole((1, width)),
-            whole((1, width)),
-            whole((width, 3 * width)),
+            whole(slab),
+            whole(vec),
+            piece(width),
+            piece(width),
+            piece(width),
+            piece(2 * width),
+            pl.BlockSpec(memory_space=pl.ANY),
+            whole(xc),
+            whole(gmc),
+            whole(dqc),
+            whole(dkvc),
+            whole(gain),
+            whole(bias),
+            whole(w),
         ],
-        out_specs=[
-            per_cell(genes, width),
-            per_cell(classes, width),
-            whole((width, 3 * width)),
-            whole((8, width)),
+        out_specs=[piece(width)] + [whole(o) for o in outs[1:]],
+        out_shape=outs,
+        scratch_shapes=[
+            pltpu.VMEM((3 * width, width), BF16),
+            pltpu.VMEM((STREAMS, part // 2, 128), BF16),
+            pltpu.VMEM(slab.shape, BF16),
+            pltpu.VMEM((STREAMS, part, 128), BF16),
+            pltpu.VMEM((bits + 1,) + vec.shape, F32),
+            pltpu.VMEM((cells, genes, 2 * width), BF16),
+            pltpu.VMEM(dkvc.shape, F32),
+            dma(STREAMS, 2 * bits + 2),
+            dma(STREAMS, 2 * bits + 2),
+            dma(bits + 1),
+            dma(bits + 1),
+            dma(cells),
+            dma(cells),
+            dma(),
+            dma(),
         ],
+        compiler_params=pltpu.CompilerParams(
+            vmem_limit_bytes=VMEM, collective_id=1, has_side_effects=True
+        ),
+        name="finish",
+    )(slab, vec, x, gm, dq, dkv, dkv, xc, gmc, dqc, dkvc, gain, bias, w)
+
+
+def unpack_kernel(slab, vec, gain, bias, w, g_up, g_down, g_out, g_qkv, *vectors):
+    width, ff = g_up.shape
+    first = 0
+
+    def take(target):
+        nonlocal first
+        rows = target.shape[0]
+        for start in range(0, target.shape[1], 128):
+            target[:, start : start + 128] = slab[first : first + rows, :].astype(F32)
+            first += rows
+
+    take(g_up)
+    take(g_down)
+    take(g_out)
+    take(g_qkv)
+    line = 0
+
+    def lines(count):
+        nonlocal line
+        line += count
+        return jnp.concatenate([vec[i : i + 1, :] for i in range(line - count, line)], 1)
+
+    up_bias, ln2_gain, ln2_bias, down_bias, ln1_gain, ln1_bias = vectors
+    up_bias[...] = lines(ff // 128)
+    ln2_gain[...] = lines(width // 128)
+    ln2_bias[...] = lines(width // 128)
+    down_bias[...] = lines(width // 128)
+    packed_sum = lines(3 * width // 128)
+    weights = w[...].astype(F32)
+    sums = g_qkv[...]
+    ln1_gain[...] = jnp.sum((weights * sums).T, 0, keepdims=True)
+    ln1_bias[...] = jnp.sum((weights * packed_sum).T, 0, keepdims=True)
+    g_qkv[...] = (
+        widen(spread_column(gain[...]), 3 * width) * sums
+        + widen(spread_column(bias[...]), 3 * width) * packed_sum
+    )
+
+
+def unpack(slab, vec, gain, bias, w, ff):
+    width = w.shape[0]
+    out = lambda *shape: jax.ShapeDtypeStruct(shape, F32)
+    row = out(1, width)
+    return pl.pallas_call(
+        unpack_kernel,
         out_shape=[
-            out((cells, genes, width)),
-            out((cells, classes, width)),
-            out((width, 3 * width), F32),
-            out((8, width), F32),
+            out(width, ff),
+            out(ff, width),
+            out(width, width),
+            out(width, 3 * width),
+            out(1, ff),
+            row,
+            row,
+            row,
+            row,
+            row,
         ],
-        scratch_shapes=[pltpu.VMEM((3 * width, width), BF16)],
         compiler_params=pltpu.CompilerParams(vmem_limit_bytes=VMEM),
-        name="tokens",
-    )(x, xc, gm, gmc, dq, dqc, dk, dv, dkvc, gain, bias, w)
+        name="unpack",
+    )(slab, vec, gain, bias, w)
 
 
 def shards(
@@ -791,15 +1131,16 @@
     gene_cot,
     class_cot,
 ):
-    width = gene_in.shape[-1]
     row = lambda vector: vector.reshape(1, -1)
     place = lax.axis_index("gene").reshape(1)
-    everything = lax.all_gather(gene_in, "gene", axis=1, tiled=True)
-    tables = project(
-        expressed, place, everything, class_in, row(ln1_gain), row(ln1_bias), w_qkv
-    )
-    gene_out, class_out, dq, dqc, dk, dv, dkvc, gm, gmc, g_up, g_down, g_out, g_vec = layer(
+    bits = (lax.axis_size("cell") - 1).bit_length()
+    near = list(range(bits - 1))
+    orders = [near[i % len(near) :] + near[: i % len(near)] + [bits - 1] for i in range(STREAMS)]
+    gain1, bias1 = row(ln1_gain), row(ln1_bias)
+    tables = project(expressed, gene_in, class_in, gain1, bias1, w_qkv)
+    gene_out, class_out, dq, dqc, dkv, dkvc, gm, gmc, slab, vec = layer(
         expressed,
+        place,
         tables,
         gene_in,
         class_in,
@@ -813,41 +1154,27 @@
         w_down,
         row(b_down),
     )
-    dk = lax.psum_scatter(dk, "gene", scatter_dimension=1, tiled=True)
-    dv = lax.psum_scatter(dv, "gene", scatter_dimension=1, tiled=True)
-    dkvc = lax.psum(dkvc, "gene")
-    gene_grad, class_grad, g_qkv, g_vec1 = tokens(
-        gene_in,
-        class_in,
-        gm,
-        gmc,
-        dq,
-        dqc,
-        dk,
-        dv,
-        dkvc,
-        row(ln1_gain),
-        row(ln1_bias),
-        w_qkv,
-    )
-    g_up, g_down, g_out, g_vec, g_qkv, g_vec1 = lax.psum(
-        (g_up, g_down, g_out, g_vec, g_qkv, g_vec1), ("cell", "gene")
+    gene_grad, class_grad, slab, vec = finish(
+        orders, slab, vec, gene_in, class_in, gm, gmc, dq, dqc, dkv, dkvc, gain1, bias1, w_qkv
+    )
+    g_up, g_down, g_out, g_qkv, g_b_up, g_gain2, g_bias2, g_b_down, g_gain1, g_bias1 = unpack(
+        slab, vec, gain1, bias1, w_qkv, w_up.shape[1]
     )
     return (
         gene_out,
         class_out,
         gene_grad,
         class_grad,
-        g_vec1[0],
-        g_vec1[1],
+        g_gain1[0],
+        g_bias1[0],
         g_qkv,
         g_out,
-        g_vec[1, :width],
-        g_vec[1, width : 2 * width],
+        g_gain2[0],
+        g_bias2[0],
         g_up,
-        g_vec[0],
+        g_b_up[0],
         g_down,
-        g_vec[1, 2 * width : 3 * width],
+        g_b_down[0],
     )
 
 

time: 388 us -> 214 us (0.55)
  waiting for transfers between devices: 191 us -> 0 us
  Pallas kernels: 128 us -> 205 us
  blocking collectives: 39.6 us -> 0 us
  between operations: 13.8 us -> 0.68 us
  local copies, waits for them, and re-layouts: 7.72 us -> 3.66 us
    psum x2 -> x0, waiting for transfers between devices: 140 us -> none  [the longest x1 96.6 us: shards(): lax.psum((g_up, g_down, g_out, g_vec, g_qkv, g_vec1), ('cell', 'gene'))]
    pallas_call x2 -> x3, Pallas kernels: 26.2 us -> 88.7 us  [the longest x1 69 us: finish(): pl.pallas_call(functools.partial(finish_kernel, orders), grid=(cells * pe...]
    psum x1 -> x0, blocking collectives: 39.6 us -> none  [shards(): lax.psum((g_up, g_down, g_out, g_vec, g_qkv, g_vec1), ('cell', 'gene'))]
    reduce_scatter x2 -> x0, waiting for transfers between devices: 31.2 us -> none  [the longest x1 15.6 us: shards(): dv = lax.psum_scatter(dv, 'gene', scatter_dimension=1, tiled=True)]
    all_gather x1 -> x0, waiting for transfers between devices: 17.3 us -> none  [shards(): everything = lax.all_gather(gene_in, 'gene', axis=1, tiled=True)]
    pallas_call x1, Pallas kernels: 102 us -> 116 us  [layer(): pl.pallas_call(layer_kernel, grid_spec=pltpu.PrefetchScalarGridSpec(num_s...]
  transfers between devices with their start and end apart: 5 -> 0, of which waited for: 5 -> 0; matrix products, arithmetic and copies ran while one was open for 0% -> 0% of each run, Pallas kernels for 0% -> 0%
where the time goes in v2:
time: 214 us; the launch traced here: 209 us
  Pallas kernels  205 us (96%)
  local copies, waits for them, and re-layouts  3.66 us (2%)
    pallas_call x1, Pallas kernels, layer(): pl.pallas_call(layer_kernel, grid_spec=pltpu.PrefetchScalarGridSpec(num_s...  116 us
    pallas_call x1, Pallas kernels, finish(): pl.pallas_call(functools.partial(finish_kernel, orders), grid=(cells * pe...  69 us
    pallas_call x1, Pallas kernels, project(): pl.pallas_call(project_kernel, grid=(cells, 2), in_specs=[pl.BlockSpec(me...  15.9 us

profile of v2, /device:TPU:3, one launch (start us, length us, event | category | flops | bytes accessed | tf_op | source)
XLA Modules:
  0.0 209.5 jit_solution(9470403388074676153)
XLA Ops:
  0.6 15.9 %project.1 = (bf16[4,256,1024]{2,1,0:T(8,128)(2,1)}, bf16[4,2048,256]{2,1,0:T(8,128)(2,1)}, bf16[4,2048,256]{2,1,0:T(8,128)(2,1)}, bf16[4,256,2048]{2,1,0:T(8,12...) custom-call(s32[4]{0:T(128)} %counts.3, ...), custom_call_target="tpu_custom_call" | custom-call | tf_op jit(solution)/shard_map/project/pallas_call | solution.py:185
  16.6 116.4 %layer.1 = (bf16[4,1024,256]{2,1,0:T(8,128)(2,1)}, bf16[4,8,256]{2,1,0:T(8,128)(2,1)}, bf16[4,1024,256]{2,1,0:T(8,128)(2,1)}, f32[4,8,256]{2,1,0:T(8,128)}, bf16...) custom-call(s32[4]{0:T(128)} %counts.3, ...), custom_call_target="tpu_custom_call" | custom-call | tf_op jit(solution)/shard_map/layer/pallas_call | solution.py:700
  133.0 69.0 %finish.1 = (bf16[4,1024,256]{2,1,0:T(8,128)(2,1)}, bf16[4,8,256]{2,1,0:T(8,128)(2,1)}, bf16[6144,128]{1,0:T(8,128)(2,1)}, f32[32,128]{1,0:T(8,128)}) custom-call(bf16[6144,128]{1,0:T(8,128)(2,1)} %get-tuple-element.56.slab, f32[32,128]{1,0:T(8,128)} %get-tuple-element.57.vec, bf16[4,1024,256]{2,1,0:T(8,128)(2,1)} %x.5, ...), custom_call_target="tpu_custom_call" | custom-call | tf_op jit(solution)/shard_map/finish/pallas_call | solution.py:1011
  202.0 3.8 %unpack.1 = (f32[256,1024]{1,0:T(8,128)}, f32[1024,256]{1,0:T(8,128)}, f32[256,256]{1,0:T(8,128)}, f32[256,768]{1,0:T(8,128)}, f32[1,1024]{1,0:T(1,128)}, /*inde...) custom-call(bf16[6144,128]{1,0:T(8,128)(2,1)} %get-tuple-element.66.slab, ...), custom_call_target="tpu_custom_call" | custom-call | tf_op jit(solution)/shard_map/unpack/pallas_call | solution.py:1098
  205.8 0.0 copy-start
  205.8 3.0 %copy.31 = bf16[4,1024,256]{2,1,0:T(8,128)(2,1)} copy(bf16[4,1024,256]{2,1,0:T(8,128)(2,1)} %get-tuple-element.94) | data formatting | bytes 4194304
  208.9 0.0 copy-done
  208.9 0.6 copy.32
Async XLA Ops:
  205.8 3.1 %copy-start = (bf16[4,8,256]{2,1,0:T(8,128)(2,1)S(1)}, bf16[4,8,256]{2,1,0:T(8,128)(2,1)}, u32[]{:S(2)}) copy-start(bf16[4,8,256]{2,1,0:T(8,128)(2,1)} %get-tuple-element.95) | copy-start | bytes 49156

commit v3 on v2

--- a/solution.py
+++ b/solution.py
@@ -13,6 +13,7 @@
 SAFE = 40.0
 KB = 256
 STREAMS = 3
+MARKS = 3
 VECTOR_ROWS = 32
 VMEM = 63 * 2**20
 F32 = jnp.float32
@@ -81,8 +82,6 @@
     w,
     qt,
     kr,
-    vr,
-    kt,
     va,
     ut,
     stat,
@@ -137,16 +136,13 @@
         valid = spot < counts[cell]
         kept = jnp.where(valid, low, 0.0).astype(BF16)
         packed_t = dot(w_t[width:, :], kept)
-        packed = dot(kept.T, w[:, width:])
-        kt[0] = packed_t[:width].astype(BF16)
         mark = jnp.where(
-            (lax.broadcasted_iota(jnp.int32, (16, genes), 0) == 0) & valid, 1.0, 0.0
+            (lax.broadcasted_iota(jnp.int32, (16, genes), 0) < MARKS) & valid, 1.0, 0.0
         ).astype(BF16)
         for h in range(HEADS):
             va[0, h, :head, :] = packed_t[width + h * head : width + (h + 1) * head].astype(BF16)
             va[0, h, head:, :] = mark
-        kr[0] = packed[:, :width].astype(BF16)
-        vr[0] = packed[:, width:].astype(BF16)
+        kr[0] = packed_t[:width].astype(BF16).T
         stat[...] = jnp.zeros_like(stat)
         norms(packed_t[:width], 0)
         return low
@@ -197,8 +193,6 @@
         out_specs=[
             per_cell(width, genes),
             rows,
-            rows,
-            columns,
             pl.BlockSpec((1, HEADS, head + 16, genes), lambda c, h: (c, 0, 0, h)),
             columns,
             pl.BlockSpec((1, 1, 8, 128), lambda c, h: (c, h, 0, 0)),
@@ -207,8 +201,6 @@
         out_shape=[
             out((cells, width, genes)),
             out((cells, total, width)),
-            out((cells, total, width)),
-            out((cells, width, total)),
             out((cells, HEADS, head + 16, total)),
             out((cells, width, total)),
             out((cells, 2, 8, 128), F32),
@@ -230,15 +222,8 @@
 
 
 def gelu_parts(u):
-    root = 0.7071067811865476
-    t = pl.reciprocal(1.0 + (0.3275911 * root) * jnp.abs(u), approx=True)
-    bell = jnp.exp2((-0.5 * LOG2E) * (u * u))
-    poly = t * (
-        0.127414796
-        + t * (-0.142248368 + t * (0.7107068705 + t * (-0.7265760135 + t * 0.5307027145)))
-    )
-    tail = poly * bell
-    phi = jnp.where(u >= 0.0, 1.0 - tail, tail)
+    phi = 0.5 + 0.5 * lax.erf(u * 0.7071067811865476)
+    bell = jnp.exp2((u * u) * (-0.5 * LOG2E))
     return u * phi, phi + (u * 0.3989422804014327) * bell
 
 
@@ -247,8 +232,6 @@
     place,
     qt,
     kr,
-    vr,
-    kt,
     va,
     ut,
     stat,
@@ -289,13 +272,12 @@
     shift_q,
     inv_sum,
     qz,
-    qn,
-    dn,
+    da,
     delta,
     att,
     datt,
     x_t,
-    dq_t,
+    dq_acc,
     up_acc,
     g_down,
     g_out,
@@ -305,6 +287,7 @@
     bias_acc,
     down_bias_acc,
     packed_sum,
+    packed_cols,
 ):
     cell = pl.program_id(0)
     cells = pl.num_programs(0)
@@ -344,6 +327,7 @@
         g_out[...] = jnp.zeros_like(g_out)
         qkv_acc[...] = jnp.zeros_like(qkv_acc)
         packed_sum[...] = jnp.zeros_like(packed_sum)
+        packed_cols[...] = jnp.zeros_like(packed_cols)
 
     head_mask = lax.broadcasted_iota(jnp.int32, (stack, width), 1) // head == (
         lax.broadcasted_iota(jnp.int32, (stack, width), 0) // classes
@@ -371,12 +355,9 @@
     query_cb, key_cb, value_cb = query_c.astype(BF16), key_c.astype(BF16), value_c.astype(BF16)
 
     half_rows = lax.broadcasted_iota(jnp.int32, (2 * head, genes), 0) // head
-    half_lanes = lax.broadcasted_iota(jnp.int32, (genes, 2 * head), 1) // head
-    query_r = qt[0].T
     for h in range(HEADS):
         pair = slice((h // 2) * 2 * head, (h // 2 + 1) * 2 * head)
         qz[h] = jnp.where(half_rows == h % 2, qt[0, pair, :].astype(F32), 0.0).astype(BF16)
-        qn[h] = jnp.where(half_lanes == h % 2, query_r[:, pair].astype(F32), 0.0).astype(BF16)
 
     size_k = jnp.max(jnp.maximum(stat[0, 0, :HEADS], stat[0, 1, :HEADS]))
     size_q = jnp.max(jnp.maximum(stat[0, 0, HEADS:], stat[0, 1, HEADS:]))
@@ -408,7 +389,7 @@
                 )
                 scores = jnp.where(key_mask(start, scores.shape, 0), scores, -1e30)
                 shift[h] = jnp.maximum(shift[h], jnp.max(scores, 0, keepdims=True))
-            scores = dot(query_cb, kt[0, :, pl.ds(start, KB)])
+            scores = dot_nt(query_cb, kr[0, pl.ds(start, KB), :])
             scores = jnp.where(key_mask(start, scores.shape, 1), scores, -1e30)
             shift_q[...] = jnp.maximum(shift_q[...], jnp.max(scores, -1, keepdims=True))
 
@@ -434,18 +415,27 @@
     own_exp = jnp.where(
         pair_mask, jnp.exp2(dot(query_cb, key_c_t) * LOG2E - shift_qc), 0.0
     ).astype(BF16)
-    own_mix = dot(own_exp, value_cb)
-    own_sum = jnp.sum(own_exp.astype(F32), -1, keepdims=True)
-
-    def forward_block(block, carried, shifted):
-        class_total, class_sum = carried
+    deep = head + 16
+
+    def spread_heads(rows, extra):
+        pieces = []
+        for h in range(HEADS):
+            pieces += [rows[:, h * head : (h + 1) * head], extra]
+        return jnp.concatenate(pieces, 1)
+
+    own_mix = spread_heads(
+        dot(own_exp, value_cb),
+        jnp.broadcast_to(jnp.sum(own_exp.astype(F32), -1, keepdims=True), (stack, 16)),
+    )
+
+    def forward_block(block, class_total, shifted):
         start = nth_block(block)
         keys = pl.ds(start, KB)
         scores = [
             dot(kr[0, keys, (h // 2) * 2 * head : (h // 2 + 1) * 2 * head], qz[h])
             for h in range(1)
         ]
-        class_scores = dot(query_cb, kt[0, :, keys]) * LOG2E - shift_qc
+        class_scores = dot_nt(query_cb, kr[0, keys, :]) * LOG2E - shift_qc
         for h in range(HEADS):
             if h + 1 < HEADS:
                 g = h + 1
@@ -456,26 +446,29 @@
             if shifted:
                 scaled = jnp.minimum(scaled - shift[h], 60.0)
             exps = jnp.exp2(scaled).astype(BF16)
-            probs[h, keys, :] = exps
             mix[h] += dot(va[0, h, :, keys], exps)
+            probs[h, :, keys] = exps.T
         class_exp = jnp.where(
             key_mask(start, class_scores.shape, 1), jnp.exp2(class_scores), 0.0
         ).astype(BF16)
         probs_cq[:, keys] = class_exp
-        class_total = class_total + dot(class_exp, vr[0, keys, :])
-        class_sum = class_sum + jnp.sum(class_exp.astype(F32), -1, keepdims=True)
-        return class_total, class_sum
-
-    carried = lax.cond(
+        return class_total + dot_nt(class_exp, va[0, :, :, keys].reshape(HEADS * deep, KB))
+
+    class_total = lax.cond(
         safe,
-        lambda: lax.fori_loop(
-            0, blocks, functools.partial(forward_block, shifted=False), (own_mix, own_sum)
-        ),
-        lambda: lax.fori_loop(
-            0, blocks, functools.partial(forward_block, shifted=True), (own_mix, own_sum)
-        ),
-    )
-    class_total, class_sum = carried
+        lambda: lax.fori_loop(0, blocks, functools.partial(forward_block, shifted=False), own_mix),
+        lambda: lax.fori_loop(0, blocks, functools.partial(forward_block, shifted=True), own_mix),
+    )
+    class_sum = jnp.concatenate(
+        [
+            class_total[h * classes : (h + 1) * classes, h * deep + head : h * deep + head + 1]
+            for h in range(HEADS)
+        ],
+        0,
+    )
+    class_total = jnp.concatenate(
+        [class_total[:, h * deep : h * deep + head] for h in range(HEADS)], 1
+    )
     class_inv = 1.0 / class_sum
     class_att = from_heads(class_total * class_inv)
     for h in range(HEADS):
@@ -548,7 +541,7 @@
             yc[0] = result_r[columns : columns + classes].astype(BF16)
             gmc[0] = middle_r[columns:].astype(F32)[:classes]
 
-    feed_step = 256
+    feed_step = 512
     pieces = genes // feed_step
 
     @pl.loop(0, pieces - 1)
@@ -561,14 +554,19 @@
         own = slice(h * head, (h + 1) * head)
         inverse = inv_sum[h]
         grad = (datt[own, :genes].astype(F32) * inverse).astype(BF16)
-        delta[h] = jnp.sum(grad.astype(F32) * (mix[h, :head, :] * inverse), 0, keepdims=True)
+        row_delta = jnp.sum(grad.astype(F32) * (mix[h, :head, :] * inverse), 0, keepdims=True)
+        delta[h] = row_delta
         datt[own, :genes] = grad
-        blank = jnp.zeros_like(grad)
-        qz[h] = jnp.concatenate([grad, blank] if h % 2 == 0 else [blank, grad], 0)
-    grad_r = datt[:, :genes].T
-    for h in range(HEADS):
-        pair = slice((h // 2) * 2 * head, (h // 2 + 1) * 2 * head)
-        dn[h] = jnp.where(half_lanes == h % 2, grad_r[:, pair].astype(F32), 0.0).astype(BF16)
+        parts = jnp.zeros((16, genes), F32)
+        rest = row_delta
+        for i in range(MARKS):
+            piece = rest.astype(BF16).astype(F32)
+            rest = rest - piece
+            parts = jnp.where(
+                lax.broadcasted_iota(jnp.int32, (16, genes), 0) == i, -piece, parts
+            )
+        blank = jnp.zeros((2 * head - deep, genes), BF16)
+        da[h] = jnp.concatenate([grad, parts.astype(BF16), blank], 0).T
 
     class_grad = datt[:, genes:].astype(F32).T[:classes]
     class_grad = by_head(class_grad) * class_inv
@@ -585,42 +583,51 @@
     )
     class_probs = probs_ck[...]
     class_dscore = (class_probs.astype(F32) * (class_dprob - delta_rows)).astype(BF16)
-    dq_t[...] = dot(key_c_t, class_dscore)
+    dq_acc[...] = dot_tn(class_dscore, key_cb)
     class_dkey = dot_nt(class_dscore, qt[0])
-    class_dvalue = dot(class_probs, grad_r)
+    class_dvalue = dot_nt(class_probs, datt[:, :genes])
     own_dprob = dot(class_grad_b, value_c_t)
     own_dscore = (own_exp.astype(F32) * (own_dprob - class_delta)).astype(BF16)
     class_dquery = dot(own_dscore, key_cb)
     class_dkey = class_dkey + dot(own_dscore.astype(F32).T.astype(BF16), query_ch)
     class_dvalue = class_dvalue + dot(own_exp.astype(F32).T.astype(BF16), class_grad_h)
 
+    class_grad_s = spread_heads(class_grad_b, jnp.zeros((stack, 16), BF16))
+    class_grad_ht = class_grad_h.T
+    query_ct = query_ch.T
+    pair_lanes = lax.broadcasted_iota(jnp.int32, (KB, 2 * head), 1) // head
+
     def backward_block(block, class_dquery):
         start = nth_block(block)
         keys = pl.ds(start, KB)
+        dprobs = [dot(da[0, :, :deep], va[0, 0, :, keys])]
         class_weights = probs_cq[:, keys]
-        class_dprob = dot_nt(class_grad_b, vr[0, keys, :])
-        dprobs = [dot(vr[0, keys, : 2 * head], qz[0])]
+        class_dprob = dot(class_grad_s, va[0, :, :, keys].reshape(HEADS * deep, KB))
         class_dscore = (class_weights.astype(F32) * (class_dprob - class_delta)).astype(BF16)
-        dkey = dot_tn(class_dscore, query_ch)
-        dvalue = dot_tn(class_weights, class_grad_h)
-        dkeys = [dkey[:, : 2 * head], dkey[:, 2 * head :]]
-        dvalues = [dvalue[:, : 2 * head], dvalue[:, 2 * head :]]
+        dkeys, dvalues, dscores, zeroed = [], [], [], []
         for h in range(HEADS):
             if h + 1 < HEADS:
-                g = h + 1
-                dprobs.append(
-                    dot(vr[0, keys, (g // 2) * 2 * head : (g // 2 + 1) * 2 * head], qz[g])
+                dprobs.append(dot(da[h + 1, :, :deep], va[0, h + 1, :, keys]))
+            weights = probs[h, :, keys]
+            dscore = weights * dprobs[h].astype(BF16)
+            own = slice(h * head, (h + 1) * head)
+            dvalues.append(dot(datt[own, :genes], weights))
+            dkeys.append(dot(qt[0, own, :], dscore))
+            pair = slice((h // 2) * 2 * head, (h // 2 + 1) * 2 * head)
+            dscores.append(dscore)
+            zeroed.append(
+                jnp.where(pair_lanes == h % 2, kr[0, keys, pair].astype(F32), 0.0).astype(BF16)
+            )
+            if h % 2 == 1:
+                dq_acc[:, pair] += dot(
+                    jnp.concatenate(dscores[h - 1 :], 1), jnp.concatenate(zeroed[h - 1 :], 0)
                 )
-            weights = probs[h, keys, :]
-            dscore = weights * (dprobs[h] - delta[h]).astype(BF16)
-            own = slice(h * head, (h + 1) * head)
-            dq_t[own, :] += dot(kt[0, own, keys], dscore)
-            dkeys[h // 2] = dkeys[h // 2] + dot(dscore, qn[h])
-            dvalues[h // 2] = dvalues[h // 2] + dot(weights, dn[h])
-        valid = key_mask(start, (KB, 2 * width), 0)
-        grads = jnp.where(valid, jnp.concatenate(dkeys + dvalues, 1), 0.0)
-        packed_sum[:, width:] += jnp.sum(grads, 0, keepdims=True)
-        grads = grads.astype(BF16)
+        dkey = jnp.concatenate(dkeys, 0) + dot(query_ct, class_dscore)
+        dvalue = jnp.concatenate(dvalues, 0) + dot(class_grad_ht, class_weights)
+        valid = key_mask(start, (1, KB), 1)
+        grads = jnp.where(valid, jnp.concatenate([dkey, dvalue], 0), 0.0)
+        packed_cols[...] += fold_lanes(grads)
+        grads = grads.astype(BF16).T
         dkv[0, keys, :] = grads
         qkv_acc[:, width:] += dot(ut[0, :, keys], grads)
         return class_dquery + dot(class_dscore, kr[0, keys, :])
@@ -633,8 +640,7 @@
     pl.loop(own_blocks, half_blocks)(blank_rows)
     pl.loop(half_blocks + other_blocks, 2 * half_blocks)(blank_rows)
 
-    dquery = dq_t[...] * factor
-    dquery_r = dquery.astype(BF16).T
+    dquery_r = (dq_acc[...] * factor).astype(BF16)
     dq[0] = dquery_r
     qkv_acc[:, :width] += dot(ut[0, :, :genes], dquery_r)
     class_dquery = from_heads(class_dquery) * factor
@@ -672,7 +678,10 @@
             jnp.sum(gain_acc[...].T, 0, keepdims=True),
             jnp.sum(bias_acc[...].T, 0, keepdims=True),
             down_bias_acc[...],
-            packed_sum[...],
+            packed_sum[...]
+            + jnp.concatenate(
+                [jnp.zeros((1, width), F32), jnp.sum(packed_cols[...].T, 0, keepdims=True)], 1
+            ),
         ):
             for start in range(0, vector.shape[1], 128):
                 g_vec[line : line + 1, :] = vector[:, start : start + 128]
@@ -705,8 +714,6 @@
             in_specs=[
                 per_cell(width, genes),
                 per_cell(total, width),
-                per_cell(total, width),
-                per_cell(width, total),
                 per_cell(HEADS, head + 16, total),
                 per_cell(width, total),
                 per_cell(2, 8, 128),
@@ -743,7 +750,7 @@
                 f32(width, 128),
                 f32(ff, 128),
                 f32(width, 128),
-                vmem(HEADS, total, genes),
+                vmem(HEADS, genes, total),
                 vmem(stack, genes),
                 vmem(stack, total),
                 f32(HEADS, head + 16, genes),
@@ -752,12 +759,11 @@
                 f32(HEADS, 1, genes),
                 vmem(HEADS, 2 * head, genes),
                 vmem(HEADS, genes, 2 * head),
-                vmem(HEADS, genes, 2 * head),
                 f32(HEADS, 1, genes),
                 vmem(width, genes + 128),
                 vmem(width, genes + 128),
                 vmem(width, genes + 128),
-                f32(width, genes),
+                f32(genes, width),
                 f32(ff, width),
                 f32(ff, width),
                 f32(width, width),
@@ -767,6 +773,7 @@
                 f32(width, 128),
                 f32(1, width),
                 f32(1, 3 * width),
+                f32(2 * width, 128),
             ],
         ),
         out_shape=[

time: 214 us -> 193 us (0.902); the launches traced: 209 us -> 194 us
  Pallas kernels: 205 us -> 190 us
    pallas_call x1, Pallas kernels: 116 us -> 89.6 us  [layer(): pl.pallas_call(layer_kernel, grid_spec=pltpu.PrefetchScalarGridSpec(num_s...]
    pallas_call x1, Pallas kernels: 69 us -> 82.9 us  [finish(): pl.pallas_call(functools.partial(finish_kernel, orders), grid=(cells * pe...]
    pallas_call x1, Pallas kernels: 15.9 us -> 13.5 us  [project(): pl.pallas_call(project_kernel, grid=(cells, 2), in_specs=[pl.BlockSpec(me...]
where the time goes in v3:
time: 193 us; the launch traced here: 194 us
  Pallas kernels  190 us (98%)
  local copies, waits for them, and re-layouts  3.66 us (2%)
    pallas_call x1, Pallas kernels, layer(): pl.pallas_call(layer_kernel, grid_spec=pltpu.PrefetchScalarGridSpec(num_s...  89.6 us
    pallas_call x1, Pallas kernels, finish(): pl.pallas_call(functools.partial(finish_kernel, orders), grid=(cells * pe...  82.9 us
    pallas_call x1, Pallas kernels, project(): pl.pallas_call(project_kernel, grid=(cells, 2), in_specs=[pl.BlockSpec(me...  13.5 us

profile of v3, /device:TPU:3, one launch (start us, length us, event | category | flops | bytes accessed | tf_op | source)
XLA Modules:
  0.0 194.2 jit_solution(18011129425360774310)
XLA Ops:
  0.6 13.5 %project.1 = (bf16[4,256,1024]{2,1,0:T(8,128)(2,1)}, bf16[4,2048,256]{2,1,0:T(8,128)(2,1)}, bf16[4,4,80,2048]{3,2,1,0:T(8,128)(2,1)}, bf16[4,256,2048]{2,1,0:T(8...) custom-call(s32[4]{0:T(128)} %counts.3, bf16[4,1024,256]{2,1,0:T(8,128)(2,1)} %x.5, bf16[4,1024,256]{2,1,0:T(8,128)(2,1)} %x.5, ...), custom_call_target="tpu_custom_call" | custom-call | tf_op jit(solution)/shard_map/project/pallas_call | solution.py:181
  14.2 89.6 %layer.1 = (bf16[4,1024,256]{2,1,0:T(8,128)(2,1)}, bf16[4,8,256]{2,1,0:T(8,128)(2,1)}, bf16[4,1024,256]{2,1,0:T(8,128)(2,1)}, f32[4,8,256]{2,1,0:T(8,128)}, bf16...) custom-call(s32[4]{0:T(128)} %counts.3, ...), custom_call_target="tpu_custom_call" | custom-call | tf_op jit(solution)/shard_map/layer/pallas_call | solution.py:709
  103.8 82.9 %finish.1 = (bf16[4,1024,256]{2,1,0:T(8,128)(2,1)}, bf16[4,8,256]{2,1,0:T(8,128)(2,1)}, bf16[6144,128]{1,0:T(8,128)(2,1)}, f32[32,128]{1,0:T(8,128)}) custom-call(bf16[6144,128]{1,0:T(8,128)(2,1)} %get-tuple-element.52.slab, f32[32,128]{1,0:T(8,128)} %get-tuple-element.53.vec, bf16[4,1024,256]{2,1,0:T(8,128)(2,1)} %x.5, ...), custom_call_target="tpu_custom_call" | custom-call | tf_op jit(solution)/shard_map/finish/pallas_call | solution.py:1018
  186.7 3.8 %unpack.1 = (f32[256,1024]{1,0:T(8,128)}, f32[1024,256]{1,0:T(8,128)}, f32[256,256]{1,0:T(8,128)}, f32[256,768]{1,0:T(8,128)}, f32[1,1024]{1,0:T(1,128)}, /*inde...) custom-call(bf16[6144,128]{1,0:T(8,128)(2,1)} %get-tuple-element.62.slab, ...), custom_call_target="tpu_custom_call" | custom-call | tf_op jit(solution)/shard_map/unpack/pallas_call | solution.py:1105
  190.5 0.0 copy-start
  190.5 3.0 %copy.31 = bf16[4,1024,256]{2,1,0:T(8,128)(2,1)} copy(bf16[4,1024,256]{2,1,0:T(8,128)(2,1)} %get-tuple-element.90) | data formatting | bytes 4194304
  193.6 0.0 copy-done
  193.6 0.6 copy.32
Async XLA Ops:
  190.5 3.1 %copy-start = (bf16[4,8,256]{2,1,0:T(8,128)(2,1)S(1)}, bf16[4,8,256]{2,1,0:T(8,128)(2,1)}, u32[]{:S(2)}) copy-start(bf16[4,8,256]{2,1,0:T(8,128)(2,1)} %get-tuple-element.91) | copy-start | bytes 49156

commit v4 on v3

--- a/solution.py
+++ b/solution.py
@@ -12,7 +12,7 @@
 LOG2E = 1.4426950408889634
 SAFE = 40.0
 KB = 256
-STREAMS = 3
+FF_STEP = 512
 MARKS = 3
 VECTOR_ROWS = 32
 VMEM = 63 * 2**20
@@ -59,10 +59,6 @@
     centered = values - jnp.sum(values, 0, keepdims=True) * scale
     inverse = lax.rsqrt(jnp.sum(centered * centered, 0, keepdims=True) * scale + EPS)
     return centered * inverse, inverse
-
-
-def flip(index, stride):
-    return index + stride * (1 - 2 * ((index // stride) % 2))
 
 
 def greet(partners):
@@ -276,8 +272,7 @@
     delta,
     att,
     datt,
-    x_t,
-    dq_acc,
+    dq_t,
     up_acc,
     g_down,
     g_out,
@@ -479,8 +474,6 @@
     def pad_rows(rows):
         return jnp.concatenate([rows, jnp.zeros((128 - rows.shape[0], width), F32)], 0)
 
-    x_t[:, :genes] = x[0].T
-    x_t[:, genes:] = pad_rows(xc[0].astype(F32)).T.astype(BF16)
     att[:, genes:] = pad_rows(class_att).T.astype(BF16)
 
     def feed(start, columns, with_class):
@@ -489,7 +482,9 @@
         wide_gain, wide_bias = widen(gain_c[...], lanes), widen(bias_c[...], lanes)
         cot_r = cot[0, pl.ds(start, columns), :]
         cot_t = cot_r.T
+        x_t = x[0, pl.ds(start, columns), :].T
         if with_class:
+            x_t = jnp.concatenate([x_t, pad_rows(xc[0].astype(F32)).T.astype(BF16)], 1)
             padded = pad_rows(cotc[0].astype(F32))
             cot_t = jnp.concatenate([cot_t, padded.T.astype(BF16)], 1)
             cot_r = jnp.concatenate([cot_r, (padded * 0.5).astype(BF16)], 0)
@@ -505,18 +500,25 @@
             weigh = lambda values: values
             weigh_rows = lambda rows: rows
         att_low = att[:, span]
-        middle = x_t[:, span].astype(F32) + dot(w_out_t[...], att_low)
-        grad_act = dot(w_down[...], cot_t)
+        middle = x_t.astype(F32) + dot(w_out_t[...], att_low)
         unit, inverse = norm_columns(middle)
         low = (unit * wide_gain + wide_bias).astype(BF16)
-        up = dot(w_up_t[...], low) + widen(b_up_c[...], lanes)
-        active, slope = gelu_parts(up)
-        active = active.astype(BF16)
-        grad_up = slope * grad_act
-        up_bias_acc[...] += fold_lanes(weigh(grad_up))
-        grad_up = grad_up.astype(BF16)
-        result = middle + dot(w_down_t[...], active) + widen(b_down_c[...], lanes)
-        back = dot(w_up[...], grad_up)
+        low_r = weigh_rows(low.T)
+        result = middle + widen(b_down_c[...], lanes)
+        back = jnp.zeros((width, lanes), F32)
+        for first in range(0, ff, FF_STEP):
+            part = slice(first, first + FF_STEP)
+            up = dot(w_up_t[part, :], low) + widen(b_up_c[part, :], lanes)
+            grad_act = dot(w_down[part, :], cot_t)
+            active, slope = gelu_parts(up)
+            active = active.astype(BF16)
+            grad_up = slope * grad_act
+            up_bias_acc[part, :] += fold_lanes(weigh(grad_up))
+            grad_up = grad_up.astype(BF16)
+            result += dot(w_down_t[:, part], active)
+            back += dot(w_up[:, part], grad_up)
+            g_down[part, :] += dot(active, cot_r)
+            up_acc[part, :] += dot(grad_up, low_r)
         scaled = back * wide_gain
         scale = 1.0 / width
         grad_middle = cot_t.astype(F32) + inverse * (
@@ -529,8 +531,6 @@
         gain_acc[...] += fold_lanes(weigh(back * unit))
         bias_acc[...] += fold_lanes(weigh(back))
         middle_r = grad_middle.T
-        g_down[...] += dot(active, cot_r)
-        up_acc[...] += dot(grad_up, weigh_rows(low.T))
         g_out[...] += dot(att_low, weigh_rows(middle_r))
         cot_sum = jnp.sum(cot_r.astype(F32), 0, keepdims=True)
         down_bias_acc[...] += cot_sum
@@ -583,7 +583,7 @@
     )
     class_probs = probs_ck[...]
     class_dscore = (class_probs.astype(F32) * (class_dprob - delta_rows)).astype(BF16)
-    dq_acc[...] = dot_tn(class_dscore, key_cb)
+    dq_t[...] = dot(key_c_t, class_dscore)
     class_dkey = dot_nt(class_dscore, qt[0])
     class_dvalue = dot_nt(class_probs, datt[:, :genes])
     own_dprob = dot(class_grad_b, value_c_t)
@@ -595,7 +595,6 @@
     class_grad_s = spread_heads(class_grad_b, jnp.zeros((stack, 16), BF16))
     class_grad_ht = class_grad_h.T
     query_ct = query_ch.T
-    pair_lanes = lax.broadcasted_iota(jnp.int32, (KB, 2 * head), 1) // head
 
     def backward_block(block, class_dquery):
         start = nth_block(block)
@@ -604,7 +603,8 @@
         class_weights = probs_cq[:, keys]
         class_dprob = dot(class_grad_s, va[0, :, :, keys].reshape(HEADS * deep, KB))
         class_dscore = (class_weights.astype(F32) * (class_dprob - class_delta)).astype(BF16)
-        dkeys, dvalues, dscores, zeroed = [], [], [], []
+        dkeys, dvalues = [], []
+        key_t = kr[0, keys, :].T
         for h in range(HEADS):
             if h + 1 < HEADS:
                 dprobs.append(dot(da[h + 1, :, :deep], va[0, h + 1, :, keys]))
@@ -613,15 +613,9 @@
             own = slice(h * head, (h + 1) * head)
             dvalues.append(dot(datt[own, :genes], weights))
             dkeys.append(dot(qt[0, own, :], dscore))
-            pair = slice((h // 2) * 2 * head, (h // 2 + 1) * 2 * head)
-            dscores.append(dscore)
-            zeroed.append(
-                jnp.where(pair_lanes == h % 2, kr[0, keys, pair].astype(F32), 0.0).astype(BF16)
-            )
-            if h % 2 == 1:
-                dq_acc[:, pair] += dot(
-                    jnp.concatenate(dscores[h - 1 :], 1), jnp.concatenate(zeroed[h - 1 :], 0)
-                )
+            spot = slice(h % 2 * 2, h % 2 * 2 + 2)
+            qz[spot] = dscore.T.reshape(2, KB // 2, genes)
+            dq_t[own, :] += dot(key_t[own, :], qz[spot].reshape(KB, genes))
         dkey = jnp.concatenate(dkeys, 0) + dot(query_ct, class_dscore)
         dvalue = jnp.concatenate(dvalues, 0) + dot(class_grad_ht, class_weights)
         valid = key_mask(start, (1, KB), 1)
@@ -640,7 +634,7 @@
     pl.loop(own_blocks, half_blocks)(blank_rows)
     pl.loop(half_blocks + other_blocks, 2 * half_blocks)(blank_rows)
 
-    dquery_r = (dq_acc[...] * factor).astype(BF16)
+    dquery_r = (dq_t[...] * factor).astype(BF16).T
     dq[0] = dquery_r
     qkv_acc[:, :width] += dot(ut[0, :, :genes], dquery_r)
     class_dquery = from_heads(class_dquery) * factor
@@ -671,6 +665,8 @@
         put(g_down[...])
         put(g_out[...])
         put(qkv_acc[...])
+        if first < slab.shape[0]:
+            slab[first:, :] = jnp.zeros((slab.shape[0] - first, 128), BF16)
         g_vec[...] = jnp.zeros_like(g_vec)
         line = 0
         for vector in (
@@ -697,7 +693,7 @@
     head = width // HEADS
     ff = w_up.shape[1]
     stack = HEADS * classes
-    slab_rows = (2 * ff + 4 * width) * width // 128
+    slab_rows = Reduction.padded((2 * ff + 4 * width) * width // 128, lax.axis_size("cell"))
     whole = lambda shape: pl.BlockSpec(
         shape, lambda c, *_: (0,) * len(shape), pipeline_mode=pl.Buffered(1)
     )
@@ -762,8 +758,7 @@
                 f32(HEADS, 1, genes),
                 vmem(width, genes + 128),
                 vmem(width, genes + 128),
-                vmem(width, genes + 128),
-                f32(genes, width),
+                f32(width, genes),
                 f32(ff, width),
                 f32(ff, width),
                 f32(width, width),
@@ -793,8 +788,234 @@
     )(counts, place, *tables, x, xc, cot, cotc, w_out, gain, bias, w_up, b_up, w_down, b_down)
 
 
+class Reduction:
+    @staticmethod
+    def groups(cells):
+        bits = (cells - 1).bit_length()
+        return [(shift, min(2, bits - shift)) for shift in range(0, bits, 2)]
+
+    @staticmethod
+    def streams(rows, cells):
+        groups = Reduction.groups(cells)
+        unit = 2 * 16 * cells
+        units = -(-rows // unit)
+        count = min(len(groups), units)
+        shares = [units // count] * count
+        if count == 2:
+            shares[1] = max(1, units // 3)
+        shares[0] = units - sum(shares[1:])
+        result, first = [], 0
+        for i, share in enumerate(shares):
+            result.append((first, share * unit, groups[i:] + groups[:i]))
+            first += share * unit
+        return result
+
+    @staticmethod
+    def padded(rows, cells):
+        first, size, _ = Reduction.streams(rows, cells)[-1]
+        return first + size
+
+    @staticmethod
+    def scratch(rows, cells):
+        rows = Reduction.padded(rows, cells)
+        hops = 2 + 2 * sum((1 << bits) - 1 for _, bits in Reduction.groups(cells))
+        sems = (len(Reduction.streams(rows, cells)), hops)
+        return [
+            pltpu.VMEM((rows // 2, 128), BF16),
+            pltpu.VMEM((rows, 128), BF16),
+            pltpu.VMEM((rows, 128), BF16),
+            pltpu.SemaphoreType.DMA(sems),
+            pltpu.SemaphoreType.DMA(sems),
+        ]
+
+    def __init__(self, source, cells, work, inbox, total, sent, received):
+        self.source, self.work, self.inbox, self.total = source, work, inbox, total
+        self.sent, self.received = sent, received
+        self.plan = self.streams(source.shape[0], cells)
+        self.depth = len(self.groups(cells))
+        self.stages = 2 * self.depth + 3
+        self.me, self.place = lax.axis_index("cell"), lax.axis_index("gene")
+
+    def peer(self, group, ahead):
+        shift, bits = group
+        radix = 1 << bits
+        digit = (self.me // (1 << shift)) % radix
+        there = (digit + ahead) % radix
+        return {"cell": self.me + (there - digit) * (1 << shift), "gene": self.place}, there
+
+    def digit(self, group):
+        return (self.me // (1 << group[0])) % (1 << group[1])
+
+    def held(self, stream, level):
+        _, rows, order = self.plan[stream]
+        first, size = 0, rows // 2
+        for group in order[:level]:
+            size = size >> group[1]
+            first = first + self.digit(group) * size
+        return first, size
+
+    def slot(self, stream, level):
+        first, rows, order = self.plan[stream]
+        size = rows // 2
+        spot = first
+        for i in range(level):
+            spot += size if i == 0 else ((1 << order[i - 1][1]) - 1) * size
+            size = size >> order[i][1] if i < len(order) else size
+        return spot
+
+    def copy(self, source, target, stream, hop, ahead, device):
+        return pltpu.make_async_remote_copy(
+            src_ref=source,
+            dst_ref=target,
+            send_sem=self.sent.at[stream, hop + ahead - 1],
+            recv_sem=self.received.at[stream, hop + ahead - 1],
+            device_id=device,
+            device_id_type=MESH,
+        )
+
+    def hop(self, stream, index):
+        peers = [1] + [(1 << bits) - 1 for _, bits in self.plan[stream][2]]
+        return sum((peers + peers[::-1])[:index])
+
+    def rows(self, first, size):
+        return pl.ds(pl.multiple_of(first, 16), size)
+
+    def scatter(self, stream, level):
+        first, rows, order = self.plan[stream]
+        half = rows // 2
+        if level == 0:
+            mate = {"cell": self.me, "gene": 1 - self.place}
+            source = self.source.at[self.rows(first + (1 - self.place) * half, half), :]
+            target = self.inbox.at[pl.ds(first, half), :]
+            return [self.copy(source, target, stream, 0, 1, mate)]
+        group = order[level - 1]
+        start, size = self.held(stream, level - 1)
+        size = size >> group[1]
+        copies = []
+        for ahead in range(1, 1 << group[1]):
+            device, there = self.peer(group, ahead)
+            source = self.work.at[self.rows(first // 2 + start + there * size, size), :]
+            target = self.inbox.at[pl.ds(self.slot(stream, level) + (ahead - 1) * size, size), :]
+            copies.append(self.copy(source, target, stream, self.hop(stream, level), ahead, device))
+        return copies
+
+    def add(self, stream, level):
+        first, rows, order = self.plan[stream]
+        half = rows // 2
+        start, size = self.held(stream, level)
+        if level == 0:
+            value = self.source[self.rows(first + self.place * half, half), :].astype(F32)
+            count = 1
+        else:
+            value = self.work[self.rows(first // 2 + start, size), :].astype(F32)
+            count = (1 << order[level - 1][1]) - 1
+        for i in range(count):
+            value += self.inbox[pl.ds(self.slot(stream, level) + i * size, size), :].astype(F32)
+        if level == self.depth:
+            self.total[self.rows(first + self.place * half + start, size), :] = value.astype(BF16)
+        else:
+            self.work[self.rows(first // 2 + start, size), :] = value.astype(BF16)
+
+    def gather(self, stream, level):
+        first, rows, order = self.plan[stream]
+        half = rows // 2
+        start, size = self.held(stream, level)
+        span = self.total.at[self.rows(first + self.place * half + start, size), :]
+        hop = self.hop(stream, 2 * self.depth + 1 - level)
+        if level == 0:
+            mate = {"cell": self.me, "gene": 1 - self.place}
+            return [self.copy(span, span, stream, hop, 1, mate)]
+        group = order[level - 1]
+        return [
+            self.copy(span, span, stream, hop, ahead, self.peer(group, ahead)[0])
+            for ahead in range(1, 1 << group[1])
+        ]
+
+    def copies(self, stream, index):
+        if index <= self.depth:
+            return self.scatter(stream, index)
+        return self.gather(stream, 2 * self.depth + 1 - index)
+
+    def stage(self, index):
+        if index > 0:
+            for stream in range(len(self.plan)):
+                for copy in self.copies(stream, index - 1):
+                    copy.wait()
+                if index - 1 <= self.depth:
+                    self.add(stream, index - 1)
+        if index < self.stages - 1:
+            for stream in range(len(self.plan)):
+                for copy in self.copies(stream, index):
+                    copy.start()
+
+
+class VectorSum:
+    @staticmethod
+    def scratch(shape, cells):
+        groups = Reduction.groups(cells)
+        return [
+            pltpu.VMEM((2 + sum(1 << bits for _, bits in groups),) + shape, F32),
+            pltpu.SemaphoreType.DMA((len(groups) + 1, 3)),
+            pltpu.SemaphoreType.DMA((len(groups) + 1, 3)),
+        ]
+
+    def __init__(self, cells, reduction, slots, sent, received):
+        self.reduction, self.slots, self.sent, self.received = reduction, slots, sent, received
+        self.groups = reduction.groups(cells)
+
+    def first(self, level):
+        return 0 if level == 0 else 2 + sum(1 << bits for _, bits in self.groups[: level - 1])
+
+    def size(self, level):
+        return 2 if level == 0 else 1 << self.groups[level - 1][1]
+
+    def copies(self, level):
+        r = self.reduction
+        if level == 0:
+            mine = r.place
+            devices = [{"cell": r.me, "gene": 1 - r.place}]
+        else:
+            group = self.groups[level - 1]
+            mine = r.digit(group)
+            devices = [r.peer(group, ahead)[0] for ahead in range(1, self.size(level))]
+        spot = self.slots.at[self.first(level) + mine]
+        return mine, [
+            pltpu.make_async_remote_copy(
+                src_ref=spot,
+                dst_ref=spot,
+                send_sem=self.sent.at[level, i],
+                recv_sem=self.received.at[level, i],
+                device_id=device,
+                device_id_type=MESH,
+            )
+            for i, device in enumerate(devices)
+        ]
+
+    def start(self, level, value):
+        mine, copies = self.copies(level)
+        self.slots[self.first(level) + mine] = value
+        for copy in copies:
+            copy.start()
+
+    def finish(self, level):
+        for copy in self.copies(level)[1]:
+            copy.wait()
+        first = self.first(level)
+        total = self.slots[first]
+        for i in range(1, self.size(level)):
+            total = total + self.slots[first + i]
+        return total
+
+    def stage(self, index, value):
+        levels = len(self.groups)
+        if 0 < index <= levels + 1:
+            value = self.finish(index - 1)
+        if index <= levels:
+            self.start(index, value)
+        return value if index == levels + 1 else None
+
+
 def finish_kernel(
-    orders,
     slab,
     vec,
     x,
@@ -814,20 +1035,13 @@
     slab_out,
     vec_out,
     w_t,
-    work,
-    summed,
-    inbox,
-    vec_in,
     other,
     other_c,
-    send_sems,
-    recv_sems,
-    vec_send,
-    vec_recv,
     swap_send,
     swap_recv,
     class_send,
     class_recv,
+    *reduction_scratch,
 ):
     step, steps = pl.program_id(0), pl.num_programs(0)
     cells = dkv_hbm.shape[0]
@@ -835,118 +1049,36 @@
     rows, width = x.shape[1:]
     classes = xc.shape[1]
     per_cell = genes // rows
-    me, place = lax.axis_index("cell"), lax.axis_index("gene")
-    bits = len(orders[0])
-    part = slab.shape[0] // STREAMS
-    half = part // 2
-    mate = {"cell": me, "gene": 1 - place}
-
-    def peer(bit):
-        return {"cell": flip(me, 1 << bit), "gene": place}
-
-    def remote(source, target, send, receive, device):
+    all_cells = lax.axis_size("cell")
+    sums = Reduction(slab, all_cells, *reduction_scratch[:5])
+    vectors = VectorSum(all_cells, sums, *reduction_scratch[5:])
+    mate = {"cell": sums.me, "gene": 1 - sums.place}
+
+    def swap(cell):
         return pltpu.make_async_remote_copy(
-            src_ref=source,
-            dst_ref=target,
-            send_sem=send,
-            recv_sem=receive,
-            device_id=device,
+            src_ref=dkv_hbm.at[cell, pl.ds(genes, genes), :],
+            dst_ref=other.at[cell],
+            send_sem=swap_send.at[cell],
+            recv_sem=swap_recv.at[cell],
+            device_id=mate,
             device_id_type=MESH,
         )
 
-    def swap(cell):
-        return remote(
-            dkv_hbm.at[cell, pl.ds(genes, genes), :],
-            other.at[cell],
-            swap_send.at[cell],
-            swap_recv.at[cell],
-            mate,
+    def swap_class():
+        return pltpu.make_async_remote_copy(
+            src_ref=dkvc,
+            dst_ref=other_c,
+            send_sem=class_send,
+            recv_sem=class_recv,
+            device_id=mate,
+            device_id_type=MESH,
         )
 
-    def swap_class():
-        return remote(dkvc, other_c, class_send, class_recv, mate)
-
-    def low(stream, level):
-        start, size = 0, half
-        for i in range(level - 1):
-            size = size // 2
-            start = start + ((me // (1 << orders[stream][i])) % 2) * size
-        return pl.multiple_of(start, 16) if level > 1 else start
-
-    def length(level):
-        return part >> level
-
-    def box(level):
-        return half - (half >> (level - 1)) + half if level else 0
-
-    def gather(stream, level):
-        sems = send_sems.at[stream, level], recv_sems.at[stream, level]
-        if level == 0:
-            source = slab.at[pl.ds(pl.multiple_of(stream * part + (1 - place) * half, 16), half), :]
-            return remote(source, inbox.at[stream, pl.ds(0, half), :], *sems, mate)
-        size = length(level + 1)
-        bit = orders[stream][level - 1]
-        away = 1 - (me // (1 << bit)) % 2
-        start = pl.multiple_of(low(stream, level) + away * size, 16)
-        return remote(
-            work.at[stream, pl.ds(start, size), :],
-            inbox.at[stream, pl.ds(box(level), size), :],
-            *sems,
-            peer(bit),
-        )
-
-    def add(stream, level):
-        size = length(level + 1)
-        if level == 0:
-            mine = slab[pl.ds(pl.multiple_of(stream * part + place * half, 16), half), :]
-            start = 0
-        else:
-            start = low(stream, level + 1)
-            mine = work[stream, pl.ds(start, size), :]
-        total = mine.astype(F32) + inbox[stream, pl.ds(box(level), size), :].astype(F32)
-        total = total.astype(BF16)
-        if level == bits:
-            summed[pl.ds(pl.multiple_of(stream * part + place * half + start, 16), size), :] = total
-        else:
-            work[stream, pl.ds(start, size), :] = total
-
-    def spread(stream, level):
-        sems = send_sems.at[stream, 2 * bits + 1 - level], recv_sems.at[stream, 2 * bits + 1 - level]
-        size = length(level + 1)
-        start = low(stream, level + 1) if level else 0
-        span = pl.ds(pl.multiple_of(stream * part + place * half + start, 16), size)
-        device = peer(orders[stream][level - 1]) if level else mate
-        return remote(summed.at[span, :], summed.at[span, :], *sems, device)
-
-    def vector(level):
-        device = peer(orders[0][level - 1]) if level else mate
-        return remote(
-            vec if level == 0 else vec_out,
-            vec_in.at[level],
-            vec_send.at[level],
-            vec_recv.at[level],
-            device,
-        )
-
     def stage(index):
-        if index > 0:
-            if index - 1 <= bits:
-                for stream in range(STREAMS):
-                    gather(stream, index - 1).wait()
-                    add(stream, index - 1)
-                vector(index - 1).wait()
-                before = vec[...] if index == 1 else vec_out[...]
-                vec_out[...] = before + vec_in[index - 1]
-            else:
-                for stream in range(STREAMS):
-                    spread(stream, 2 * bits + 2 - index).wait()
-        if index <= bits:
-            for stream in range(STREAMS):
-                gather(stream, index).start()
-            vector(index).start()
-        elif index < 2 * bits + 2:
-            for stream in range(STREAMS):
-                spread(stream, 2 * bits + 1 - index).start()
+        sums.stage(index)
+        done = vectors.stage(index, vec[...] if index == 0 else None)
+        if done is not None:
+            vec_out[...] = done
 
     def rows_back(values, grads, packed):
         unit, inverse = norm_rows(values)
@@ -957,14 +1089,17 @@
             - unit * jnp.mean(scaled * unit, -1, keepdims=True)
         )
 
-    stages = 2 * bits + 3
     last = cells * per_cell - 1
-    for index in range(min(stages, last + 1)):
+    for index in range(min(sums.stages, last + 1)):
 
         @pl.when(step == index)
         def _(index=index):
             if index == 0:
-                greet([mate] + [peer(bit) for bit in range(bits)])
+                partners = [mate]
+                for group in sums.groups(all_cells):
+                    for ahead in range(1, 1 << group[1]):
+                        partners.append(sums.peer(group, ahead)[0])
+                greet(partners)
             stage(index)
             if index == 0:
                 for cell in range(cells):
@@ -992,31 +1127,30 @@
         packed = jnp.concatenate([dqc[...], class_grads], 2).reshape(stack, 3 * width)
         values = xc[...].astype(F32).reshape(stack, width)
         result = rows_back(values, gmc[...].reshape(stack, width), packed.astype(BF16))
-        g_xc[...] = result.reshape(cells, classes, width).astype(BF16)
-        for index in range(last + 1, stages):
+        g_xc[...] = result.reshape(cells, classes, width)
+        for index in range(last + 1, sums.stages):
             stage(index)
-        slab_out[...] = summed[...]
-
-
-def finish(orders, slab, vec, x, xc, gm, gmc, dq, dqc, dkv, dkvc, gain, bias, w):
+        slab_out[...] = sums.total[...]
+
+
+def finish(slab, vec, x, xc, gm, gmc, dq, dqc, dkv, dkvc, gain, bias, w):
     cells, genes, width = x.shape
     classes = xc.shape[1]
     rows = genes // 2
     per_cell = genes // rows
-    bits = len(orders[0])
-    part = slab.shape[0] // STREAMS
+    all_cells = lax.axis_size("cell")
     whole = lambda array: pl.BlockSpec(array.shape, lambda i: (0,) * array.ndim)
     piece = lambda lanes: pl.BlockSpec((1, rows, lanes), lambda i: (i // per_cell, i % per_cell, 0))
     out = lambda shape, kind=BF16: jax.ShapeDtypeStruct(shape, kind)
     dma = lambda *shape: pltpu.SemaphoreType.DMA(shape)
     outs = [
         out((cells, genes, width)),
-        out((cells, classes, width)),
+        out((cells, classes, width), F32),
         out(slab.shape),
         out(vec.shape, F32),
     ]
     return pl.pallas_call(
-        functools.partial(finish_kernel, orders),
+        finish_kernel,
         grid=(cells * per_cell,),
         in_specs=[
             whole(slab),
@@ -1038,21 +1172,15 @@
         out_shape=outs,
         scratch_shapes=[
             pltpu.VMEM((3 * width, width), BF16),
-            pltpu.VMEM((STREAMS, part // 2, 128), BF16),
-            pltpu.VMEM(slab.shape, BF16),
-            pltpu.VMEM((STREAMS, part, 128), BF16),
-            pltpu.VMEM((bits + 1,) + vec.shape, F32),
             pltpu.VMEM((cells, genes, 2 * width), BF16),
             pltpu.VMEM(dkvc.shape, F32),
-            dma(STREAMS, 2 * bits + 2),
-            dma(STREAMS, 2 * bits + 2),
-            dma(bits + 1),
-            dma(bits + 1),
             dma(cells),
             dma(cells),
             dma(),
             dma(),
-        ],
+        ]
+        + Reduction.scratch(slab.shape[0], all_cells)
+        + VectorSum.scratch(vec.shape, all_cells),
         compiler_params=pltpu.CompilerParams(
             vmem_limit_bytes=VMEM, collective_id=1, has_side_effects=True
         ),
@@ -1060,21 +1188,29 @@
     )(slab, vec, x, gm, dq, dkv, dkv, xc, gmc, dqc, dkvc, gain, bias, w)
 
 
-def unpack_kernel(slab, vec, gain, bias, w, g_up, g_down, g_out, g_qkv, *vectors):
+def unpack_kernel(
+    slab, vec, gain, bias, w, x, xc, g_up, g_down, g_out, g_qkv, g_x, g_xc, *vectors
+):
+    step = pl.program_id(0)
     width, ff = g_up.shape
+    g_x[...] = x[...]
     first = 0
 
-    def take(target):
+    def take(target, at):
         nonlocal first
         rows = target.shape[0]
-        for start in range(0, target.shape[1], 128):
-            target[:, start : start + 128] = slab[first : first + rows, :].astype(F32)
-            first += rows
-
-    take(g_up)
-    take(g_down)
-    take(g_out)
-    take(g_qkv)
+        begin = first
+        first += rows * target.shape[1] // 128
+
+        @pl.when(step == at)
+        def _():
+            for i in range(target.shape[1] // 128):
+                spot = begin + i * rows
+                target[:, i * 128 : (i + 1) * 128] = slab[spot : spot + rows, :].astype(F32)
+
+    take(g_up, 0)
+    take(g_down, 1)
+    take(g_out, 1)
     line = 0
 
     def lines(count):
@@ -1083,42 +1219,63 @@
         return jnp.concatenate([vec[i : i + 1, :] for i in range(line - count, line)], 1)
 
     up_bias, ln2_gain, ln2_bias, down_bias, ln1_gain, ln1_bias = vectors
-    up_bias[...] = lines(ff // 128)
-    ln2_gain[...] = lines(width // 128)
-    ln2_bias[...] = lines(width // 128)
-    down_bias[...] = lines(width // 128)
-    packed_sum = lines(3 * width // 128)
-    weights = w[...].astype(F32)
-    sums = g_qkv[...]
-    ln1_gain[...] = jnp.sum((weights * sums).T, 0, keepdims=True)
-    ln1_bias[...] = jnp.sum((weights * packed_sum).T, 0, keepdims=True)
-    g_qkv[...] = (
-        widen(spread_column(gain[...]), 3 * width) * sums
-        + widen(spread_column(bias[...]), 3 * width) * packed_sum
-    )
-
-
-def unpack(slab, vec, gain, bias, w, ff):
+
+    @pl.when(step == 2)
+    def _():
+        g_xc[...] = xc[...].astype(BF16)
+        up_bias[...] = lines(ff // 128)
+        ln2_gain[...] = lines(width // 128)
+        ln2_bias[...] = lines(width // 128)
+        down_bias[...] = lines(width // 128)
+        packed_sum = lines(3 * width // 128)
+        weights = w[...].astype(F32)
+        sums = jnp.concatenate(
+            [
+                slab[first + i * width : first + (i + 1) * width, :].astype(F32)
+                for i in range(3 * width // 128)
+            ],
+            1,
+        )
+        ln1_gain[...] = jnp.sum((weights * sums).T, 0, keepdims=True)
+        ln1_bias[...] = jnp.sum((weights * packed_sum).T, 0, keepdims=True)
+        g_qkv[...] = (
+            widen(spread_column(gain[...]), 3 * width) * sums
+            + widen(spread_column(bias[...]), 3 * width) * packed_sum
+        )
+
+
+def unpack(slab, vec, gain, bias, w, x, xc, ff):
     width = w.shape[0]
+    cells, genes, _ = x.shape
     out = lambda *shape: jax.ShapeDtypeStruct(shape, F32)
+    whole = lambda array: pl.BlockSpec(array.shape, lambda i: (0,) * len(array.shape))
+    piece = pl.BlockSpec((1, genes, width), lambda i: (i, 0, 0))
     row = out(1, width)
+    outs = [
+        out(width, ff),
+        out(ff, width),
+        out(width, width),
+        out(width, 3 * width),
+        jax.ShapeDtypeStruct(x.shape, BF16),
+        jax.ShapeDtypeStruct(xc.shape, BF16),
+        out(1, ff),
+        row,
+        row,
+        row,
+        row,
+        row,
+    ]
+    specs = [whole(o) for o in outs]
+    specs[4] = piece
     return pl.pallas_call(
         unpack_kernel,
-        out_shape=[
-            out(width, ff),
-            out(ff, width),
-            out(width, width),
-            out(width, 3 * width),
-            out(1, ff),
-            row,
-            row,
-            row,
-            row,
-            row,
-        ],
+        grid=(cells,),
+        in_specs=[whole(slab), whole(vec), whole(gain), whole(bias), whole(w), piece, whole(xc)],
+        out_specs=specs,
+        out_shape=outs,
         compiler_params=pltpu.CompilerParams(vmem_limit_bytes=VMEM),
         name="unpack",
-    )(slab, vec, gain, bias, w)
+    )(slab, vec, gain, bias, w, x, xc)
 
 
 def shards(
@@ -1140,9 +1297,6 @@
 ):
     row = lambda vector: vector.reshape(1, -1)
     place = lax.axis_index("gene").reshape(1)
-    bits = (lax.axis_size("cell") - 1).bit_length()
-    near = list(range(bits - 1))
-    orders = [near[i % len(near) :] + near[: i % len(near)] + [bits - 1] for i in range(STREAMS)]
     gain1, bias1 = row(ln1_gain), row(ln1_bias)
     tables = project(expressed, gene_in, class_in, gain1, bias1, w_qkv)
     gene_out, class_out, dq, dqc, dkv, dkvc, gm, gmc, slab, vec = layer(
@@ -1162,11 +1316,22 @@
         row(b_down),
     )
     gene_grad, class_grad, slab, vec = finish(
-        orders, slab, vec, gene_in, class_in, gm, gmc, dq, dqc, dkv, dkvc, gain1, bias1, w_qkv
+        slab, vec, gene_in, class_in, gm, gmc, dq, dqc, dkv, dkvc, gain1, bias1, w_qkv
     )
-    g_up, g_down, g_out, g_qkv, g_b_up, g_gain2, g_bias2, g_b_down, g_gain1, g_bias1 = unpack(
-        slab, vec, gain1, bias1, w_qkv, w_up.shape[1]
-    )
+    (
+        g_up,
+        g_down,
+        g_out,
+        g_qkv,
+        gene_grad,
+        class_grad,
+        g_b_up,
+        g_gain2,
+        g_bias2,
+        g_b_down,
+        g_gain1,
+        g_bias1,
+    ) = unpack(slab, vec, gain1, bias1, w_qkv, gene_grad, class_grad, w_up.shape[1])
     return (
         gene_out,
         class_out,

time: 193 us -> 183 us (0.948); the launches traced: 194 us -> 179 us
  Pallas kernels: 190 us -> 178 us
  local copies, waits for them, and re-layouts: 3.66 us -> 0 us
    pallas_call x2, Pallas kernels: 86.7 us -> 57.6 us  [the longest x1 51.6 us: finish(): pl.pallas_call(finish_kernel, grid=(cells * per_cell,), in_specs=[whole(s...]
    pallas_call x1, Pallas kernels: 89.6 us -> 107 us  [layer(): pl.pallas_call(layer_kernel, grid_spec=pltpu.PrefetchScalarGridSpec(num_s...]
    unnamed x4 -> x0, local copies, waits for them, and re-layouts: 3.66 us -> none
where the time goes in v4:
time: 183 us; the launch traced here: 179 us
  Pallas kernels  178 us (97%)
    pallas_call x1, Pallas kernels, layer(): pl.pallas_call(layer_kernel, grid_spec=pltpu.PrefetchScalarGridSpec(num_s...  107 us
    pallas_call x1, Pallas kernels, finish(): pl.pallas_call(finish_kernel, grid=(cells * per_cell,), in_specs=[whole(s...  51.6 us
    pallas_call x1, Pallas kernels, project(): pl.pallas_call(project_kernel, grid=(cells, 2), in_specs=[pl.BlockSpec(me...  13.5 us
    pallas_call x1, Pallas kernels, unpack(): pl.pallas_call(unpack_kernel, grid=(cells,), in_specs=[whole(slab), whole...  5.98 us

profile of v4, /device:TPU:3, one launch (start us, length us, event | category | flops | bytes accessed | tf_op | source)
XLA Modules:
  0.0 179.2 jit_solution(634297766154124903)
XLA Ops:
  0.6 13.5 %project.1 = (bf16[4,256,1024]{2,1,0:T(8,128)(2,1)}, bf16[4,2048,256]{2,1,0:T(8,128)(2,1)}, bf16[4,4,80,2048]{3,2,1,0:T(8,128)(2,1)}, bf16[4,256,2048]{2,1,0:T(8...) custom-call(s32[4]{0:T(128)} %counts.3, bf16[4,1024,256]{2,1,0:T(8,128)(2,1)} %x.5, bf16[4,1024,256]{2,1,0:T(8,128)(2,1)} %x.5, ...), custom_call_target="tpu_custom_call" | custom-call | tf_op jit(solution)/shard_map/project/pallas_call | solution.py:177
  14.2 107.3 %layer.1 = (bf16[4,1024,256]{2,1,0:T(8,128)(2,1)}, bf16[4,8,256]{2,1,0:T(8,128)(2,1)}, bf16[4,1024,256]{2,1,0:T(8,128)(2,1)}, f32[4,8,256]{2,1,0:T(8,128)}, bf16...) custom-call(s32[4]{0:T(128)} %counts.3, ...), custom_call_target="tpu_custom_call" | custom-call | tf_op jit(solution)/shard_map/layer/pallas_call | solution.py:705
  121.5 51.6 %finish.1 = (bf16[4,1024,256]{2,1,0:T(8,128)(2,1)}, f32[4,8,256]{2,1,0:T(8,128)}, bf16[6144,128]{1,0:T(8,128)(2,1)}, f32[32,128]{1,0:T(8,128)}) custom-call(bf16[6144,128]{1,0:T(8,128)(2,1)} %get-tuple-element.54.slab, f32[32,128]{1,0:T(8,128)} %get-tuple-element.55.vec, bf16[4,1024,256]{2,1,0:T(8,128)(2,1)} %x.5, ...), custom_call_target="tpu_custom_call" | custom-call | tf_op jit(solution)/shard_map/finish/pallas_call | solution.py:1152
  173.1 6.0 %unpack.1 = (f32[256,1024]{1,0:T(8,128)}, f32[1024,256]{1,0:T(8,128)}, f32[256,256]{1,0:T(8,128)}, f32[256,768]{1,0:T(8,128)}, bf16[4,1024,256]{2,1,0:T(8,128)(2...) custom-call(bf16[6144,128]{1,0:T(8,128)(2,1)} %get-tuple-element.62., ...), custom_call_target="tpu_custom_call" | custom-call | tf_op jit(solution)/shard_map/unpack/pallas_call | solution.py:1270
